TPU v7x, 256 devices: a whole 4x4x8 slice. The times are simulated.
256 devices in a mesh: region: 4 (over x), level: 32 (over z, y), member: 2 (over core).
Axes of the slice: x: 4, y: 4, z: 8, core: 2. Of those that a mesh axis runs over, the one named last changes fastest.
Arguments:
- state: float32 [3, 64, 80, 8192], P(None, 'level', 'member', 'region'), may hold values from -6 to 6
- ray_cols: int32 [2, 128, 64], replicated, may hold values from 0 to 8191, as said below
- ray_len: int32 [2, 128], replicated, may hold values from 16 to 64, as said below
- ray_weight: float32 [2, 128, 3, 64], replicated, may hold values from -0.4375 to 0.4375
- owner: int32 [2, 128], replicated, may hold values from 0 to 3, as said below
- loc_regions: int32 [2, 128, 2], replicated, may hold values from 0 to 3, as said below
- loc_weight: float32 [2, 128, 2], replicated, may hold values from 0.3 to 0.9
- obs_value: float32 [2, 128, 64], replicated, may hold values from -12 to 12
- obs_var: float32 [2, 128, 64], replicated, may hold values from 4 to 40
Outputs:
- analysis: float32 [3, 64, 80, 8192], P(None, 'level', 'member', 'region')
Inputs may be any that keep to these rules, and one draw needn't show every extreme that they name: `ray_cols`: all ray points of one occultation lie in consecutive columns of a single region. In each step, for every region and every owner, exactly 8 occultations of that owner have their rays in that region. `ray_len`: so at most 512 live ray points of one owner's occultations lie in one region in a step; in every step some owner's occultations all have 64 live points, so that owner has exactly 512 in every region. `owner`: each region owns exactly 32 occultations in each step. `loc_regions`: the 2 listed regions of a profile are distinct and never its owner.
All inputs are finite; a program needn't handle non-finite values.
Results may differ from a plain program's by a relative error of at most 0.00018.
Values sent between devices are 32-bit elements; how exact they have to be, the bound alone decides.
No kernel may reach another device: no remote copies, remote signals or barrier semaphores. Data moves between devices by JAX's collectives and lax.ppermute only.
A program may use at most 64 MiB of HBM per device.

v0:
```python
import jax
import jax.numpy as jnp
from jax import lax
from jax.sharding import PartitionSpec as P

STEPS = 2


def body(state, ray_cols, ray_len, ray_weight, owner, loc_regions, loc_weight, obs_value, obs_var):
    highest = lax.Precision.HIGHEST
    region_count = lax.axis_size("region")
    own_region = lax.axis_index("region")
    level_count = lax.axis_size("level")
    member_axis = lax.axis_size("member")
    member_index = lax.axis_index("member")
    var_count, lev_local, mem_local, col_local = state.shape
    members = mem_local * member_axis
    levels = lev_local * level_count
    occ_count = ray_cols.shape[1]
    ray_count = ray_cols.shape[2]
    occ_local = occ_count // region_count
    lev_first = lax.axis_index("level") * lev_local
    mem_first = member_index * mem_local
    occ_index = jnp.arange(occ_count, dtype=jnp.int32)
    earlier = occ_index[None, :] < occ_index[:, None]
    level_axis = jnp.arange(levels, dtype=jnp.float32)
    scaled = (level_axis[:, None] - level_axis[None, :]) / (levels / 4.0)
    vertical = lax.dynamic_slice_in_dim(jnp.exp(-jnp.abs(scaled)), lev_first, lev_local, 1)
    local_width = lev_local * mem_local
    current = state
    for step_index in range(STEPS):
        columns = ray_cols[step_index]
        lengths = ray_len[step_index]
        owners = owner[step_index]
        home_region = columns[:, 0] // col_local
        live_mask = jnp.arange(ray_count, dtype=jnp.int32)[None, :] < lengths[:, None]
        masked_weight = ray_weight[step_index] * live_mask[:, None, :].astype(jnp.float32)
        same_home = home_region[None, :] == home_region[:, None]
        home_rank = jnp.sum(same_home & earlier, axis=1)
        position = home_region * occ_local + home_rank
        home_key = jnp.where(home_region == own_region, home_rank, occ_local)
        home_index = jnp.zeros((occ_local,), jnp.int32).at[home_key].set(occ_index, mode="drop")
        home_weight = masked_weight[home_index]
        column_rows = current.reshape(var_count * local_width, col_local).T
        home_columns = columns[home_index] - own_region * col_local
        ray_rows = jnp.take(column_rows, home_columns.reshape(-1), axis=0)
        ray_rows = ray_rows.reshape(occ_local, ray_count, var_count, local_width)
        local_panel = jnp.einsum("krvf,kvr->kf", ray_rows, home_weight, precision=highest)
        all_panels = lax.all_gather(local_panel, "region", axis=0, tiled=True)
        ordered = all_panels[position]
        profiles = lax.all_gather(ordered, ("level", "member"), axis=1, tiled=True)
        profiles = profiles.reshape(occ_count, level_count, member_axis, lev_local, mem_local)
        profiles = profiles.transpose(0, 1, 3, 2, 4).reshape(occ_count, levels, members)
        ens_mean = jnp.mean(profiles, axis=2)
        spread = profiles - ens_mean[:, :, None]
        variance = jnp.sum(spread * spread, axis=2) / (members - 1.0)
        total_var = variance + obs_var[step_index]
        kalman_gain = (obs_value[step_index] - ens_mean) / total_var
        shrink = 1.0 / (1.0 + jnp.sqrt(obs_var[step_index] / total_var))
        listed = (loc_regions[step_index] == own_region).astype(jnp.float32)
        horiz_loc = (owners == own_region).astype(jnp.float32) + jnp.sum(
            loc_weight[step_index] * listed, axis=1
        )
        mean_coef = horiz_loc[:, None, None] * vertical[None] * kalman_gain[:, :, None]
        spread_coef = horiz_loc[:, None, None] * vertical[None] * (shrink / total_var)[:, :, None]
        mean_weights = jnp.einsum("oli,oln->in", mean_coef, spread, precision=highest)
        local_spread = lax.dynamic_slice_in_dim(spread, mem_first, mem_local, 2)
        weighted = spread_coef[:, :, :, None] * local_spread[:, :, None, :]
        spread_matrix = jnp.einsum("olim,oln->imn", weighted, spread, precision=highest)
        mixing = (mean_weights[:, None, :] - spread_matrix) / (members - 1.0)

        def absorb(running, member_rows, first_row, mixing=mixing):
            return running + jnp.einsum("imn,vinc->vimc", mixing, member_rows, precision=highest)

        current = absorb(
            current, lax.all_gather(current, "member", axis=2, tiled=True), jnp.int32(0)
        )
    return current


def solution(mesh):
    in_specs = (P(None, "level", "member", "region"), P(), P(), P(), P(), P(), P(), P(), P())
    out_specs = P(None, "level", "member", "region")
    return jax.shard_map(body, mesh=mesh, in_specs=in_specs, out_specs=out_specs, check_vma=False)
```

profile of v0, /device:TPU:1, one launch (start us, length us, event | category | flops | bytes accessed | tf_op | source)
XLA Modules:
  0.0 299.0 jit_solution(2129858351426116823)
XLA Ops:
  8.7 1.0 scatter_custom_fusion
  11.4 1.9 copy.84
  13.3 8.6 %gather_fusion.6 = f32[2048,240]{1,0:T(8,128)} fusion(f32[2048,240]{1,0:T(8,128)S(1)} %bitcast.149, s32[2048]{0:T(1024)S(1)} %fusion.86), kind=kCustom, calls=%fused_computation.clone | custom fusion | bytes 3940352 | tf_op jit(solution)/shard_map/jit(_take)/gather | solution.py:46
  21.9 1.9 broadcast_select_fusion.1
  23.8 3.4 %reshape.398 = f32[32,64,3,80]{3,2,1,0:T(4,128)} reshape(f32[2048,240]{1,0:T(8,128)S(1)} %broadcast_select_fusion.1) | data formatting | bytes 3932160 | tf_op jit(solution)/shard_map/reshape | solution.py:47
  28.2 5.0 %fusion.2 = f32[32,1,80,1]{2,1,3,0:T(1,128)S(1)} fusion(f32[32,64,3,80]{3,2,1,0:T(4,128)} %reshape.398, f32[32,3,64,1]{2,1,0,3:T(4,128)S(1)} %bitcast.171), kind=kOutput, calls=%fused_computation.12 | convolution fusion | flops 5898240 | bytes 2000896 | tf_op jit(solution)/shard_map/krvf,kvr->kf/dot_general | solution.py:48
  33.2 10.1 %all_gather.18 = f32[128,80]{1,0:T(8,128)S(1)} all-gather(f32[32,80]{1,0:T(8,128)S(1)} %bitcast.174), channel_id=1, replica_groups=mesh['region'=4,'level'=32,'member'=2] {'region'}, dimensions={0}, use_global_device_ids=true | all-gather | bytes 51200 | tf_op jit(solution)/shard_map/all_gather | solution.py:49
  44.7 1.4 copy.95
  47.9 80.4 %all-gather.11.cloned.1.call-done = f32[128,5120]{0,1:T(8,128)} async-done(((f32[128,80]{0,1:T(8,128)}), f32[128,5120]{0,1:T(8,128)}) %all-gather.11.cloned.1.call-update) | async-done | bytes 2621456 | tf_op jit(solution)/shard_map/all_gather | solution.py:51
  128.3 3.6 %copy.90 = f32[128,32,2,2,40]{0,4,3,2,1:T(8,128)} copy(f32[128,32,2,2,40]{0,4,2,3,1:T(8,128)} %bitcast.150) | data formatting | bytes 5242880 | tf_op jit(solution)/shard_map/transpose | solution.py:53
  132.1 2.0 broadcast_subtract_fusion.1
  134.1 4.0 %copy.91 = f32[128,64,80]{2,1,0:T(8,128)} copy(f32[128,64,80]{0,2,1:T(8,128)S(1)} %broadcast_subtract_fusion.1) | data formatting | bytes 5242880 | tf_op jit(solution)/shard_map/sub | solution.py:55
  138.1 2.5 multiply_reduce_fusion.1
  141.3 4.7 %convolution_bitcast_fusion.3 = f32[2,80]{1,0:T(2,128)S(1)} fusion(f32[128,64,80]{2,1,0:T(8,128)} %copy.91, f32[128,64]{1,0:T(8,128)S(1)} %copy.89, f32[64,2]{0,1:T(2,128)S(1)} %fusion.93, f32[128]{0:T(128)S(1)} %get-tuple-element.25), kind=kOutput, calls=%fused_computation.41 | convolution fusion | flops 15761408 | bytes 2655872 | tf_op jit(solution)/shard_map/oli,oln->in/dot_general | solution.py:66
  146.1 2.3 fusion.51
  148.4 4.7 %fusion.5 = f32[3,2,40,2048]{3,2,0,1:T(8,128)S(1)} fusion(f32[2,40,80,1]{2,1,3,0:T(8,128)S(1)} %fusion.51, f32[3,2,80,2048]{3,2,0,1:T(8,128)} %all-gather.7.cloned.1.call-done, f32[3,2,40,2048]{3,2,1,0:T(8,128)} %param.11), kind=kOutput, calls=%fused_computation.17 | convolution fusion | flops 472350720 | bytes 7889920 | tf_op jit(solution)/shard_map/imn,vinc->vimc/dot_general | solution.py:73
  153.2 1.5 copy.98
  155.1 1.9 copy.99
  157.0 8.6 %gather_fusion.7 = f32[2048,240]{1,0:T(8,128)} fusion(f32[2048,240]{1,0:T(8,128)S(1)} %bitcast.148, s32[2048]{0:T(1024)S(1)} %fusion.87), kind=kCustom, calls=%fused_computation.1.clone | custom fusion | bytes 3940352 | tf_op jit(solution)/shard_map/jit(_take)/gather | solution.py:46
  165.6 1.9 broadcast_select_fusion
  167.5 3.4 %reshape.399 = f32[32,64,3,80]{3,2,1,0:T(4,128)} reshape(f32[2048,240]{1,0:T(8,128)S(1)} %broadcast_select_fusion) | data formatting | bytes 3932160 | tf_op jit(solution)/shard_map/reshape | solution.py:47
  170.9 5.0 %fusion = f32[32,1,80,1]{2,1,3,0:T(1,128)S(1)} fusion(f32[32,64,3,80]{3,2,1,0:T(4,128)} %reshape.399, f32[32,3,64,1]{2,1,0,3:T(4,128)S(1)} %bitcast.170), kind=kOutput, calls=%fused_computation.10 | convolution fusion | flops 5898240 | bytes 2000896 | tf_op jit(solution)/shard_map/krvf,kvr->kf/dot_general | solution.py:48
  175.8 9.6 %all_gather.22 = f32[128,80]{1,0:T(8,128)S(1)} all-gather(f32[32,80]{1,0:T(8,128)S(1)} %bitcast.175), channel_id=1, replica_groups=mesh['region'=4,'level'=32,'member'=2] {'region'}, dimensions={0}, use_global_device_ids=true | all-gather | bytes 51200 | tf_op jit(solution)/shard_map/all_gather | solution.py:49
  187.4 78.5 %all-gather.13.cloned.1.call-done = f32[128,5120]{0,1:T(8,128)} async-done(((f32[128,80]{0,1:T(8,128)}), f32[128,5120]{0,1:T(8,128)}) %all-gather.13.cloned.1.call-update) | async-done | bytes 2621456 | tf_op jit(solution)/shard_map/all_gather | solution.py:51
  265.9 3.6 %copy.105 = f32[128,32,2,2,40]{0,4,3,2,1:T(8,128)} copy(f32[128,32,2,2,40]{0,4,2,3,1:T(8,128)} %bitcast.153) | data formatting | bytes 5242880 | tf_op jit(solution)/shard_map/transpose | solution.py:53
  269.7 2.0 broadcast_subtract_fusion
  271.7 3.8 %copy.106 = f32[128,64,80]{2,1,0:T(8,128)} copy(f32[128,64,80]{0,2,1:T(8,128)S(1)} %broadcast_subtract_fusion) | data formatting | bytes 5242880 | tf_op jit(solution)/shard_map/sub | solution.py:55
  275.6 2.5 multiply_reduce_fusion
  278.7 4.7 %convolution_bitcast_fusion.2 = f32[2,80]{1,0:T(2,128)S(1)} fusion(f32[128,64,80]{2,1,0:T(8,128)} %copy.106, f32[128,64]{1,0:T(8,128)S(1)} %copy.104, f32[64,2]{0,1:T(2,128)S(1)} %fusion.93, f32[128]{0:T(128)S(1)} %get-tuple-element.24), kind=kOutput, calls=%fused_computation.40 | convolution fusion | flops 15761408 | bytes 2655872 | tf_op jit(solution)/shard_map/oli,oln->in/dot_general | solution.py:66
  283.4 2.3 fusion.36
  285.8 5.1 %fusion.4 = f32[3,2,40,2048]{3,2,0,1:T(8,128)S(1)} fusion(f32[3,2,40,2048]{3,2,0,1:T(8,128)} %copy-done, f32[3,2,80,2048]{3,2,0,1:T(8,128)} %all-gather.9.cloned.1.call-done, f32[2,40,80,1]{2,1,3,0:T(8,128)S(1)} %fusion.36), kind=kOutput, calls=%fused_computation.15 | convolution fusion | flops 472350720 | bytes 7889920 | tf_op jit(solution)/shard_map/imn,vinc->vimc/dot_general | solution.py:73
  290.9 1.5 copy.109
  (97 shorter events, 11.9 us)
Async XLA Ops:
  6.5 121.7 %all-gather.11.cloned.1.call-start = ((), (), s32[]{:S(2)}) async-start(), calls=%async_computation.2 | async-start | bytes 2662400 | tf_op jit(solution)/shard_map/all_gather | solution.py:51
  23.8 3.4 %copy-start.10 = (s32[2,128]{1,0:T(2,128)S(1)}, s32[2,128]{1,0:T(2,128)}, u32[]{:S(2)}) copy-start(s32[2,128]{1,0:T(2,128)} %param.13) | copy-start | bytes 3076
  23.8 3.4 %copy-start.4 = (f32[2,128,3,64]{1,3,2,0:T(8,128)S(1)}, f32[2,128,3,64]{1,3,2,0:T(8,128)}, u32[]{:S(2)}) copy-start(f32[2,128,3,64]{1,3,2,0:T(8,128)} %param.14) | copy-start | bytes 589828
  27.2 17.5 %copy-start.3 = (f32[3,2,40,2048]{3,2,1,0:T(8,128)S(1)}, f32[3,2,40,2048]{3,2,1,0:T(8,128)}, u32[]{:S(2)}) copy-start(f32[3,2,40,2048]{3,2,1,0:T(8,128)} %param.11) | copy-start | bytes 5898244
  44.7 103.7 %all-gather.7.cloned.1.call-start = ((), (), s32[]{:S(2)}) async-start(), calls=%async_computation | async-start | bytes 5898240 | tf_op jit(solution)/shard_map/all_gather | solution.py:76
  46.2 1.6 copy-start.7
  46.2 1.6 copy-start.8
  46.2 1.7 copy-start.9
  46.2 219.7 %all-gather.13.cloned.1.call-start = ((), (), s32[]{:S(2)}) async-start(), calls=%async_computation.3 | async-start | bytes 2662400 | tf_op jit(solution)/shard_map/all_gather | solution.py:51
  128.3 3.6 %copy-start.1 = (f32[128,5120]{0,1:T(8,128)S(1)}, f32[128,5120]{0,1:T(8,128)}, u32[]{:S(2)}) copy-start(f32[128,5120]{0,1:T(8,128)} %all-gather.11.cloned.1.call-done) | copy-start | bytes 7864324
  138.1 2.6 copy-start.5
  138.1 2.6 copy-start.6
  153.2 1.9 copy-start
  186.8 99.0 %all-gather.9.cloned.1.call-start = ((), (), s32[]{:S(2)}) async-start(), calls=%async_computation.1 | async-start | bytes 5898240 | tf_op jit(solution)/shard_map/all_gather | solution.py:76
  265.9 3.6 %copy-start.2 = (f32[128,5120]{0,1:T(8,128)S(1)}, f32[128,5120]{0,1:T(8,128)}, u32[]{:S(2)}) copy-start(f32[128,5120]{0,1:T(8,128)} %all-gather.13.cloned.1.call-done) | copy-start | bytes 7864324
Sparse Core Ops, SparseCore 0:
  44.8 83.4 all-gather.10
  130.1 16.4 all-gather.6
  186.9 78.9 all-gather.12
  267.5 16.4 all-gather.8
where the time goes:
time: 299 us
  waiting for transfers between devices  159 us (53%)
  local copies, waits for them, and re-layouts  56.9 us (19%)
  matrix products  33.9 us (11%)
  blocking collectives  19.7 us (7%)
  other arithmetic  15.1 us (5%)
  between operations  13.6 us (5%)
    all_gather x2, waiting for transfers between devices, body(): profiles = lax.all_gather(ordered, ('level', 'member'), axis=1, tiled=True)  159 us
    all_gather x2, blocking collectives, body(): all_panels = lax.all_gather(local_panel, 'region', axis=0, tiled=True)  19.7 us
    gather x2, local copies, waits for them, and re-layouts, body(): ray_rows = jnp.take(column_rows, home_columns.reshape(-1), axis=0)  17.1 us
    dot_general x2, matrix products, body(): jnp.einsum('krvf,kvr->kf', ray_rows, home_weight, precision=highest)  9.96 us
    dot_general x2, matrix products, absorb(): jnp.einsum('imn,vinc->vimc', mixing, member_rows, precision=highest)  9.83 us
    dot_general x2, matrix products, body(): jnp.einsum('oli,oln->in', mean_coef, spread, precision=highest)  9.48 us
    sub x2, local copies, waits for them, and re-layouts, body(): spread = profiles - ens_mean[:, :, None]  7.87 us
    transpose x2, local copies, waits for them, and re-layouts, body(): profiles.transpose(0, 1, 3, 2, 4).reshape(occ_count, levels, members)  7.15 us
  transfers between devices with their start and end apart: 4, of which 2 were waited for; matrix products, arithmetic and copies ran while one was open for 14% of the time, Pallas kernels for 0%

commit v1 on v0

v1 whole, which is shorter than its diff:
```python
import math

import jax
import jax.numpy as jnp
from jax import lax
from jax.experimental import pallas as pl
from jax.experimental.pallas import tpu as pltpu
from jax.sharding import PartitionSpec as P

STEPS = 2
LANES = 128
SUB = 8
HIGHEST = lax.Precision.HIGHEST
F32 = jnp.float32
VMEM = pltpu.VMEM


def iota(shape, dim):
    return lax.broadcasted_iota(jnp.int32, shape, dim)


def dot(a, b):
    return jnp.dot(a, b, precision=HIGHEST, preferred_element_type=F32)


def predict_kernel(nl, nm, nc, regions, slots, rays,
                   state_ref, cols_ref, len_ref, weight_ref, owner_ref, locr_ref, locw_ref, obs_ref, var_ref,
                   msg_ref, later_ref, meta_ref,
                   held, picked, meta_in, tile_v, tile_s, state_sem, tile_sem):
    nv = state_ref.shape[0]
    region = lax.axis_index("region")
    level = lax.axis_index("level")
    copies = [pltpu.make_async_copy(state_ref.at[v], held.at[v], state_sem.at[v]) for v in range(nv)]
    for copy in copies:
        copy.start()
    lane_i = iota((LANES, LANES), 1)
    lane = lane_i.astype(F32)
    sub = iota((LANES, LANES), 0).astype(F32)

    def to_column(row):
        return jnp.sum(jnp.where(sub == lane, row, 0.0), axis=1, keepdims=True)

    region_f = region.astype(F32)
    total = None
    meta_in[...] = jnp.zeros_like(meta_in)
    for step in range(STEPS):
        cols = cols_ref[step].astype(F32)
        first = jnp.min(cols, axis=0, keepdims=True)
        home = jnp.zeros_like(first)
        for q in range(1, regions):
            home = home + (first >= float(q * nc)).astype(F32)
        same = (to_column(home) == home) & (sub < lane)
        rank = jnp.sum(same.astype(F32), axis=0, keepdims=True)
        place = to_column(home * float(slots) + rank)
        order = (place == lane).astype(F32)
        shifted = lane + (region_f - float(step)) * float(slots)
        mine = (place == shifted) & (lane_i >= step * slots) & (lane_i < (step + 1) * slots)
        live = sub[:rays] < len_ref[step:step + 1].astype(F32)
        data = [cols] + [jnp.where(live, weight_ref[step, v], 0.0) for v in range(nv)]
        term = dot(jnp.concatenate(data, axis=0), mine.astype(F32))
        total = term if total is None else total + term
        horiz = (owner_ref[step:step + 1] == region).astype(F32)
        listed = (locr_ref[step] == region).astype(F32)
        horiz = horiz + jnp.sum(locw_ref[step] * listed, axis=0, keepdims=True)
        for l in range(nl):
            meta_in[l:l + 1] = var_ref[step, pl.ds(level * nl + l, 1)]
            meta_in[nl + l:nl + l + 1] = obs_ref[step, pl.ds(level * nl + l, 1)]
        meta_in[2 * nl:2 * nl + 1] = horiz
        meta_ref[step] = dot(meta_in[...], order)
    picked[...] = total
    low = jnp.min(total[:rays], axis=0, keepdims=True) - region_f * float(nc)
    tile_v[...] = jnp.clip(low.astype(jnp.int32) // LANES, 0, nc // LANES - 2)
    scalars = pltpu.make_async_copy(tile_v, tile_s, tile_sem)
    scalars.start()
    scalars.wait()
    for copy in copies:
        copy.wait()
    groups = nl * nm // SUB
    packed = -(-groups // regions)
    lane8 = iota((SUB, LANES), 1)
    lane_r = lane[:rays]
    for step in range(STEPS):
        def eight(block, parts, step=step):
            first_slot = step * slots + block * SUB
            turned = pltpu.roll(picked[...], LANES - first_slot, 1)
            parts = list(parts)
            for u in range(SUB):
                tile = tile_s[0, first_slot + u]
                start = pl.multiple_of(tile * LANES, LANES)
                origin = region * nc + start
                place = turned[:rays, u:u + 1] - origin.astype(F32)
                sums = [None] * nl
                for half in range(2):
                    hit = place == lane_r + float(half * LANES)
                    for v in range(nv):
                        weights = turned[(v + 1) * rays:(v + 2) * rays, u:u + 1]
                        row = jnp.sum(jnp.where(hit, weights, 0.0), axis=0, keepdims=True)
                        for l in range(nl):
                            term = held[v, l, :, pl.ds(start + half * LANES, LANES)] * row
                            sums[l] = term if sums[l] is None else sums[l] + term
                for l in range(nl):
                    result = jnp.sum(sums[l], axis=1, keepdims=True)
                    for r in range(nm // SUB):
                        g = l * (nm // SUB) + r
                        spot = slots * (g % regions) + block * SUB + u
                        parts[g // regions] = jnp.where(lane8 == spot, result[r * SUB:(r + 1) * SUB], parts[g // regions])
            return tuple(parts)
        parts = lax.fori_loop(0, slots // SUB, eight, (jnp.zeros((SUB, LANES), F32),) * packed)
        for j in range(packed):
            if step == 0:
                for d in range(msg_ref.shape[0]):
                    msg_ref[d, j * SUB:(j + 1) * SUB] = parts[j]
            else:
                later_ref[j * SUB:(j + 1) * SUB] = parts[j]


def turn(x, by):
    by = by % LANES
    return pltpu.roll(x, by, 1) if by else x


def pack_mixing(a):
    members = 2 * a.shape[0]
    free = LANES - members
    lane8 = iota((SUB, LANES), 1)
    kept = a.shape[0] - SUB
    last = a[kept:]
    pieces = []
    for j in range(kept // SUB):
        part = a[j * SUB:(j + 1) * SUB]
        low, high = j * free, min((j + 1) * free, members)
        if low < high:
            part = part + turn(jnp.where((lane8 >= low) & (lane8 < high), last, 0.0), members - low)
        pieces.append(part)
    return jnp.concatenate(pieces, axis=0)


def unpack_mixing(p):
    rows = p.shape[0] + SUB
    members = 2 * rows
    free = LANES - members
    lane8 = iota((SUB, LANES), 1)
    last = jnp.zeros((SUB, LANES), F32)
    pieces = []
    for j in range(p.shape[0] // SUB):
        part = p[j * SUB:(j + 1) * SUB]
        low, high = j * free, min((j + 1) * free, members)
        if low < high:
            last = last + jnp.where((lane8 >= low) & (lane8 < high), turn(part, low - members), 0.0)
        pieces.append(jnp.where(lane8 < members, part, 0.0))
    return jnp.concatenate(pieces + [last], axis=0)


def local_kernel(step, nl, nm, regions, slots, levels, level_count, cores,
                 got_ref, meta_ref, msg_ref, local_ref, spread_ref):
    level = lax.axis_index("level")
    member = lax.axis_index("member")
    members = nm * cores
    scale = levels / 4.0
    lane8 = iota((SUB, LANES), 1)
    spread_ref[...] = jnp.zeros_like(spread_ref)
    mats = []
    for l in range(nl):
        rows = []
        for c in range(cores):
            for r in range(nm // SUB):
                g = l * (nm // SUB) + r
                j, k = g // regions, g % regions
                row = None
                for p in range(regions):
                    part = turn(got_ref[p * cores + c, j * SUB:(j + 1) * SUB], slots * (p - k))
                    row = part if row is None else jnp.where(lane8 >= slots * p, part, row)
                rows.append(row)
        predicted = jnp.concatenate(rows, axis=0)
        mean = jnp.sum(predicted, axis=0, keepdims=True) * (1.0 / members)
        spread = predicted - mean
        variance = jnp.sum(spread * spread, axis=0, keepdims=True) * (1.0 / (members - 1.0))
        obs_var = meta_ref[step, l:l + 1]
        obs_value = meta_ref[step, nl + l:nl + l + 1]
        horiz = meta_ref[step, 2 * nl:2 * nl + 1]
        total_var = variance + obs_var
        gain = (obs_value - mean) / total_var
        shrink = 1.0 / (1.0 + jnp.sqrt(obs_var / total_var))
        scaled = horiz * (1.0 / (members - 1.0))
        mean_coef = scaled * gain
        spread_coef = scaled * (shrink / total_var)
        spread_ref[l, 0:members] = spread
        own = spread_ref[l, pl.ds(pl.multiple_of(member * nm, SUB), nm)]
        left = mean_coef - spread_coef * own
        mats.append(lax.dot_general(left, spread_ref[l], (((1,), (1,)), ((), ())), precision=HIGHEST, preferred_element_type=F32))
    up = sum(math.exp(-(nl - 1 - l) / scale) * mats[l] for l in range(nl))
    down = sum(math.exp(-l / scale) * mats[l] for l in range(nl))
    up, down = pack_mixing(up), pack_mixing(down)
    for l in range(nl):
        local_ref[l] = pack_mixing(sum(math.exp(-abs(l - k) / scale) * mats[k] for k in range(nl)))
    for d in range(level_count):
        msg_ref[d] = jnp.where(d > level, up, down)


def combine_levels(nl, levels, level_count, got_ref, local_ref):
    level = lax.axis_index("level")
    scale = levels / 4.0
    fade = math.exp(-nl / scale)
    zero = jnp.zeros(got_ref.shape[1:], F32)
    below = lax.fori_loop(0, level, lambda d, acc: acc * fade + got_ref[d], zero)
    above = lax.fori_loop(0, level_count - 1 - level, lambda d, acc: acc * fade + got_ref[level_count - 1 - d], zero)
    return [
        unpack_mixing(math.exp(-(l + 1) / scale) * below + math.exp(-(nl - l) / scale) * above + local_ref[l])
        for l in range(nl)
    ]


def forecast_kernel(nl, nm, regions, slots, levels, level_count,
                    got_ref, local_ref, own_ref, other_ref, mix_ref, msg_ref, full_ref):
    member = lax.axis_index("member")
    lane8 = iota((SUB, LANES), 1)
    full_ref[...] = jnp.zeros_like(full_ref)
    groups = nl * nm // SUB
    packed = -(-groups // regions)
    parts = [jnp.zeros((SUB, LANES), F32) for _ in range(packed)]
    mats = combine_levels(nl, levels, level_count, got_ref, local_ref)
    for l in range(nl):
        mix_ref[l] = mats[l]
        rows = {}
        for name, ref, at in (("own", own_ref, member), ("other", other_ref, 1 - member)):
            pieces = []
            for r in range(nm // SUB):
                g = l * (nm // SUB) + r
                j, k = g // regions, g % regions
                pieces.append(turn(ref[j * SUB:(j + 1) * SUB], -slots * k))
            rows[name] = jnp.concatenate(pieces, axis=0)
            full_ref[l, pl.ds(pl.multiple_of(at * nm, SUB), nm)] = rows[name]
        result = rows["own"] + dot(mats[l], full_ref[l])
        for r in range(nm // SUB):
            g = l * (nm // SUB) + r
            j, k = g // regions, g % regions
            keep = (lane8 >= slots * k) & (lane8 < slots * (k + 1))
            parts[j] = jnp.where(keep, turn(result[r * SUB:(r + 1) * SUB], slots * k), parts[j])
    for d in range(msg_ref.shape[0]):
        for j in range(packed):
            msg_ref[d, j * SUB:(j + 1) * SUB] = parts[j]


def split(x):
    high = x.astype(jnp.bfloat16).astype(F32)
    return high, x - high


def update_kernel(nl, nm, levels, level_count,
                  got_ref, local_ref, mine_ref, theirs_ref, state_ref, other_ref, out_ref, full_ref, left_ref):
    member = lax.axis_index("member")
    members = 2 * nm

    @pl.when((pl.program_id(0) == 0) & (pl.program_id(1) == 0))
    def _():
        lane = iota((nm, LANES), 1)
        full_ref[...] = jnp.zeros_like(full_ref)
        mats = combine_levels(nl, levels, level_count, got_ref, local_ref)
        for l in range(nl):
            full_ref[l, pl.ds(pl.multiple_of(member * nm, SUB), nm)] = mine_ref[l]
            full_ref[l, pl.ds(pl.multiple_of((1 - member) * nm, SUB), nm)] = theirs_ref[l]
            both = mats[l] + mine_ref[l] + dot(mats[l], full_ref[l])
            swapped = jnp.where(lane < nm, turn(both, -nm), jnp.where(lane < members, turn(both, nm), 0.0))
            both = jnp.where(member == 0, both, swapped)
            high, low = split(both)
            again = turn(high, members)
            left_ref[l, :, 0:LANES] = high + jnp.where(lane >= members, again, 0.0)
            left_ref[l, :, LANES:] = jnp.where(lane < 2 * members - LANES, again, 0.0) + turn(low, 2 * members - LANES)

    own = state_ref[0, 0]
    high, low = split(jnp.concatenate([own, other_ref[0, 0]], axis=0))
    pad = jnp.zeros((2 * LANES - 3 * members, own.shape[1]), F32)
    right = jnp.concatenate([high, low, high, pad], axis=0).astype(jnp.bfloat16)
    left = left_ref[pl.program_id(0)].astype(jnp.bfloat16)
    out_ref[0, 0] = own + jnp.dot(left, right, preferred_element_type=F32)


def body(state, ray_cols, ray_len, ray_weight, owner, loc_regions, loc_weight, obs_value, obs_var):
    regions = lax.axis_size("region")
    level_count = lax.axis_size("level")
    cores = lax.axis_size("member")
    nv, nl, nm, nc = state.shape
    occ, rays = ray_cols.shape[1:]
    slots = occ // regions
    levels = nl * level_count
    assert occ == LANES and regions * slots == LANES and nm % SUB == 0 and cores == 2
    groups = nl * nm // SUB
    block = (-(-groups // regions) * SUB, LANES)
    mixing = (nm - SUB, LANES)
    whole = pl.BlockSpec(memory_space=VMEM)
    swap = [(0, 1), (1, 0)]

    def call(kernel, statics, outs, scratch, *args, specs=None, name=None):
        def wrapped(*refs):
            return kernel(*statics, *refs)
        return pl.pallas_call(
            wrapped,
            out_shape=[jax.ShapeDtypeStruct(s, F32) for s in outs],
            in_specs=specs or [whole] * len(args),
            out_specs=[whole] * len(outs),
            scratch_shapes=scratch,
            compiler_params=pltpu.CompilerParams(vmem_limit_bytes=32 * 2**20),
            name=name,
        )(*args)

    other_state = lax.ppermute(state, "member", swap)
    msg, later, meta = call(
        predict_kernel, (nl, nm, nc, regions, slots, rays),
        [(regions * cores,) + block, block, (STEPS, SUB, LANES)],
        [VMEM(state.shape, F32), VMEM(((nv + 1) * rays, LANES), F32), VMEM((SUB, LANES), F32),
         VMEM((1, LANES), jnp.int32), pltpu.SMEM((1, LANES), jnp.int32),
         pltpu.SemaphoreType.DMA((nv,)), pltpu.SemaphoreType.DMA],
        state, ray_cols.swapaxes(1, 2), ray_len, ray_weight.transpose(0, 2, 3, 1), owner,
        loc_regions.swapaxes(1, 2), loc_weight.swapaxes(1, 2), obs_value.swapaxes(1, 2), obs_var.swapaxes(1, 2),
        specs=[pl.BlockSpec(memory_space=pl.ANY)] + [whole] * 8, name="predict",
    )
    other_later = lax.ppermute(later, "member", swap)

    def assimilate(step, msg):
        got = lax.all_to_all(msg, ("region", "member"), 0, 0, tiled=True)
        out, local = call(
            local_kernel, (step, nl, nm, regions, slots, levels, level_count, cores),
            [(level_count,) + mixing, (nl,) + mixing], [VMEM((nl, LANES, LANES), F32)],
            got, meta, name="local",
        )
        return lax.all_to_all(out, "level", 0, 0, tiled=True), local

    got, local = assimilate(0, msg)
    mine, msg = call(
        forecast_kernel, (nl, nm, regions, slots, levels, level_count),
        [(nl, nm, LANES), (regions * cores,) + block], [VMEM((nl, LANES, LANES), F32)],
        got, local, later, other_later, name="forecast",
    )
    theirs = lax.ppermute(mine, "member", swap)
    got, local = assimilate(1, msg)
    tile = pl.BlockSpec((1, 1, nm, nc), lambda l, v: (v, l, 0, 0))

    def update(*refs):
        return update_kernel(nl, nm, levels, level_count, *refs)

    return pl.pallas_call(
        update,
        grid=(nl, nv),
        out_shape=jax.ShapeDtypeStruct(state.shape, F32),
        in_specs=[whole] * 4 + [tile] * 2,
        out_specs=tile,
        scratch_shapes=[VMEM((nl, LANES, LANES), F32), VMEM((nl, nm, 2 * LANES), F32)],
        compiler_params=pltpu.CompilerParams(vmem_limit_bytes=32 * 2**20),
        name="update",
    )(got, local, mine, theirs, state, other_state)


def solution(mesh):
    in_specs = (P(None, "level", "member", "region"), P(), P(), P(), P(), P(), P(), P(), P())
    out_specs = P(None, "level", "member", "region")
    return jax.shard_map(body, mesh=mesh, in_specs=in_specs, out_specs=out_specs, check_vma=False)
```

time: 299 us -> 98 us (0.33)
  waiting for transfers between devices: 159 us -> 28.6 us
  local copies, waits for them, and re-layouts: 56.9 us -> 7.71 us
  matrix products: 33.9 us -> 0 us
  Pallas kernels: 0 us -> 20.8 us
  starting transfers between devices: 0.35 us -> 18 us
  other arithmetic: 15.1 us -> 0 us
  between operations: 13.6 us -> 0.05 us
    all_gather x4 -> x0, waiting for transfers between devices: 159 us -> none  [the longest x2 159 us: body(): profiles = lax.all_gather(ordered, ('level', 'member'), axis=1, tiled=True)]
    dot_general x8 -> x0, matrix products: 33.9 us -> none  [the longest x2 9.96 us: body(): jnp.einsum('krvf,kvr->kf', ray_rows, home_weight, precision=highest)]
    all_to_all x0 -> x2, waiting for transfers between devices: none -> 24.3 us  [assimilate(): return (lax.all_to_all(out, 'level', 0, 0, tiled=True), local)]
    gather x10 -> x0, local copies, waits for them, and re-layouts: 22.2 us -> none  [the longest x2 17.1 us: body(): ray_rows = jnp.take(column_rows, home_columns.reshape(-1), axis=0)]
    all_to_all x0 -> x2, blocking collectives: none -> 21.2 us  [assimilate(): got = lax.all_to_all(msg, ('region', 'member'), 0, 0, tiled=True)]
    pallas_call x0 -> x5, Pallas kernels: none -> 20.8 us  [the longest x4 14.8 us: call(): pl.pallas_call(wrapped, out_shape=[jax.ShapeDtypeStruct(s, F32) for s in...]
    all_gather x2 -> x0, blocking collectives: 19.7 us -> none  [body(): all_panels = lax.all_gather(local_panel, 'region', axis=0, tiled=True)]
    all_to_all x0 -> x2, starting transfers between devices: none -> 15.5 us  [assimilate(): return (lax.all_to_all(out, 'level', 0, 0, tiled=True), local)]
  transfers between devices with their start and end apart: 4 -> 5, of which waited for: 2 -> 4; matrix products, arithmetic and copies ran while one was open for 14% -> 0% of each run, Pallas kernels for 0% -> 2%
where the time goes in v1:
time: 98 us; the launch traced here: 96.3 us
  waiting for transfers between devices  28.6 us (29%)
  blocking collectives  21.2 us (22%)
  Pallas kernels  20.8 us (21%)
  starting transfers between devices  18 us (18%)
  local copies, waits for them, and re-layouts  7.71 us (8%)
    all_to_all x2, waiting for transfers between devices, assimilate(): return (lax.all_to_all(out, 'level', 0, 0, tiled=True), local)  24.3 us
    all_to_all x2, blocking collectives, assimilate(): got = lax.all_to_all(msg, ('region', 'member'), 0, 0, tiled=True)  21.2 us
    all_to_all x2, starting transfers between devices, assimilate(): return (lax.all_to_all(out, 'level', 0, 0, tiled=True), local)  15.5 us
    pallas_call x4, Pallas kernels, call(): pl.pallas_call(wrapped, out_shape=[jax.ShapeDtypeStruct(s, F32) for s in...  14.8 us
    unnamed x20, local copies, waits for them, and re-layouts  7.71 us
    pallas_call x1, Pallas kernels, body(): pl.pallas_call(update, grid=(nl, nv), out_shape=jax.ShapeDtypeStruct(stat...  6.03 us
    ppermute x1, waiting for transfers between devices, body(): other_later = lax.ppermute(later, 'member', swap)  3.38 us
  transfers between devices with their start and end apart: 5, of which 4 were waited for; matrix products, arithmetic and copies ran while one was open for 0% of the time, Pallas kernels for 2%

profile of v1, /device:TPU:1, one launch (start us, length us, event | category | flops | bytes accessed | tf_op | source)
XLA Modules:
  0.0 96.3 jit_solution(6606900256795934337)
XLA Ops:
  0.0 0.0 copy-start
  0.0 1.5 %copy-done = f32[3,2,40,2048]{3,2,1,0:T(8,128)S(1)} copy-done((f32[3,2,40,2048]{3,2,1,0:T(8,128)S(1)}, f32[3,2,40,2048]{3,2,1,0:T(8,128)}, u32[]{:S(2)}) %copy-start) | copy-done | bytes 1966104
  1.5 0.0 copy-start.2
  1.5 0.9 copy-done.2
  2.5 0.0 copy-start.3
  2.5 0.8 copy-done.3
  3.3 0.0 copy-start.4
  3.3 0.8 copy-done.4
  4.2 0.0 copy-start.5
  4.2 0.8 copy-done.5
  5.0 0.7 copy-done.6
  5.7 0.7 copy-done.7
  6.4 0.7 copy-done.8
  7.0 0.7 copy-done.9
  7.7 11.4 %predict.1 = (f32[8,24,128]{2,1,0:T(8,128)S(1)}, f32[24,128]{1,0:T(8,128)S(1)}, f32[2,8,128]{2,1,0:T(8,128)S(1)}) custom-call(f32[3,2,40,2048]{3,2,1,0:T(8,128)S(1)} %copy-done, s32[2,64,128]{2,1,0:T(8,128)S(1)} %bitcast.7, s32[2,128]{1,0:T(2,128)S(1)} %copy-done.8, f32[2,3,64,128]{3,2,1,0:T(8,128)S(1)} %bitcast.6, s32[2,128]{1,0:T(2,128)S(1)} %copy-done.9, ...), custom_call_target="tpu_custom_call" | custom-call | tf_op jit(solution)/shard_map/predict/pallas_call | solution.py:296
  19.1 10.6 %all_to_all.20.refs_0_ = f32[8,24,128]{2,1,0:T(8,128)S(1)} all-to-all(f32[8,24,128]{2,1,0:T(8,128)S(1)} %get-tuple-element.14), channel_id=1, replica_groups=mesh['region'=4,'level'=32,'member'=2] {'region','member'}, dimensions={0} | all-to-all | bytes 196608 | tf_op jit(solution)/shard_map/all_to_all | solution.py:320
  29.7 1.4 %local.2 = (f32[32,32,128]{2,1,0:T(8,128)}, f32[2,32,128]{2,1,0:T(8,128)S(1)}) custom-call(f32[8,24,128]{2,1,0:T(8,128)S(1)} %all_to_all.20.refs_0_, f32[2,8,128]{2,1,0:T(8,128)S(1)} %get-tuple-element.15.refs_1_), custom_call_target="tpu_custom_call" | custom-call | tf_op jit(solution)/shard_map/local/pallas_call | solution.py:296
  31.1 11.2 %all-to-all-start.1 = ((f32[32,32,128]{2,1,0:T(8,128)}), f32[32,32,128]{2,1,0:T(8,128)S(1)}, u32[]{:S(2)}, u32[]{:S(2)}) async-start(f32[32,32,128]{2,1,0:T(8,128)} %get-tuple-element.16), calls=%async_computation.1 | async-start | bytes 1048576 | tf_op jit(solution)/shard_map/all_to_all | solution.py:326
  42.3 0.0 copy-done.1
  42.3 1.2 %collective-permute-start.2 = (f32[3,2,40,2048]{3,2,1,0:T(8,128)S(1)}, f32[3,2,40,2048]{3,2,1,0:T(8,128)}, u32[]{:S(2)}, u32[]{:S(2)}) collective-permute-start(f32[3,2,40,2048]{3,2,1,0:T(8,128)S(1)} %copy-done.1), channel_id=1, source_target_pairs={{0,1},{1,0},{2,3},{3,2},{4,5},{5,4},{6,7},{7,6},{8,9},{9,8},{10,11... | collective-permute-start | bytes 5898248 | tf_op jit(solution)/shard_map/ppermute | solution.py:306
  43.5 0.1 collective-permute-start
  43.6 3.4 %collective-permute-done.refs_3_ = f32[24,128]{1,0:T(8,128)S(1)} collective-permute-done((f32[24,128]{1,0:T(8,128)S(1)}, f32[24,128]{1,0:T(8,128)S(1)}, u32[]{:S(2)}, u32[]{:S(2)}) %collective-permute-start) | collective-permute-done | bytes 12320 | tf_op jit(solution)/shard_map/ppermute | solution.py:317
  47.0 10.8 %all-to-all-done.1.refs_0_ = f32[32,32,128]{2,1,0:T(8,128)S(1)} async-done(((f32[32,32,128]{2,1,0:T(8,128)}), f32[32,32,128]{2,1,0:T(8,128)S(1)}, u32[]{:S(2)}, u32[]{:S(2)}) %all-to-all-start.1) | async-done | bytes 524320 | tf_op jit(solution)/shard_map/all_to_all | solution.py:326
  57.9 0.6 forecast.1
  58.4 10.6 %all_to_all.21.refs_0_ = f32[8,24,128]{2,1,0:T(8,128)S(1)} all-to-all(f32[8,24,128]{2,1,0:T(8,128)S(1)} %get-tuple-element.19), channel_id=1, replica_groups=mesh['region'=4,'level'=32,'member'=2] {'region','member'}, dimensions={0} | all-to-all | bytes 196608 | tf_op jit(solution)/shard_map/all_to_all | solution.py:320
  69.0 1.4 %local.3 = (f32[32,32,128]{2,1,0:T(8,128)}, f32[2,32,128]{2,1,0:T(8,128)S(1)}) custom-call(f32[8,24,128]{2,1,0:T(8,128)S(1)} %all_to_all.21.refs_0_, f32[2,8,128]{2,1,0:T(8,128)S(1)} %get-tuple-element.15.refs_1_), custom_call_target="tpu_custom_call" | custom-call | tf_op jit(solution)/shard_map/local/pallas_call | solution.py:296
  70.4 4.3 %all-to-all-start.3 = ((f32[32,32,128]{2,1,0:T(8,128)}), f32[32,32,128]{2,1,0:T(8,128)S(1)}, u32[]{:S(2)}, u32[]{:S(2)}) async-start(f32[32,32,128]{2,1,0:T(8,128)} %get-tuple-element.20), calls=%async_computation.3 | async-start | bytes 1048576 | tf_op jit(solution)/shard_map/all_to_all | solution.py:326
  74.8 1.2 %collective-permute-start.1 = (f32[2,40,128]{2,1,0:T(8,128)S(1)}, f32[2,40,128]{2,1,0:T(8,128)S(1)}, u32[]{:S(2)}, u32[]{:S(2)}) collective-permute-start(f32[2,40,128]{2,1,0:T(8,128)S(1)} %get-tuple-element.22.refs_2_), channel_id=1, source_target_pairs={{0,1},{1,0},{2,3},{3,2},{4,5},{5,4},{6,7},{7,6},{8,9},{9,8},{10,11... | collective-permute-start | bytes 122888 | tf_op jit(solution)/shard_map/ppermute | solution.py:334
  75.9 0.9 collective-permute-done.1.refs_3_
  76.8 0.0 collective-permute-done.2.refs_5_
  76.8 13.5 %all-to-all-done.3.refs_0_ = f32[32,32,128]{2,1,0:T(8,128)S(1)} async-done(((f32[32,32,128]{2,1,0:T(8,128)}), f32[32,32,128]{2,1,0:T(8,128)S(1)}, u32[]{:S(2)}, u32[]{:S(2)}) %all-to-all-start.3) | async-done | bytes 524320 | tf_op jit(solution)/shard_map/all_to_all | solution.py:326
  90.3 6.0 %update.1 = f32[3,2,40,2048]{3,2,1,0:T(8,128)} custom-call(f32[32,32,128]{2,1,0:T(8,128)S(1)} %all-to-all-done.3.refs_0_, f32[2,32,128]{2,1,0:T(8,128)S(1)} %get-tuple-element.21.refs_1_, f32[2,40,128]{2,1,0:T(8,128)S(1)} %get-tuple-element.22.refs_2_, f32[2,40,128]{2,1,0:T(8,128)S(1)} %collective-permute-done.1.refs_3_, f32[3,2,40,2048]{3,2,1,0:T(8,128)S(1)} %copy-done.1, ...), custom_call_target="tpu_custom_call" | custom-call | tf_op jit(solution)/shard_map/update/pallas_call | solution.py:341
  (5 shorter events, 0.0 us)
Async XLA Ops:
  0.0 1.5 %copy-start = (f32[3,2,40,2048]{3,2,1,0:T(8,128)S(1)}, f32[3,2,40,2048]{3,2,1,0:T(8,128)}, u32[]{:S(2)}) copy-start(f32[3,2,40,2048]{3,2,1,0:T(8,128)} %refs_4_.3) | copy-start | bytes 5898244
  1.5 0.9 copy-start.2
  2.5 0.8 copy-start.3
  3.3 0.8 copy-start.4
  4.2 0.8 copy-start.5
  5.0 0.7 copy-start.6
  5.7 0.7 copy-start.7
  6.4 0.7 copy-start.8
  7.0 0.7 copy-start.9
  7.7 34.6 %copy-start.1 = (f32[3,2,40,2048]{3,2,1,0:T(8,128)S(1)}, f32[3,2,40,2048]{3,2,1,0:T(8,128)}, u32[]{:S(2)}) copy-start(f32[3,2,40,2048]{3,2,1,0:T(8,128)} %refs_4_.3) | copy-start | bytes 5898244
  31.1 26.7 %all-to-all-start.1 = ((f32[32,32,128]{2,1,0:T(8,128)}), f32[32,32,128]{2,1,0:T(8,128)S(1)}, u32[]{:S(2)}, u32[]{:S(2)}) async-start(f32[32,32,128]{2,1,0:T(8,128)} %get-tuple-element.16), calls=%async_computation.1 | async-start | bytes 1048576 | tf_op jit(solution)/shard_map/all_to_all | solution.py:326
  42.3 34.5 %collective-permute-start.2 = (f32[3,2,40,2048]{3,2,1,0:T(8,128)S(1)}, f32[3,2,40,2048]{3,2,1,0:T(8,128)}, u32[]{:S(2)}, u32[]{:S(2)}) collective-permute-start(f32[3,2,40,2048]{3,2,1,0:T(8,128)S(1)} %copy-done.1), channel_id=1, source_target_pairs={{0,1},{1,0},{2,3},{3,2},{4,5},{5,4},{6,7},{7,6},{8,9},{9,8},{10,11... | collective-permute-start | bytes 5898248 | tf_op jit(solution)/shard_map/ppermute | solution.py:306
  43.5 3.5 %collective-permute-start = (f32[24,128]{1,0:T(8,128)S(1)}, f32[24,128]{1,0:T(8,128)S(1)}, u32[]{:S(2)}, u32[]{:S(2)}) collective-permute-start(f32[24,128]{1,0:T(8,128)S(1)} %get-tuple-element.18.refs_2_), channel_id=1, source_target_pairs={{0,1},{1,0},{2,3},{3,2},{4,5},{5,4},{6,7},{7,6},{8,9},{9,8},{10,11... | collective-permute-start | bytes 36872 | tf_op jit(solution)/shard_map/ppermute | solution.py:317
  70.4 19.9 %all-to-all-start.3 = ((f32[32,32,128]{2,1,0:T(8,128)}), f32[32,32,128]{2,1,0:T(8,128)S(1)}, u32[]{:S(2)}, u32[]{:S(2)}) async-start(f32[32,32,128]{2,1,0:T(8,128)} %get-tuple-element.20), calls=%async_computation.3 | async-start | bytes 1048576 | tf_op jit(solution)/shard_map/all_to_all | solution.py:326
  74.8 2.1 %collective-permute-start.1 = (f32[2,40,128]{2,1,0:T(8,128)S(1)}, f32[2,40,128]{2,1,0:T(8,128)S(1)}, u32[]{:S(2)}, u32[]{:S(2)}) collective-permute-start(f32[2,40,128]{2,1,0:T(8,128)S(1)} %get-tuple-element.22.refs_2_), channel_id=1, source_target_pairs={{0,1},{1,0},{2,3},{3,2},{4,5},{5,4},{6,7},{7,6},{8,9},{9,8},{10,11... | collective-permute-start | bytes 122888 | tf_op jit(solution)/shard_map/ppermute | solution.py:334

commit v2 on v1

v2 whole, which is shorter than its diff:
```python
import math

import jax
import jax.numpy as jnp
from jax import lax
from jax.experimental import pallas as pl
from jax.experimental.pallas import tpu as pltpu
from jax.sharding import PartitionSpec as P

STEPS = 2
LANES = 128
SUB = 8
HIGHEST = lax.Precision.HIGHEST
F32 = jnp.float32
BF16 = jnp.bfloat16
VMEM = pltpu.VMEM
BY_LANES = (((1,), (1,)), ((), ()))


def iota(shape, dim):
    return lax.broadcasted_iota(jnp.int32, shape, dim)


def dot(a, b):
    return jnp.dot(a, b, precision=HIGHEST, preferred_element_type=F32)


def turn(x, by):
    by = by % LANES
    return pltpu.roll(x, by, 1) if by else x


def pick(chosen, values):
    chosen = chosen.astype(BF16)
    total = None
    for _ in range(3):
        part = values.astype(BF16)
        term = lax.dot_general(chosen, part, BY_LANES, preferred_element_type=F32)
        total = term if total is None else total + term
        values = values - part.astype(F32)
    return total


def predict_kernel(nl, nm, nc, regions, slots, rays,
                   state_hbm, cols_hbm, len_hbm, weight_hbm, owner_hbm, locr_hbm, locw_hbm, obs_hbm, var_hbm,
                   msg_ref, later_ref, meta_ref,
                   held, cols_ref, len_ref, weight_ref, owner_ref, locr_ref, locw_ref, obs_ref, var_ref,
                   rows_ref, masked, sorted_ref, meta_in, place_v, place_s, state_sem, arg_sem, place_sem):
    nv = state_hbm.shape[0]
    region = lax.axis_index("region")
    level = lax.axis_index("level")
    pairs = [(cols_hbm, cols_ref), (len_hbm, len_ref), (weight_hbm, weight_ref), (owner_hbm, owner_ref),
             (locr_hbm, locr_ref), (locw_hbm, locw_ref), (obs_hbm, obs_ref), (var_hbm, var_ref)]
    fetches = [pltpu.make_async_copy(a, b, arg_sem.at[i]) for i, (a, b) in enumerate(pairs)]
    for copy in fetches:
        copy.start()
    copies = [pltpu.make_async_copy(state_hbm.at[v], held.at[v], state_sem.at[v]) for v in range(nv)]
    for copy in copies:
        copy.start()
    for copy in fetches:
        copy.wait()
    lane = iota((LANES, LANES), 1)
    sub = iota((LANES, LANES), 0)
    sub8 = iota((SUB, LANES), 0)
    earlier = (sub < lane).astype(BF16)
    region_f = region.astype(F32)
    firsts, places, worst = [], [], None
    for step in range(STEPS):
        cols = cols_ref[step].astype(F32)
        first = jnp.min(cols, axis=0, keepdims=True)
        off = jnp.max(jnp.abs(cols - first - sub[:rays].astype(F32)))
        worst = off if worst is None else jnp.maximum(worst, off)
        home = jnp.zeros_like(first)
        for q in range(1, regions):
            home = home + (first >= float(q * nc)).astype(F32)
        at_home = (sub8.astype(F32) == home).astype(F32)
        count = jnp.dot(at_home.astype(BF16), earlier, preferred_element_type=F32)
        rank = jnp.sum(at_home * count, axis=0, keepdims=True)
        places.append(home * float(slots) + rank)
        firsts.append(first)
        live = sub[:rays] < len_ref[step:step + 1]
        for v in range(nv):
            masked[v, :, step * LANES:(step + 1) * LANES] = jnp.where(live, weight_ref[step, v], 0.0)
    slot = sub[:STEPS * slots].astype(F32)
    mine = []
    for step in range(STEPS):
        ours = (slot >= float(step * slots)) & (slot < float((step + 1) * slots))
        mine.append(((places[step] == slot + (region_f - float(step)) * float(slots)) & ours).astype(F32))
    mine = jnp.concatenate(mine, axis=1)
    first = jnp.broadcast_to(jnp.concatenate(firsts, axis=1), (SUB, STEPS * LANES))
    own_first = jnp.zeros((SUB, STEPS * slots), F32)
    for _ in range(2):
        part = first.astype(BF16)
        own_first = own_first + lax.dot_general(part, mine.astype(BF16), BY_LANES, preferred_element_type=F32)
        first = first - part.astype(F32)
    low = own_first.astype(jnp.int32) - region * nc
    tile = jnp.clip(low // LANES, 0, nc // LANES - 2)
    place_v[...] = jnp.zeros_like(place_v)
    place_v[:, 0:STEPS * slots] = jnp.where(sub8[:, :STEPS * slots] == 0, tile, jnp.clip(low - tile * LANES, 0, 2 * LANES - 1))
    scalars = pltpu.make_async_copy(place_v, place_s, place_sem)
    scalars.start()

    @pl.when(worst > 0.5)
    def _():
        column = jnp.concatenate([cols_ref[s].astype(F32) - firsts[s] for s in range(STEPS)], axis=1)

        def one(d, carry):
            hit = column == d.astype(F32)
            for v in range(nv):
                sorted_ref[v, pl.ds(d, 1)] = jnp.sum(jnp.where(hit, masked[v], 0.0), axis=0, keepdims=True)
            return carry
        lax.fori_loop(0, rays, one, 0)
        masked[...] = sorted_ref[...]

    for v in range(nv):
        rows_ref[v] = jnp.zeros((STEPS * slots, LANES), F32)
        rows_ref[v, :, 0:rays] = pick(mine, masked[v])
    meta_in[...] = jnp.zeros_like(meta_in)
    for step in range(STEPS):
        horiz = (owner_ref[step:step + 1] == region).astype(F32)
        listed = (locr_ref[step] == region).astype(F32)
        horiz = horiz + jnp.sum(locw_ref[step] * listed, axis=0, keepdims=True)
        for l in range(nl):
            meta_in[l:l + 1] = var_ref[step, pl.ds(level * nl + l, 1)]
            meta_in[nl + l:nl + l + 1] = obs_ref[step, pl.ds(level * nl + l, 1)]
        meta_in[2 * nl:2 * nl + 1] = horiz
        order = (places[step] == sub.astype(F32)).astype(F32)
        meta_ref[step] = lax.dot_general(meta_in[...], order, BY_LANES, precision=HIGHEST, preferred_element_type=F32)
    scalars.wait()
    for copy in copies:
        copy.wait()
    groups = nl * nm // SUB
    packed = -(-groups // regions)
    lane8 = iota((SUB, LANES), 1)
    for step in range(STEPS):
        def eight(block, parts, step=step):
            parts = list(parts)
            for u in range(SUB):
                slot = block * SUB + u
                tile = place_s[0, step * slots + slot]
                shift = place_s[1, step * slots + slot]
                start = pl.multiple_of(tile * LANES, LANES)
                sums = [None] * nl
                for v in range(nv):
                    row = jnp.broadcast_to(rows_ref[v, pl.ds(step * slots + slot, 1)], (SUB, LANES))
                    row = pltpu.roll(row, shift & (LANES - 1), 1)
                    for half in range(2):
                        kept = jnp.where((lane8 >= shift) if half == 0 else (lane8 < shift), row, 0.0)
                        for l in range(nl):
                            data = held[v, l, :, pl.ds(start + half * LANES, LANES)]
                            terms = [data[r * SUB:(r + 1) * SUB] * kept for r in range(nm // SUB)]
                            sums[l] = terms if sums[l] is None else [a + b for a, b in zip(sums[l], terms)]
                for l in range(nl):
                    for r in range(nm // SUB):
                        g = l * (nm // SUB) + r
                        result = jnp.sum(sums[l][r], axis=1, keepdims=True)
                        parts[g // regions] = jnp.where(lane8 == slots * (g % regions) + slot, result, parts[g // regions])
            return tuple(parts)
        parts = lax.fori_loop(0, slots // SUB, eight, (jnp.zeros((SUB, LANES), F32),) * packed)
        for j in range(packed):
            if step == 0:
                for d in range(msg_ref.shape[0]):
                    msg_ref[d, j * SUB:(j + 1) * SUB] = parts[j]
            else:
                later_ref[j * SUB:(j + 1) * SUB] = parts[j]


def skew(x, by, sign):
    x = turn(x, by)
    sub8 = iota((SUB, LANES), 0)
    for bit in range(3):
        x = jnp.where((sub8 >> bit) % 2 == 1, turn(x, sign << bit), x)
    return x


def pack_mixing(s, w):
    nm = s.shape[0]
    width, across = nm + 2, LANES // (nm + 2)
    lane8 = iota((SUB, LANES), 1)
    pieces = []
    for g in range(nm // SUB):
        at = width * (g % across)
        part = skew(s[g * SUB:(g + 1) * SUB], at - g * SUB, -1)
        part = jnp.where((lane8 >= at) & (lane8 <= at + nm), part, 0.0)
        part = jnp.where(lane8 == at + nm + 1, w[g * SUB:(g + 1) * SUB], part)
        if g % across:
            pieces[-1] = pieces[-1] + part
        else:
            pieces.append(part)
    return jnp.concatenate(pieces, axis=0)


def unpack_mixing(p, nm):
    width, across = nm + 2, LANES // (nm + 2)
    lane8 = iota((SUB, LANES), 1)
    band, w = [], []
    for g in range(nm // SUB):
        at, j = width * (g % across), g // across
        part = p[j * SUB:(j + 1) * SUB]
        band.append(skew(jnp.where((lane8 >= at) & (lane8 <= at + nm), part, 0.0), g * SUB - at, 1))
        w.append(part[:, at + nm + 1:at + nm + 2])
    return jnp.concatenate(band, axis=0), jnp.concatenate(w, axis=0)


def mixing_rows(first, second, nm):
    (band, w), (band_2, w_2) = first, second
    lane = iota((nm, LANES), 1)
    sub = iota((nm, LANES), 0)
    top = jnp.where((lane > sub) & (lane < nm), band, 0.0)
    low = jnp.where(lane < sub, turn(band_2, -nm), 0.0)
    top = jnp.where(lane == nm, w, top)
    low = jnp.where(lane == nm, w_2, low)
    rest = jnp.zeros((LANES - 2 * nm, LANES), F32)
    turned = jnp.concatenate([top, low, rest], axis=0).T
    return turned[nm:nm + 1] - (band + turned[:nm])


def local_kernel(step, nl, nm, regions, slots, levels, level_count, cores,
                 got_ref, meta_ref, msg_ref, local_ref, spread_ref):
    level = lax.axis_index("level")
    member = lax.axis_index("member")
    members = nm * cores
    scale = levels / 4.0
    lane8 = iota((SUB, LANES), 1)
    mats = []
    for l in range(nl):
        rows = []
        for c in (member, 1 - member):
            for r in range(nm // SUB):
                g = l * (nm // SUB) + r
                j, k = g // regions, g % regions
                row = None
                for p in range(regions):
                    part = turn(got_ref[p * cores + c, j * SUB:(j + 1) * SUB], slots * (p - k))
                    row = part if row is None else jnp.where(lane8 >= slots * p, part, row)
                rows.append(row)
        predicted = jnp.concatenate(rows, axis=0)
        mean = jnp.sum(predicted, axis=0, keepdims=True) * (1.0 / members)
        spread = predicted - mean
        variance = jnp.sum(spread * spread, axis=0, keepdims=True) * (1.0 / (members - 1.0))
        obs_var = meta_ref[step, l:l + 1]
        obs_value = meta_ref[step, nl + l:nl + l + 1]
        horiz = meta_ref[step, 2 * nl:2 * nl + 1]
        total_var = variance + obs_var
        gain = (obs_value - mean) / total_var
        shrink = 1.0 / (1.0 + jnp.sqrt(obs_var / total_var))
        scaled = horiz * (1.0 / (members - 1.0))
        spread_ref[l, 0:members] = spread
        spread_ref[l, members:] = jnp.zeros((LANES - members, LANES), F32)
        own = spread[:nm]
        left = scaled * (shrink / total_var) * own
        s = lax.dot_general(left, spread_ref[l], BY_LANES, precision=HIGHEST, preferred_element_type=F32)
        mats.append(pack_mixing(s, jnp.sum(scaled * gain * own, axis=1, keepdims=True)))
    up = sum(math.exp(-(nl - 1 - l) / scale) * mats[l] for l in range(nl))
    down = sum(math.exp(-l / scale) * mats[l] for l in range(nl))
    for l in range(nl):
        local_ref[l] = sum(math.exp(-abs(l - k) / scale) * mats[k] for k in range(nl))
    for d in range(level_count):
        msg_ref[d] = jnp.where(d > level, up, down)


def combine_kernel(nl, levels, level_count, got_ref, local_ref, *refs):
    out_ref = refs[-1]
    level = lax.axis_index("level")
    scale = levels / 4.0
    fade = math.exp(-nl / scale)
    rows = got_ref.shape[1]
    zero = jnp.zeros(got_ref.shape[1:], F32)
    below = lax.fori_loop(0, level, lambda d, acc: acc * fade + got_ref[d], zero)
    above = lax.fori_loop(0, level_count - 1 - level, lambda d, acc: acc * fade + got_ref[level_count - 1 - d], zero)
    for l in range(nl):
        out_ref[l * rows:(l + 1) * rows] = (
            math.exp(-(l + 1) / scale) * below + math.exp(-(nl - l) / scale) * above + local_ref[l]
        )
    if len(refs) > 1:
        out_ref[nl * rows:] = refs[0][...]


def forecast_kernel(nl, nm, regions, slots, own_ref, other_ref, mix_ref, msg_ref, full_ref):
    lane8 = iota((SUB, LANES), 1)
    lane = iota((nm, LANES), 1)
    groups = nl * nm // SUB
    packed = -(-groups // regions)
    first = own_ref.shape[0] - packed * SUB
    rows = first // nl
    parts = [jnp.zeros((SUB, LANES), F32) for _ in range(packed)]
    for l in range(nl):
        pieces = []
        for ref in (own_ref, other_ref):
            for r in range(nm // SUB):
                g = l * (nm // SUB) + r
                j, k = g // regions, g % regions
                pieces.append(turn(ref[first + j * SUB:first + (j + 1) * SUB], -slots * k))
        own = jnp.concatenate(pieces[:nm // SUB], axis=0)
        pieces.append(jnp.zeros((LANES - 2 * nm, LANES), F32))
        full_ref[l] = jnp.concatenate(pieces, axis=0)
        bands = [unpack_mixing(ref[l * rows:(l + 1) * rows], nm) for ref in (own_ref, other_ref)]
        upper = mixing_rows(bands[0], bands[1], nm)
        mix_ref[l, 0:nm] = upper
        result = own + dot(upper, full_ref[l])
        for r in range(nm // SUB):
            g = l * (nm // SUB) + r
            j, k = g // regions, g % regions
            keep = (lane8 >= slots * k) & (lane8 < slots * (k + 1))
            parts[j] = jnp.where(keep, turn(result[r * SUB:(r + 1) * SUB], slots * k), parts[j])
        lower = mixing_rows(bands[1], bands[0], nm)
        swapped = jnp.where(lane < nm, turn(lower, -nm), jnp.where(lane < 2 * nm, turn(lower, nm), 0.0))
        mix_ref[l, nm:2 * nm] = swapped
        mix_ref[l, 2 * nm:] = jnp.zeros((LANES - 2 * nm, LANES), F32)
    for d in range(msg_ref.shape[0]):
        for j in range(packed):
            msg_ref[d, j * SUB:(j + 1) * SUB] = parts[j]


def split(x):
    high = x.astype(BF16).astype(F32)
    return high, x - high


def update_kernel(nl, nm, own_ref, other_ref, mix_ref, state_hbm, theirs_hbm, out_hbm,
                  mine_v, theirs_v, out_v, left_ref, in_sem, out_sem):
    nv = state_hbm.shape[0]
    members = 2 * nm
    blocks = [(v, l) for l in range(nl) for v in range(nv)]
    fetches = []
    for i, (v, l) in enumerate(blocks):
        pair = (pltpu.make_async_copy(state_hbm.at[v, l], mine_v.at[v, l], in_sem.at[2 * i]),
                pltpu.make_async_copy(theirs_hbm.at[v, l], theirs_v.at[v, l], in_sem.at[2 * i + 1]))
        for copy in pair:
            copy.start()
        fetches.append(pair)
    rows = own_ref.shape[0] // nl
    lane = iota((nm, LANES), 1)
    for l in range(nl):
        bands = [unpack_mixing(ref[l * rows:(l + 1) * rows], nm) for ref in (own_ref, other_ref)]
        second = mixing_rows(bands[0], bands[1], nm)
        both = second + mix_ref[l, 0:nm] + dot(second, mix_ref[l])
        high, low = split(both)
        again = turn(high, members)
        left_ref[l, :, 0:LANES] = high + jnp.where(lane >= members, again, 0.0)
        left_ref[l, :, LANES:] = jnp.where(lane < 2 * members - LANES, again, 0.0) + turn(low, 2 * members - LANES)
    pad = jnp.zeros((2 * LANES - 3 * members, state_hbm.shape[3]), F32)
    stores = []
    for i, (v, l) in enumerate(blocks):
        for copy in fetches[i]:
            copy.wait()
        own = mine_v[v, l]
        high, low = split(jnp.concatenate([own, theirs_v[v, l]], axis=0))
        right = jnp.concatenate([high, low, high, pad], axis=0).astype(BF16)
        out_v[v, l] = own + jnp.dot(left_ref[l].astype(BF16), right, preferred_element_type=F32)
        copy = pltpu.make_async_copy(out_v.at[v, l], out_hbm.at[v, l], out_sem.at[i])
        copy.start()
        stores.append(copy)
    for copy in stores:
        copy.wait()


def body(state, ray_cols, ray_len, ray_weight, owner, loc_regions, loc_weight, obs_value, obs_var):
    regions = lax.axis_size("region")
    level_count = lax.axis_size("level")
    cores = lax.axis_size("member")
    nv, nl, nm, nc = state.shape
    occ, rays = ray_cols.shape[1:]
    slots = occ // regions
    levels = nl * level_count
    assert occ == LANES and regions * slots == LANES and nm % SUB == 0 and cores == 2
    groups = nl * nm // SUB
    block = (-(-groups // regions) * SUB, LANES)
    mixing = (-(-(nm // SUB) // (LANES // (nm + 2))) * SUB, LANES)
    whole = pl.BlockSpec(memory_space=VMEM)
    outside = pl.BlockSpec(memory_space=pltpu.HBM)
    swap = [(0, 1), (1, 0)]
    dma = pltpu.SemaphoreType.DMA

    def call(kernel, statics, outs, scratch, *args, specs=None, out_specs=None, name=None):
        def wrapped(*refs):
            return kernel(*statics, *refs)
        return pl.pallas_call(
            wrapped,
            out_shape=[jax.ShapeDtypeStruct(s, F32) for s in outs],
            in_specs=specs or [whole] * len(args),
            out_specs=out_specs or [whole] * len(outs),
            scratch_shapes=scratch,
            compiler_params=pltpu.CompilerParams(vmem_limit_bytes=32 * 2**20),
            name=name,
        )(*args)

    other_state = lax.ppermute(state, "member", swap)
    given = [ray_cols.swapaxes(1, 2), ray_len, ray_weight.transpose(0, 2, 3, 1), owner, loc_regions.swapaxes(1, 2),
             loc_weight.swapaxes(1, 2), obs_value.swapaxes(1, 2), obs_var.swapaxes(1, 2)]
    msg, later, meta = call(
        predict_kernel, (nl, nm, nc, regions, slots, rays),
        [(regions * cores,) + block, block, (STEPS, SUB, LANES)],
        [VMEM(state.shape, F32)] + [VMEM(a.shape, a.dtype) for a in given]
        + [VMEM((nv, STEPS * slots, LANES), F32), VMEM((nv, rays, STEPS * LANES), F32),
           VMEM((nv, rays, STEPS * LANES), F32), VMEM((SUB, LANES), F32),
           VMEM((SUB, LANES), jnp.int32), pltpu.SMEM((SUB, LANES), jnp.int32), dma((nv,)), dma((len(given),)), dma],
        state, *given, specs=[outside] * (1 + len(given)), name="predict",
    )

    def assimilate(step, msg, *more):
        got = lax.all_to_all(msg, ("region", "member"), 0, 0, tiled=True)
        out, local = call(
            local_kernel, (step, nl, nm, regions, slots, levels, level_count, cores),
            [(level_count,) + mixing, (nl,) + mixing], [VMEM((nl, LANES, LANES), F32)],
            got, meta, name="local",
        )
        got = lax.all_to_all(out, "level", 0, 0, tiled=True)
        rows = nl * mixing[0] + sum(a.shape[0] for a in more)
        own, = call(combine_kernel, (nl, levels, level_count), [(rows, LANES)], [], got, local, *more, name="combine")
        return own, lax.ppermute(own, "member", swap)

    own, other = assimilate(0, msg, later)
    mix, msg = call(
        forecast_kernel, (nl, nm, regions, slots),
        [(nl, LANES, LANES), (regions * cores,) + block], [VMEM((nl, LANES, LANES), F32)],
        own, other, name="forecast",
    )
    own, other = assimilate(1, msg)
    out, = call(
        update_kernel, (nl, nm), [state.shape],
        [VMEM(state.shape, F32)] * 3 + [VMEM((nl, nm, 2 * LANES), F32), dma((2 * nv * nl,)), dma((nv * nl,))],
        own, other, mix, state, other_state, specs=[whole] * 3 + [outside] * 2, out_specs=[outside], name="update",
    )
    return out


def solution(mesh):
    in_specs = (P(None, "level", "member", "region"), P(), P(), P(), P(), P(), P(), P(), P())
    out_specs = P(None, "level", "member", "region")
    return jax.shard_map(body, mesh=mesh, in_specs=in_specs, out_specs=out_specs, check_vma=False)
```

time: 98 us -> 84.4 us (0.86); the launches traced: 96.3 us -> 83.9 us
  blocking collectives: 21.2 us -> 52.1 us
  waiting for transfers between devices: 28.6 us -> 1.7 us
  starting transfers between devices: 18 us -> 8.34 us
  Pallas kernels: 20.8 us -> 14 us
    all_to_all x0 -> x2, blocking collectives: none -> 37 us  [assimilate(): got = lax.all_to_all(out, 'level', 0, 0, tiled=True)]
    all_to_all x2 -> x0, waiting for transfers between devices: 24.3 us -> none  [assimilate(): return (lax.all_to_all(out, 'level', 0, 0, tiled=True), local)]
    all_to_all x2 -> x0, starting transfers between devices: 15.5 us -> none  [assimilate(): return (lax.all_to_all(out, 'level', 0, 0, tiled=True), local)]
    pallas_call x1 -> x0, Pallas kernels: 6.03 us -> none  [body(): pl.pallas_call(update, grid=(nl, nv), out_shape=jax.ShapeDtypeStruct(stat...]
    all_to_all x2, blocking collectives: 21.2 us -> 15.2 us  [assimilate(): got = lax.all_to_all(msg, ('region', 'member'), 0, 0, tiled=True)]
    ppermute x2, starting transfers between devices: 1.29 us -> 5.1 us  [assimilate(): return (own, lax.ppermute(own, 'member', swap))]
    ppermute x2, waiting for transfers between devices: 4.26 us -> 1.69 us  [assimilate(): return (own, lax.ppermute(own, 'member', swap))]
    ppermute x1, starting transfers between devices: 1.19 us -> 3.24 us  [body(): other_state = lax.ppermute(state, 'member', swap)]
  transfers between devices with their start and end apart: 5 -> 3, of which waited for: 4 -> 2; matrix products, arithmetic and copies ran while one was open for 0% -> 0% of each run, Pallas kernels for 2% -> 11%
where the time goes in v2:
time: 84.4 us; the launch traced here: 83.9 us
  blocking collectives  52.1 us (62%)
  Pallas kernels  14 us (17%)
  starting transfers between devices  8.34 us (10%)
  local copies, waits for them, and re-layouts  7.71 us (9%)
  waiting for transfers between devices  1.7 us (2%)
    all_to_all x2, blocking collectives, assimilate(): got = lax.all_to_all(out, 'level', 0, 0, tiled=True)  37 us
    all_to_all x2, blocking collectives, assimilate(): got = lax.all_to_all(msg, ('region', 'member'), 0, 0, tiled=True)  15.2 us
    pallas_call x7, Pallas kernels, call(): pl.pallas_call(wrapped, out_shape=[jax.ShapeDtypeStruct(s, F32) for s in...  14 us
    unnamed x20, local copies, waits for them, and re-layouts  7.71 us
    ppermute x2, starting transfers between devices, assimilate(): return (own, lax.ppermute(own, 'member', swap))  5.1 us
    ppermute x1, starting transfers between devices, body(): other_state = lax.ppermute(state, 'member', swap)  3.24 us
    ppermute x2, waiting for transfers between devices, assimilate(): return (own, lax.ppermute(own, 'member', swap))  1.69 us
  transfers between devices with their start and end apart: 3, of which 2 were waited for; matrix products, arithmetic and copies ran while one was open for 0% of the time, Pallas kernels for 11%

profile of v2, /device:TPU:1, one launch (start us, length us, event | category | flops | bytes accessed | tf_op | source)
XLA Modules:
  0.0 83.9 jit_solution(15297637636466643000)
XLA Ops:
  0.0 3.2 %collective-permute-start.2 = (f32[3,2,40,2048]{3,2,1,0:T(8,128)}, f32[3,2,40,2048]{3,2,1,0:T(8,128)S(1)}, u32[]{:S(2)}, u32[]{:S(2)}) collective-permute-start(f32[3,2,40,2048]{3,2,1,0:T(8,128)} %refs_3_.1), channel_id=1, source_target_pairs={{0,1},{1,0},{2,3},{3,2},{4,5},{5,4},{6,7},{7,6},{8,9},{9,8},{10,11... | collective-permute-start | bytes 5898248 | tf_op jit(solution)/shard_map/ppermute | solution.py:388
  3.2 0.0 copy-start
  3.2 1.5 %copy-done = f32[3,2,40,2048]{3,2,1,0:T(8,128)S(1)} copy-done((f32[3,2,40,2048]{3,2,1,0:T(8,128)S(1)}, f32[3,2,40,2048]{3,2,1,0:T(8,128)}, u32[]{:S(2)}) %copy-start) | copy-done | bytes 1966104
  4.8 0.0 copy-start.2
  4.8 0.9 %copy-done.2 = f32[2,128,3,64]{1,3,2,0:T(8,128)S(1)} copy-done((f32[2,128,3,64]{1,3,2,0:T(8,128)S(1)}, f32[2,128,3,64]{1,3,2,0:T(8,128)}, u32[]{:S(2)}) %copy-start.2) | copy-done | bytes 196632
  5.7 0.0 copy-start.3
  5.7 0.8 copy-done.3
  6.6 0.0 copy-start.4
  6.6 0.8 copy-done.4
  7.4 0.0 copy-start.5
  7.4 0.8 copy-done.5
  8.2 0.7 copy-done.6
  8.9 0.7 copy-done.7
  9.6 0.7 copy-done.8
  10.3 0.7 copy-done.9
  11.0 6.7 %predict.1 = (f32[8,24,128]{2,1,0:T(8,128)S(1)}, f32[24,128]{1,0:T(8,128)S(1)}, f32[2,8,128]{2,1,0:T(8,128)S(1)}) custom-call(f32[3,2,40,2048]{3,2,1,0:T(8,128)S(1)} %copy-done, s32[2,64,128]{2,1,0:T(8,128)S(1)} %bitcast.7, s32[2,128]{1,0:T(2,128)S(1)} %copy-done.8, f32[2,3,64,128]{3,2,1,0:T(8,128)S(1)} %bitcast.6, s32[2,128]{1,0:T(2,128)S(1)} %copy-done.9, ...), custom_call_target="tpu_custom_call" | custom-call | tf_op jit(solution)/shard_map/predict/pallas_call | solution.py:378
  17.7 7.5 %all_to_all.20.refs_0_ = f32[8,24,128]{2,1,0:T(8,128)S(1)} all-to-all(f32[8,24,128]{2,1,0:T(8,128)S(1)} %get-tuple-element.14), channel_id=1, replica_groups=mesh['region'=4,'level'=32,'member'=2] {'region','member'}, dimensions={0} | all-to-all | bytes 196608 | tf_op jit(solution)/shard_map/all_to_all | solution.py:402
  25.2 0.7 local.2
  25.9 22.2 %all_to_all.21.refs_0_ = f32[32,16,128]{2,1,0:T(8,128)S(1)} all-to-all(f32[32,16,128]{2,1,0:T(8,128)S(1)} %get-tuple-element.16), channel_id=1, replica_groups=mesh['region'=4,'level'=32,'member'=2] {'level'}, dimensions={0} | all-to-all | bytes 524288 | tf_op jit(solution)/shard_map/all_to_all | solution.py:408
  48.1 0.2 combine.2.refs_0_
  48.3 2.5 %collective-permute-start = (f32[56,128]{1,0:T(8,128)S(1)}, f32[56,128]{1,0:T(8,128)S(1)}, u32[]{:S(2)}, u32[]{:S(2)}) collective-permute-start(f32[56,128]{1,0:T(8,128)S(1)} %combine.2.refs_0_), channel_id=1, source_target_pairs={{0,1},{1,0},{2,3},{3,2},{4,5},{5,4},{6,7},{7,6},{8,9},{9,8},{10,11... | collective-permute-start | bytes 86024 | tf_op jit(solution)/shard_map/ppermute | solution.py:411
  50.8 0.9 %collective-permute-done.refs_1_ = f32[56,128]{1,0:T(8,128)S(1)} collective-permute-done((f32[56,128]{1,0:T(8,128)S(1)}, f32[56,128]{1,0:T(8,128)S(1)}, u32[]{:S(2)}, u32[]{:S(2)}) %collective-permute-start) | collective-permute-done | bytes 28704 | tf_op jit(solution)/shard_map/ppermute | solution.py:411
  51.7 0.8 forecast.1
  52.5 7.7 %all_to_all.22.refs_0_ = f32[8,24,128]{2,1,0:T(8,128)S(1)} all-to-all(f32[8,24,128]{2,1,0:T(8,128)S(1)} %get-tuple-element.19), channel_id=1, replica_groups=mesh['region'=4,'level'=32,'member'=2] {'region','member'}, dimensions={0} | all-to-all | bytes 196608 | tf_op jit(solution)/shard_map/all_to_all | solution.py:402
  60.1 0.7 local.3
  60.9 14.8 %all_to_all.23.refs_0_ = f32[32,16,128]{2,1,0:T(8,128)S(1)} all-to-all(f32[32,16,128]{2,1,0:T(8,128)S(1)} %get-tuple-element.20), channel_id=1, replica_groups=mesh['region'=4,'level'=32,'member'=2] {'level'}, dimensions={0} | all-to-all | bytes 524288 | tf_op jit(solution)/shard_map/all_to_all | solution.py:408
  75.7 0.2 combine.3.refs_0_
  75.9 2.5 %collective-permute-start.1 = (f32[32,128]{1,0:T(8,128)S(1)}, f32[32,128]{1,0:T(8,128)S(1)}, u32[]{:S(2)}, u32[]{:S(2)}) collective-permute-start(f32[32,128]{1,0:T(8,128)S(1)} %combine.3.refs_0_), channel_id=1, source_target_pairs={{0,1},{1,0},{2,3},{3,2},{4,5},{5,4},{6,7},{7,6},{8,9},{9,8},{10,11... | collective-permute-start | bytes 49160 | tf_op jit(solution)/shard_map/ppermute | solution.py:411
  78.4 0.8 collective-permute-done.1.refs_1_
  79.3 0.0 collective-permute-done.2.refs_4_
  79.3 0.0 copy-done.1
  79.3 4.6 %update.1 = f32[3,2,40,2048]{3,2,1,0:T(8,128)} custom-call(f32[32,128]{1,0:T(8,128)S(1)} %combine.3.refs_0_, f32[32,128]{1,0:T(8,128)S(1)} %collective-permute-done.1.refs_1_, f32[2,128,128]{2,1,0:T(8,128)S(1)} %get-tuple-element.22.refs_2_, f32[3,2,40,2048]{3,2,1,0:T(8,128)S(1)} %copy-done.1, f32[3,2,40,2048]{3,2,1,0:T(8,128)S(1)} %collective-permute-done.2.refs_4_), custom_call_target="tpu_custom_call" | custom-call | tf_op jit(solution)/shard_map/update/pallas_call | solution.py:378
  (5 shorter events, 0.0 us)
Async XLA Ops:
  0.0 79.3 %collective-permute-start.2 = (f32[3,2,40,2048]{3,2,1,0:T(8,128)}, f32[3,2,40,2048]{3,2,1,0:T(8,128)S(1)}, u32[]{:S(2)}, u32[]{:S(2)}) collective-permute-start(f32[3,2,40,2048]{3,2,1,0:T(8,128)} %refs_3_.1), channel_id=1, source_target_pairs={{0,1},{1,0},{2,3},{3,2},{4,5},{5,4},{6,7},{7,6},{8,9},{9,8},{10,11... | collective-permute-start | bytes 5898248 | tf_op jit(solution)/shard_map/ppermute | solution.py:388
  3.2 1.5 %copy-start = (f32[3,2,40,2048]{3,2,1,0:T(8,128)S(1)}, f32[3,2,40,2048]{3,2,1,0:T(8,128)}, u32[]{:S(2)}) copy-start(f32[3,2,40,2048]{3,2,1,0:T(8,128)} %refs_3_.1) | copy-start | bytes 5898244
  4.8 0.9 %copy-start.2 = (f32[2,128,3,64]{1,3,2,0:T(8,128)S(1)}, f32[2,128,3,64]{1,3,2,0:T(8,128)}, u32[]{:S(2)}) copy-start(f32[2,128,3,64]{1,3,2,0:T(8,128)} %param.12) | copy-start | bytes 589828
  5.7 0.8 %copy-start.3 = (s32[2,128,64]{1,2,0:T(8,128)S(1)}, s32[2,128,64]{1,2,0:T(8,128)}, u32[]{:S(2)}) copy-start(s32[2,128,64]{1,2,0:T(8,128)} %param.10) | copy-start | bytes 196612
  6.6 0.8 %copy-start.4 = (f32[2,128,64]{1,2,0:T(8,128)S(1)}, f32[2,128,64]{1,2,0:T(8,128)}, u32[]{:S(2)}) copy-start(f32[2,128,64]{1,2,0:T(8,128)} %param.16) | copy-start | bytes 196612
  7.4 0.8 %copy-start.5 = (f32[2,128,64]{1,2,0:T(8,128)S(1)}, f32[2,128,64]{1,2,0:T(8,128)}, u32[]{:S(2)}) copy-start(f32[2,128,64]{1,2,0:T(8,128)} %param.17) | copy-start | bytes 196612
  8.2 0.7 copy-start.6
  8.9 0.7 copy-start.7
  9.6 0.7 copy-start.8
  10.3 0.7 copy-start.9
  11.0 68.3 %copy-start.1 = (f32[3,2,40,2048]{3,2,1,0:T(8,128)S(1)}, f32[3,2,40,2048]{3,2,1,0:T(8,128)}, u32[]{:S(2)}) copy-start(f32[3,2,40,2048]{3,2,1,0:T(8,128)} %refs_3_.1) | copy-start | bytes 5898244
  48.3 3.4 %collective-permute-start = (f32[56,128]{1,0:T(8,128)S(1)}, f32[56,128]{1,0:T(8,128)S(1)}, u32[]{:S(2)}, u32[]{:S(2)}) collective-permute-start(f32[56,128]{1,0:T(8,128)S(1)} %combine.2.refs_0_), channel_id=1, source_target_pairs={{0,1},{1,0},{2,3},{3,2},{4,5},{5,4},{6,7},{7,6},{8,9},{9,8},{10,11... | collective-permute-start | bytes 86024 | tf_op jit(solution)/shard_map/ppermute | solution.py:411
  75.9 3.4 %collective-permute-start.1 = (f32[32,128]{1,0:T(8,128)S(1)}, f32[32,128]{1,0:T(8,128)S(1)}, u32[]{:S(2)}, u32[]{:S(2)}) collective-permute-start(f32[32,128]{1,0:T(8,128)S(1)} %combine.3.refs_0_), channel_id=1, source_target_pairs={{0,1},{1,0},{2,3},{3,2},{4,5},{5,4},{6,7},{7,6},{8,9},{9,8},{10,11... | collective-permute-start | bytes 49160 | tf_op jit(solution)/shard_map/ppermute | solution.py:411

commit v3 on v2

--- a/solution.py
+++ b/solution.py
@@ -317,18 +317,11 @@
     return high, x - high
 
 
-def update_kernel(nl, nm, own_ref, other_ref, mix_ref, state_hbm, theirs_hbm, out_hbm,
-                  mine_v, theirs_v, out_v, left_ref, in_sem, out_sem):
-    nv = state_hbm.shape[0]
+def update_kernel(nl, nm, own_ref, other_ref, mix_ref, state_ref, theirs_ref, out_hbm,
+                  out_v, left_ref, out_sem):
+    nv = state_ref.shape[0]
     members = 2 * nm
     blocks = [(v, l) for l in range(nl) for v in range(nv)]
-    fetches = []
-    for i, (v, l) in enumerate(blocks):
-        pair = (pltpu.make_async_copy(state_hbm.at[v, l], mine_v.at[v, l], in_sem.at[2 * i]),
-                pltpu.make_async_copy(theirs_hbm.at[v, l], theirs_v.at[v, l], in_sem.at[2 * i + 1]))
-        for copy in pair:
-            copy.start()
-        fetches.append(pair)
     rows = own_ref.shape[0] // nl
     lane = iota((nm, LANES), 1)
     for l in range(nl):
@@ -339,13 +332,11 @@
         again = turn(high, members)
         left_ref[l, :, 0:LANES] = high + jnp.where(lane >= members, again, 0.0)
         left_ref[l, :, LANES:] = jnp.where(lane < 2 * members - LANES, again, 0.0) + turn(low, 2 * members - LANES)
-    pad = jnp.zeros((2 * LANES - 3 * members, state_hbm.shape[3]), F32)
+    pad = jnp.zeros((2 * LANES - 3 * members, state_ref.shape[3]), F32)
     stores = []
     for i, (v, l) in enumerate(blocks):
-        for copy in fetches[i]:
-            copy.wait()
-        own = mine_v[v, l]
-        high, low = split(jnp.concatenate([own, theirs_v[v, l]], axis=0))
+        own = state_ref[v, l]
+        high, low = split(jnp.concatenate([own, theirs_ref[v, l]], axis=0))
         right = jnp.concatenate([high, low, high, pad], axis=0).astype(BF16)
         out_v[v, l] = own + jnp.dot(left_ref[l].astype(BF16), right, preferred_element_type=F32)
         copy = pltpu.make_async_copy(out_v.at[v, l], out_hbm.at[v, l], out_sem.at[i])
@@ -372,7 +363,7 @@
     swap = [(0, 1), (1, 0)]
     dma = pltpu.SemaphoreType.DMA
 
-    def call(kernel, statics, outs, scratch, *args, specs=None, out_specs=None, name=None):
+    def call(kernel, statics, outs, scratch, *args, specs=None, out_specs=None, name=None, limit=32):
         def wrapped(*refs):
             return kernel(*statics, *refs)
         return pl.pallas_call(
@@ -381,7 +372,7 @@
             in_specs=specs or [whole] * len(args),
             out_specs=out_specs or [whole] * len(outs),
             scratch_shapes=scratch,
-            compiler_params=pltpu.CompilerParams(vmem_limit_bytes=32 * 2**20),
+            compiler_params=pltpu.CompilerParams(vmem_limit_bytes=limit * 2**20),
             name=name,
         )(*args)
 
@@ -395,7 +386,7 @@
         + [VMEM((nv, STEPS * slots, LANES), F32), VMEM((nv, rays, STEPS * LANES), F32),
            VMEM((nv, rays, STEPS * LANES), F32), VMEM((SUB, LANES), F32),
            VMEM((SUB, LANES), jnp.int32), pltpu.SMEM((SUB, LANES), jnp.int32), dma((nv,)), dma((len(given),)), dma],
-        state, *given, specs=[outside] * (1 + len(given)), name="predict",
+        state, *given, specs=[outside] * (1 + len(given)), name="predict", limit=60,
     )
 
     def assimilate(step, msg, *more):
@@ -419,8 +410,8 @@
     own, other = assimilate(1, msg)
     out, = call(
         update_kernel, (nl, nm), [state.shape],
-        [VMEM(state.shape, F32)] * 3 + [VMEM((nl, nm, 2 * LANES), F32), dma((2 * nv * nl,)), dma((nv * nl,))],
-        own, other, mix, state, other_state, specs=[whole] * 3 + [outside] * 2, out_specs=[outside], name="update",
+        [VMEM(state.shape, F32), VMEM((nl, nm, 2 * LANES), F32), dma((nv * nl,))],
+        own, other, mix, state, other_state, out_specs=[outside], name="update",
     )
     return out
 

time: 84.4 us -> 78.1 us (0.925)
  local copies, waits for them, and re-layouts: 7.71 us -> 2.1 us
  Pallas kernels: 14 us -> 13 us
    unnamed x20 -> x8, local copies, waits for them, and re-layouts: 7.71 us -> 2.1 us
    pallas_call x7, Pallas kernels: 14 us -> 13 us  [call(): pl.pallas_call(wrapped, out_shape=[jax.ShapeDtypeStruct(s, F32) for s in...]
  transfers between devices with their start and end apart: 3 -> 3, of which waited for: 2 -> 2; matrix products, arithmetic and copies ran while one was open for 0% -> 0% of each run, Pallas kernels for 11% -> 13%
where the time goes in v3:
time: 78.1 us; the launch traced here: 77.6 us
  blocking collectives  52.3 us (67%)
  Pallas kernels  13 us (17%)
  starting transfers between devices  8.34 us (11%)
  local copies, waits for them, and re-layouts  2.1 us (3%)
  waiting for transfers between devices  1.7 us (2%)
    all_to_all x2, blocking collectives, assimilate(): got = lax.all_to_all(out, 'level', 0, 0, tiled=True)  36.4 us
    all_to_all x2, blocking collectives, assimilate(): got = lax.all_to_all(msg, ('region', 'member'), 0, 0, tiled=True)  16 us
    pallas_call x7, Pallas kernels, call(): pl.pallas_call(wrapped, out_shape=[jax.ShapeDtypeStruct(s, F32) for s in...  13 us
    ppermute x2, starting transfers between devices, assimilate(): return (own, lax.ppermute(own, 'member', swap))  5.1 us
    ppermute x1, starting transfers between devices, body(): other_state = lax.ppermute(state, 'member', swap)  3.24 us
    unnamed x8, local copies, waits for them, and re-layouts  2.1 us
    ppermute x2, waiting for transfers between devices, assimilate(): return (own, lax.ppermute(own, 'member', swap))  1.69 us
  transfers between devices with their start and end apart: 3, of which 2 were waited for; matrix products, arithmetic and copies ran while one was open for 0% of the time, Pallas kernels for 13%

profile of v3, /device:TPU:1, one launch (start us, length us, event | category | flops | bytes accessed | tf_op | source)
XLA Modules:
  0.0 77.6 jit_solution(8377743792242043666)
XLA Ops:
  0.0 3.2 %collective-permute-start.2 = (f32[3,2,40,2048]{3,2,1,0:T(8,128)}, f32[3,2,40,2048]{3,2,1,0:T(8,128)S(1)}, u32[]{:S(2)}, u32[]{:S(2)}) collective-permute-start(f32[3,2,40,2048]{3,2,1,0:T(8,128)} %refs_3_.1), channel_id=1, source_target_pairs={{0,1},{1,0},{2,3},{3,2},{4,5},{5,4},{6,7},{7,6},{8,9},{9,8},{10,11... | collective-permute-start | bytes 5898248 | tf_op jit(solution)/shard_map/ppermute | solution.py:379
  3.2 0.0 copy-start
  3.2 7.8 %predict.1 = (f32[8,24,128]{2,1,0:T(8,128)}, f32[24,128]{1,0:T(8,128)}, f32[2,8,128]{2,1,0:T(8,128)}) custom-call(f32[3,2,40,2048]{3,2,1,0:T(8,128)} %refs_3_.1, s32[2,64,128]{2,1,0:T(8,128)} %bitcast.7, s32[2,128]{1,0:T(2,128)} %refs_2_.1, f32[2,3,64,128]{3,2,1,0:T(8,128)} %bitcast.6, s32[2,128]{1,0:T(2,128)} %refs_4_.1, s32[2,2,128]{2,1,0:T(2,128)} %bitcast.10, ...), custom_call_target="tpu_custom_call" | custom-call | tf_op jit(solution)/shard_map/predict/pallas_call | solution.py:369
  11.1 8.3 %all_to_all.20.refs_0_ = f32[8,24,128]{2,1,0:T(8,128)S(1)} all-to-all(f32[8,24,128]{2,1,0:T(8,128)} %get-tuple-element.14), channel_id=1, replica_groups=mesh['region'=4,'level'=32,'member'=2] {'region','member'}, dimensions={0} | all-to-all | bytes 196608 | tf_op jit(solution)/shard_map/all_to_all | solution.py:393
  19.3 0.0 copy-start.1
  19.3 0.7 copy-done.1
  20.0 0.7 local.2
  20.8 21.6 %all_to_all.21.refs_0_ = f32[32,16,128]{2,1,0:T(8,128)S(1)} all-to-all(f32[32,16,128]{2,1,0:T(8,128)S(1)} %get-tuple-element.16), channel_id=1, replica_groups=mesh['region'=4,'level'=32,'member'=2] {'level'}, dimensions={0} | all-to-all | bytes 524288 | tf_op jit(solution)/shard_map/all_to_all | solution.py:399
  42.4 0.0 copy-start.3
  42.4 0.7 copy-done.3
  43.1 0.2 combine.2.refs_0_
  43.2 2.5 %collective-permute-start = (f32[56,128]{1,0:T(8,128)S(1)}, f32[56,128]{1,0:T(8,128)S(1)}, u32[]{:S(2)}, u32[]{:S(2)}) collective-permute-start(f32[56,128]{1,0:T(8,128)S(1)} %combine.2.refs_0_), channel_id=1, source_target_pairs={{0,1},{1,0},{2,3},{3,2},{4,5},{5,4},{6,7},{7,6},{8,9},{9,8},{10,11... | collective-permute-start | bytes 86024 | tf_op jit(solution)/shard_map/ppermute | solution.py:402
  45.8 0.9 %collective-permute-done.refs_1_ = f32[56,128]{1,0:T(8,128)S(1)} collective-permute-done((f32[56,128]{1,0:T(8,128)S(1)}, f32[56,128]{1,0:T(8,128)S(1)}, u32[]{:S(2)}, u32[]{:S(2)}) %collective-permute-start) | collective-permute-done | bytes 28704 | tf_op jit(solution)/shard_map/ppermute | solution.py:402
  46.7 0.8 forecast.1
  47.4 7.7 %all_to_all.22.refs_0_ = f32[8,24,128]{2,1,0:T(8,128)S(1)} all-to-all(f32[8,24,128]{2,1,0:T(8,128)S(1)} %get-tuple-element.19), channel_id=1, replica_groups=mesh['region'=4,'level'=32,'member'=2] {'region','member'}, dimensions={0} | all-to-all | bytes 196608 | tf_op jit(solution)/shard_map/all_to_all | solution.py:393
  55.1 0.0 copy-start.2
  55.1 0.7 copy-done.2
  55.8 0.7 local.3
  56.6 14.8 %all_to_all.23.refs_0_ = f32[32,16,128]{2,1,0:T(8,128)S(1)} all-to-all(f32[32,16,128]{2,1,0:T(8,128)S(1)} %get-tuple-element.20), channel_id=1, replica_groups=mesh['region'=4,'level'=32,'member'=2] {'level'}, dimensions={0} | all-to-all | bytes 524288 | tf_op jit(solution)/shard_map/all_to_all | solution.py:399
  71.4 0.2 combine.3.refs_0_
  71.5 2.5 %collective-permute-start.1 = (f32[32,128]{1,0:T(8,128)S(1)}, f32[32,128]{1,0:T(8,128)S(1)}, u32[]{:S(2)}, u32[]{:S(2)}) collective-permute-start(f32[32,128]{1,0:T(8,128)S(1)} %combine.3.refs_0_), channel_id=1, source_target_pairs={{0,1},{1,0},{2,3},{3,2},{4,5},{5,4},{6,7},{7,6},{8,9},{9,8},{10,11... | collective-permute-start | bytes 49160 | tf_op jit(solution)/shard_map/ppermute | solution.py:402
  74.1 0.8 %collective-permute-done.1.refs_1_ = f32[32,128]{1,0:T(8,128)S(1)} collective-permute-done((f32[32,128]{1,0:T(8,128)S(1)}, f32[32,128]{1,0:T(8,128)S(1)}, u32[]{:S(2)}, u32[]{:S(2)}) %collective-permute-start.1) | collective-permute-done | bytes 16416 | tf_op jit(solution)/shard_map/ppermute | solution.py:402
  74.9 0.0 collective-permute-done.2.refs_4_
  74.9 0.0 copy-done
  74.9 2.7 %update.1 = f32[3,2,40,2048]{3,2,1,0:T(8,128)} custom-call(f32[32,128]{1,0:T(8,128)S(1)} %combine.3.refs_0_, f32[32,128]{1,0:T(8,128)S(1)} %collective-permute-done.1.refs_1_, f32[2,128,128]{2,1,0:T(8,128)S(1)} %get-tuple-element.22.refs_2_, f32[3,2,40,2048]{3,2,1,0:T(8,128)S(1)} %copy-done, f32[3,2,40,2048]{3,2,1,0:T(8,128)S(1)} %collective-permute-done.2.refs_4_), custom_call_target="tpu_custom_call" | custom-call | tf_op jit(solution)/shard_map/update/pallas_call | solution.py:369
Async XLA Ops:
  0.0 74.9 %collective-permute-start.2 = (f32[3,2,40,2048]{3,2,1,0:T(8,128)}, f32[3,2,40,2048]{3,2,1,0:T(8,128)S(1)}, u32[]{:S(2)}, u32[]{:S(2)}) collective-permute-start(f32[3,2,40,2048]{3,2,1,0:T(8,128)} %refs_3_.1), channel_id=1, source_target_pairs={{0,1},{1,0},{2,3},{3,2},{4,5},{5,4},{6,7},{7,6},{8,9},{9,8},{10,11... | collective-permute-start | bytes 5898248 | tf_op jit(solution)/shard_map/ppermute | solution.py:379
  3.2 71.7 %copy-start = (f32[3,2,40,2048]{3,2,1,0:T(8,128)S(1)}, f32[3,2,40,2048]{3,2,1,0:T(8,128)}, u32[]{:S(2)}) copy-start(f32[3,2,40,2048]{3,2,1,0:T(8,128)} %refs_3_.1) | copy-start | bytes 5898244
  19.3 0.7 copy-start.1
  42.4 0.7 copy-start.3
  43.2 3.4 %collective-permute-start = (f32[56,128]{1,0:T(8,128)S(1)}, f32[56,128]{1,0:T(8,128)S(1)}, u32[]{:S(2)}, u32[]{:S(2)}) collective-permute-start(f32[56,128]{1,0:T(8,128)S(1)} %combine.2.refs_0_), channel_id=1, source_target_pairs={{0,1},{1,0},{2,3},{3,2},{4,5},{5,4},{6,7},{7,6},{8,9},{9,8},{10,11... | collective-permute-start | bytes 86024 | tf_op jit(solution)/shard_map/ppermute | solution.py:402
  55.1 0.7 copy-start.2
  71.5 3.4 %collective-permute-start.1 = (f32[32,128]{1,0:T(8,128)S(1)}, f32[32,128]{1,0:T(8,128)S(1)}, u32[]{:S(2)}, u32[]{:S(2)}) collective-permute-start(f32[32,128]{1,0:T(8,128)S(1)} %combine.3.refs_0_), channel_id=1, source_target_pairs={{0,1},{1,0},{2,3},{3,2},{4,5},{5,4},{6,7},{7,6},{8,9},{9,8},{10,11... | collective-permute-start | bytes 49160 | tf_op jit(solution)/shard_map/ppermute | solution.py:402

commit v4 on v3

--- a/solution.py
+++ b/solution.py
@@ -45,7 +45,7 @@
                    state_hbm, cols_hbm, len_hbm, weight_hbm, owner_hbm, locr_hbm, locw_hbm, obs_hbm, var_hbm,
                    msg_ref, later_ref, meta_ref,
                    held, cols_ref, len_ref, weight_ref, owner_ref, locr_ref, locw_ref, obs_ref, var_ref,
-                   rows_ref, masked, sorted_ref, meta_in, place_v, place_s, state_sem, arg_sem, place_sem):
+                   masked, sorted_ref, spread_out, meta_in, state_sem, arg_sem):
     nv = state_hbm.shape[0]
     region = lax.axis_index("region")
     level = lax.axis_index("level")
@@ -57,13 +57,15 @@
     copies = [pltpu.make_async_copy(state_hbm.at[v], held.at[v], state_sem.at[v]) for v in range(nv)]
     for copy in copies:
         copy.start()
-    for copy in fetches:
-        copy.wait()
     lane = iota((LANES, LANES), 1)
     sub = iota((LANES, LANES), 0)
     sub8 = iota((SUB, LANES), 0)
     earlier = (sub < lane).astype(BF16)
     region_f = region.astype(F32)
+    masked[nv * rays:] = jnp.zeros((masked.shape[0] - nv * rays, STEPS * LANES), F32)
+    meta_in[...] = jnp.zeros_like(meta_in)
+    for copy in fetches:
+        copy.wait()
     firsts, places, worst = [], [], None
     for step in range(STEPS):
         cols = cols_ref[step].astype(F32)
@@ -80,25 +82,13 @@
         firsts.append(first)
         live = sub[:rays] < len_ref[step:step + 1]
         for v in range(nv):
-            masked[v, :, step * LANES:(step + 1) * LANES] = jnp.where(live, weight_ref[step, v], 0.0)
+            masked[v * rays:(v + 1) * rays, step * LANES:(step + 1) * LANES] = jnp.where(live, weight_ref[step, v], 0.0)
     slot = sub[:STEPS * slots].astype(F32)
     mine = []
     for step in range(STEPS):
         ours = (slot >= float(step * slots)) & (slot < float((step + 1) * slots))
         mine.append(((places[step] == slot + (region_f - float(step)) * float(slots)) & ours).astype(F32))
     mine = jnp.concatenate(mine, axis=1)
-    first = jnp.broadcast_to(jnp.concatenate(firsts, axis=1), (SUB, STEPS * LANES))
-    own_first = jnp.zeros((SUB, STEPS * slots), F32)
-    for _ in range(2):
-        part = first.astype(BF16)
-        own_first = own_first + lax.dot_general(part, mine.astype(BF16), BY_LANES, preferred_element_type=F32)
-        first = first - part.astype(F32)
-    low = own_first.astype(jnp.int32) - region * nc
-    tile = jnp.clip(low // LANES, 0, nc // LANES - 2)
-    place_v[...] = jnp.zeros_like(place_v)
-    place_v[:, 0:STEPS * slots] = jnp.where(sub8[:, :STEPS * slots] == 0, tile, jnp.clip(low - tile * LANES, 0, 2 * LANES - 1))
-    scalars = pltpu.make_async_copy(place_v, place_s, place_sem)
-    scalars.start()
 
     @pl.when(worst > 0.5)
     def _():
@@ -107,15 +97,30 @@
         def one(d, carry):
             hit = column == d.astype(F32)
             for v in range(nv):
-                sorted_ref[v, pl.ds(d, 1)] = jnp.sum(jnp.where(hit, masked[v], 0.0), axis=0, keepdims=True)
+                weights = masked[v * rays:(v + 1) * rays]
+                sorted_ref[pl.ds(v * rays + d, 1)] = jnp.sum(jnp.where(hit, weights, 0.0), axis=0, keepdims=True)
             return carry
         lax.fori_loop(0, rays, one, 0)
-        masked[...] = sorted_ref[...]
-
+        masked[0:nv * rays] = sorted_ref[...]
+
+    first = jnp.broadcast_to(jnp.concatenate(firsts, axis=1), (LANES, STEPS * LANES))
+    low = pick(mine, first).astype(jnp.int32) - region * nc
+    tile, shift = low >> 7, low & (LANES - 1)
+    picked = pick(mine, masked[...])
+    lane_s = lane[:STEPS * slots]
     for v in range(nv):
-        rows_ref[v] = jnp.zeros((STEPS * slots, LANES), F32)
-        rows_ref[v, :, 0:rays] = pick(mine, masked[v])
-    meta_in[...] = jnp.zeros_like(meta_in)
+        at = v * rays
+        row = picked[:, at // LANES * LANES:(at // LANES + 1) * LANES]
+        at = at % LANES
+        row = turn(jnp.where((lane_s >= at) & (lane_s < at + rays), row, 0.0), -at)
+        for bit in range(7):
+            row = jnp.where((shift >> bit) % 2 == 1, turn(row, 1 << bit), row)
+        near, far = jnp.where(lane_s >= shift, row, 0.0), jnp.where(lane_s < shift, row, 0.0)
+        for t in range(nc // LANES):
+            there = jnp.where(tile == t, near, jnp.where(tile == t - 1, far, 0.0))
+            high = there.astype(BF16)
+            spread_out[v, 0:STEPS * slots, t * LANES:(t + 1) * LANES] = high
+            spread_out[v, STEPS * slots:, t * LANES:(t + 1) * LANES] = (there - high.astype(F32)).astype(BF16)
     for step in range(STEPS):
         horiz = (owner_ref[step:step + 1] == region).astype(F32)
         listed = (locr_ref[step] == region).astype(F32)
@@ -126,37 +131,25 @@
         meta_in[2 * nl:2 * nl + 1] = horiz
         order = (places[step] == sub.astype(F32)).astype(F32)
         meta_ref[step] = lax.dot_general(meta_in[...], order, BY_LANES, precision=HIGHEST, preferred_element_type=F32)
-    scalars.wait()
-    for copy in copies:
-        copy.wait()
+    total = None
+    for v in range(nv):
+        copies[v].wait()
+        prior = jnp.concatenate([held[v, l] for l in range(nl)], axis=0)
+        high = prior.astype(BF16)
+        left = jnp.concatenate([high, (prior - high.astype(F32)).astype(BF16)], axis=0)
+        term = lax.dot_general(left, spread_out[v], BY_LANES, preferred_element_type=F32)
+        total = term if total is None else total + term
+    result = total[:nl * nm] + total[nl * nm:]
+    result = result + turn(result, -STEPS * slots)
     groups = nl * nm // SUB
     packed = -(-groups // regions)
-    lane8 = iota((SUB, LANES), 1)
+    lane8 = lane[:SUB]
     for step in range(STEPS):
-        def eight(block, parts, step=step):
-            parts = list(parts)
-            for u in range(SUB):
-                slot = block * SUB + u
-                tile = place_s[0, step * slots + slot]
-                shift = place_s[1, step * slots + slot]
-                start = pl.multiple_of(tile * LANES, LANES)
-                sums = [None] * nl
-                for v in range(nv):
-                    row = jnp.broadcast_to(rows_ref[v, pl.ds(step * slots + slot, 1)], (SUB, LANES))
-                    row = pltpu.roll(row, shift & (LANES - 1), 1)
-                    for half in range(2):
-                        kept = jnp.where((lane8 >= shift) if half == 0 else (lane8 < shift), row, 0.0)
-                        for l in range(nl):
-                            data = held[v, l, :, pl.ds(start + half * LANES, LANES)]
-                            terms = [data[r * SUB:(r + 1) * SUB] * kept for r in range(nm // SUB)]
-                            sums[l] = terms if sums[l] is None else [a + b for a, b in zip(sums[l], terms)]
-                for l in range(nl):
-                    for r in range(nm // SUB):
-                        g = l * (nm // SUB) + r
-                        result = jnp.sum(sums[l][r], axis=1, keepdims=True)
-                        parts[g // regions] = jnp.where(lane8 == slots * (g % regions) + slot, result, parts[g // regions])
-            return tuple(parts)
-        parts = lax.fori_loop(0, slots // SUB, eight, (jnp.zeros((SUB, LANES), F32),) * packed)
+        parts = [jnp.zeros((SUB, LANES), F32) for _ in range(packed)]
+        for g in range(groups):
+            j, k = g // regions, g % regions
+            here = (lane8 >= slots * k) & (lane8 < slots * (k + 1))
+            parts[j] = jnp.where(here, turn(result[g * SUB:(g + 1) * SUB], slots * (k - step)), parts[j])
         for j in range(packed):
             if step == 0:
                 for d in range(msg_ref.shape[0]):
@@ -216,13 +209,22 @@
 
 
 def local_kernel(step, nl, nm, regions, slots, levels, level_count, cores,
-                 got_ref, meta_ref, msg_ref, local_ref, spread_ref):
+                 got_ref, meta_ref, *refs):
     level = lax.axis_index("level")
     member = lax.axis_index("member")
     members = nm * cores
     scale = levels / 4.0
     lane8 = iota((SUB, LANES), 1)
-    mats = []
+    fetches = []
+    if step == 0:
+        later_hbm, msg_ref, local_ref, meta_out, later_ref, spread_ref, sem = refs
+        fetches = [pltpu.make_async_copy(meta_ref, meta_out, sem.at[0]), pltpu.make_async_copy(later_hbm, later_ref, sem.at[1])]
+        meta_ref = meta_out
+    else:
+        msg_ref, local_ref, spread_ref = refs
+    for copy in fetches:
+        copy.start()
+    all_spread = []
     for l in range(nl):
         rows = []
         for c in (member, 1 - member):
@@ -238,6 +240,11 @@
         mean = jnp.sum(predicted, axis=0, keepdims=True) * (1.0 / members)
         spread = predicted - mean
         variance = jnp.sum(spread * spread, axis=0, keepdims=True) * (1.0 / (members - 1.0))
+        all_spread.append((mean, spread, variance))
+    for copy in fetches:
+        copy.wait()
+    mats = []
+    for l, (mean, spread, variance) in enumerate(all_spread):
         obs_var = meta_ref[step, l:l + 1]
         obs_value = meta_ref[step, nl + l:nl + l + 1]
         horiz = meta_ref[step, 2 * nl:2 * nl + 1]
@@ -355,6 +362,7 @@
     slots = occ // regions
     levels = nl * level_count
     assert occ == LANES and regions * slots == LANES and nm % SUB == 0 and cores == 2
+    assert LANES % rays == 0 and 2 * STEPS * slots == LANES
     groups = nl * nm // SUB
     block = (-(-groups // regions) * SUB, LANES)
     mixing = (-(-(nm // SUB) // (LANES // (nm + 2))) * SUB, LANES)
@@ -383,31 +391,36 @@
         predict_kernel, (nl, nm, nc, regions, slots, rays),
         [(regions * cores,) + block, block, (STEPS, SUB, LANES)],
         [VMEM(state.shape, F32)] + [VMEM(a.shape, a.dtype) for a in given]
-        + [VMEM((nv, STEPS * slots, LANES), F32), VMEM((nv, rays, STEPS * LANES), F32),
-           VMEM((nv, rays, STEPS * LANES), F32), VMEM((SUB, LANES), F32),
-           VMEM((SUB, LANES), jnp.int32), pltpu.SMEM((SUB, LANES), jnp.int32), dma((nv,)), dma((len(given),)), dma],
+        + [VMEM((-(-nv * rays // LANES) * LANES, STEPS * LANES), F32), VMEM((nv * rays, STEPS * LANES), F32),
+           VMEM((nv, 2 * STEPS * slots, nc), BF16), VMEM((SUB, LANES), F32), dma((nv,)), dma((len(given),))],
         state, *given, specs=[outside] * (1 + len(given)), name="predict", limit=60,
     )
 
-    def assimilate(step, msg, *more):
+    def assimilate(step, msg, meta, later=None):
         got = lax.all_to_all(msg, ("region", "member"), 0, 0, tiled=True)
-        out, local = call(
-            local_kernel, (step, nl, nm, regions, slots, levels, level_count, cores),
-            [(level_count,) + mixing, (nl,) + mixing], [VMEM((nl, LANES, LANES), F32)],
-            got, meta, name="local",
-        )
+        statics = (step, nl, nm, regions, slots, levels, level_count, cores)
+        outs, scratch = [(level_count,) + mixing, (nl,) + mixing], [VMEM((nl, LANES, LANES), F32)]
+        if later is None:
+            out, local = call(local_kernel, statics, outs, scratch, got, meta, name="local")
+            more = []
+        else:
+            out, local, meta, later = call(
+                local_kernel, statics, outs + [meta.shape, later.shape], scratch + [dma((2,))],
+                got, meta, later, specs=[whole] + [outside] * 2, name="local",
+            )
+            more = [later]
         got = lax.all_to_all(out, "level", 0, 0, tiled=True)
         rows = nl * mixing[0] + sum(a.shape[0] for a in more)
         own, = call(combine_kernel, (nl, levels, level_count), [(rows, LANES)], [], got, local, *more, name="combine")
-        return own, lax.ppermute(own, "member", swap)
-
-    own, other = assimilate(0, msg, later)
+        return own, lax.ppermute(own, "member", swap), meta
+
+    own, other, meta = assimilate(0, msg, meta, later)
     mix, msg = call(
         forecast_kernel, (nl, nm, regions, slots),
         [(nl, LANES, LANES), (regions * cores,) + block], [VMEM((nl, LANES, LANES), F32)],
         own, other, name="forecast",
     )
-    own, other = assimilate(1, msg)
+    own, other, _ = assimilate(1, msg, meta)
     out, = call(
         update_kernel, (nl, nm), [state.shape],
         [VMEM(state.shape, F32), VMEM((nl, nm, 2 * LANES), F32), dma((nv * nl,))],

time: 78.1 us -> 74.7 us (0.956)
  Pallas kernels: 13 us -> 10.4 us
    pallas_call x7, Pallas kernels: 13 us -> 10.4 us  [call(): pl.pallas_call(wrapped, out_shape=[jax.ShapeDtypeStruct(s, F32) for s in...]
    unnamed x8 -> x6, local copies, waits for them, and re-layouts: 2.1 us -> 1.41 us
  transfers between devices with their start and end apart: 3 -> 3, of which waited for: 2 -> 2; matrix products, arithmetic and copies ran while one was open for 0% -> 0% of each run, Pallas kernels for 13% -> 10%
where the time goes in v4:
time: 74.7 us; the launch traced here: 74.2 us
  blocking collectives  52.3 us (70%)
  Pallas kernels  10.4 us (14%)
  starting transfers between devices  8.34 us (11%)
  waiting for transfers between devices  1.7 us (2%)
  local copies, waits for them, and re-layouts  1.41 us (2%)
    all_to_all x2, blocking collectives, assimilate(): got = lax.all_to_all(out, 'level', 0, 0, tiled=True)  36.4 us
    all_to_all x2, blocking collectives, assimilate(): got = lax.all_to_all(msg, ('region', 'member'), 0, 0, tiled=True)  16 us
    pallas_call x7, Pallas kernels, call(): pl.pallas_call(wrapped, out_shape=[jax.ShapeDtypeStruct(s, F32) for s in...  10.4 us
    ppermute x2, starting transfers between devices, assimilate(): return (own, lax.ppermute(own, 'member', swap), meta)  5.1 us
    ppermute x1, starting transfers between devices, body(): other_state = lax.ppermute(state, 'member', swap)  3.24 us
    ppermute x2, waiting for transfers between devices, assimilate(): return (own, lax.ppermute(own, 'member', swap), meta)  1.69 us
  transfers between devices with their start and end apart: 3, of which 2 were waited for; matrix products, arithmetic and copies ran while one was open for 0% of the time, Pallas kernels for 10%

profile of v4, /device:TPU:1, one launch (start us, length us, event | category | flops | bytes accessed | tf_op | source)
XLA Modules:
  0.0 74.2 jit_solution(3791058163338506362)
XLA Ops:
  0.0 3.2 %collective-permute-start.2 = (f32[3,2,40,2048]{3,2,1,0:T(8,128)}, f32[3,2,40,2048]{3,2,1,0:T(8,128)S(1)}, u32[]{:S(2)}, u32[]{:S(2)}) collective-permute-start(f32[3,2,40,2048]{3,2,1,0:T(8,128)} %refs_3_.1), channel_id=1, source_target_pairs={{0,1},{1,0},{2,3},{3,2},{4,5},{5,4},{6,7},{7,6},{8,9},{9,8},{10,11... | collective-permute-start | bytes 5898248 | tf_op jit(solution)/shard_map/ppermute | solution.py:387
  3.2 0.0 copy-start
  3.2 5.1 %predict.1 = (f32[8,24,128]{2,1,0:T(8,128)}, f32[24,128]{1,0:T(8,128)}, f32[2,8,128]{2,1,0:T(8,128)}) custom-call(f32[3,2,40,2048]{3,2,1,0:T(8,128)} %refs_3_.1, s32[2,64,128]{2,1,0:T(8,128)} %bitcast.7, s32[2,128]{1,0:T(2,128)} %refs_2_.1, f32[2,3,64,128]{3,2,1,0:T(8,128)} %bitcast.6, s32[2,128]{1,0:T(2,128)} %refs_4_.1, s32[2,2,128]{2,1,0:T(2,128)} %bitcast.10, ...), custom_call_target="tpu_custom_call" | custom-call | tf_op jit(solution)/shard_map/predict/pallas_call | solution.py:377
  8.3 8.3 %all_to_all.20.refs_0_ = f32[8,24,128]{2,1,0:T(8,128)S(1)} all-to-all(f32[8,24,128]{2,1,0:T(8,128)} %get-tuple-element.16), channel_id=1, replica_groups=mesh['region'=4,'level'=32,'member'=2] {'region','member'}, dimensions={0} | all-to-all | bytes 196608 | tf_op jit(solution)/shard_map/all_to_all | solution.py:400
  16.6 0.0 copy-start.1
  16.6 0.7 copy-done.1
  17.3 0.0 copy-start.2
  17.3 0.7 copy-done.2
  18.0 0.8 %local.2 = (f32[32,16,128]{2,1,0:T(8,128)S(1)}, f32[2,16,128]{2,1,0:T(8,128)S(1)}, f32[2,8,128]{2,1,0:T(8,128)S(1)}, f32[24,128]{1,0:T(8,128)S(1)}) custom-call(f32[8,24,128]{2,1,0:T(8,128)S(1)} %all_to_all.20.refs_0_, f32[2,8,128]{2,1,0:T(8,128)S(1)} %copy-done.2, f32[24,128]{1,0:T(8,128)S(1)} %copy-done.1), custom_call_target="tpu_custom_call" | custom-call | tf_op jit(solution)/shard_map/local/pallas_call | solution.py:377
  18.8 21.6 %all_to_all.21.refs_0_ = f32[32,16,128]{2,1,0:T(8,128)S(1)} all-to-all(f32[32,16,128]{2,1,0:T(8,128)S(1)} %get-tuple-element.19), channel_id=1, replica_groups=mesh['region'=4,'level'=32,'member'=2] {'level'}, dimensions={0} | all-to-all | bytes 524288 | tf_op jit(solution)/shard_map/all_to_all | solution.py:412
  40.4 0.2 combine.2.refs_0_
  40.6 2.5 %collective-permute-start = (f32[56,128]{1,0:T(8,128)S(1)}, f32[56,128]{1,0:T(8,128)S(1)}, u32[]{:S(2)}, u32[]{:S(2)}) collective-permute-start(f32[56,128]{1,0:T(8,128)S(1)} %combine.2.refs_0_), channel_id=1, source_target_pairs={{0,1},{1,0},{2,3},{3,2},{4,5},{5,4},{6,7},{7,6},{8,9},{9,8},{10,11... | collective-permute-start | bytes 86024 | tf_op jit(solution)/shard_map/ppermute | solution.py:415
  43.1 0.9 %collective-permute-done.refs_1_ = f32[56,128]{1,0:T(8,128)S(1)} collective-permute-done((f32[56,128]{1,0:T(8,128)S(1)}, f32[56,128]{1,0:T(8,128)S(1)}, u32[]{:S(2)}, u32[]{:S(2)}) %collective-permute-start) | collective-permute-done | bytes 28704 | tf_op jit(solution)/shard_map/ppermute | solution.py:415
  44.0 0.8 %forecast.1 = (f32[2,128,128]{2,1,0:T(8,128)S(1)}, f32[8,24,128]{2,1,0:T(8,128)S(1)}) custom-call(f32[56,128]{1,0:T(8,128)S(1)} %combine.2.refs_0_, f32[56,128]{1,0:T(8,128)S(1)} %collective-permute-done.refs_1_), custom_call_target="tpu_custom_call" | custom-call | tf_op jit(solution)/shard_map/forecast/pallas_call | solution.py:377
  44.7 7.7 %all_to_all.22.refs_0_ = f32[8,24,128]{2,1,0:T(8,128)S(1)} all-to-all(f32[8,24,128]{2,1,0:T(8,128)S(1)} %get-tuple-element.22), channel_id=1, replica_groups=mesh['region'=4,'level'=32,'member'=2] {'region','member'}, dimensions={0} | all-to-all | bytes 196608 | tf_op jit(solution)/shard_map/all_to_all | solution.py:400
  52.4 0.7 %local.3 = (f32[32,16,128]{2,1,0:T(8,128)S(1)}, f32[2,16,128]{2,1,0:T(8,128)S(1)}) custom-call(f32[8,24,128]{2,1,0:T(8,128)S(1)} %all_to_all.22.refs_0_, f32[2,8,128]{2,1,0:T(8,128)S(1)} %get-tuple-element.23.refs_1_), custom_call_target="tpu_custom_call" | custom-call | tf_op jit(solution)/shard_map/local/pallas_call | solution.py:377
  53.2 14.8 %all_to_all.23.refs_0_ = f32[32,16,128]{2,1,0:T(8,128)S(1)} all-to-all(f32[32,16,128]{2,1,0:T(8,128)S(1)} %get-tuple-element.24), channel_id=1, replica_groups=mesh['region'=4,'level'=32,'member'=2] {'level'}, dimensions={0} | all-to-all | bytes 524288 | tf_op jit(solution)/shard_map/all_to_all | solution.py:412
  68.0 0.2 combine.3.refs_0_
  68.1 2.5 %collective-permute-start.1 = (f32[32,128]{1,0:T(8,128)S(1)}, f32[32,128]{1,0:T(8,128)S(1)}, u32[]{:S(2)}, u32[]{:S(2)}) collective-permute-start(f32[32,128]{1,0:T(8,128)S(1)} %combine.3.refs_0_), channel_id=1, source_target_pairs={{0,1},{1,0},{2,3},{3,2},{4,5},{5,4},{6,7},{7,6},{8,9},{9,8},{10,11... | collective-permute-start | bytes 49160 | tf_op jit(solution)/shard_map/ppermute | solution.py:415
  70.7 0.8 %collective-permute-done.1.refs_1_ = f32[32,128]{1,0:T(8,128)S(1)} collective-permute-done((f32[32,128]{1,0:T(8,128)S(1)}, f32[32,128]{1,0:T(8,128)S(1)}, u32[]{:S(2)}, u32[]{:S(2)}) %collective-permute-start.1) | collective-permute-done | bytes 16416 | tf_op jit(solution)/shard_map/ppermute | solution.py:415
  71.5 0.0 collective-permute-done.2.refs_4_
  71.5 0.0 copy-done
  71.5 2.7 %update.1 = f32[3,2,40,2048]{3,2,1,0:T(8,128)} custom-call(f32[32,128]{1,0:T(8,128)S(1)} %combine.3.refs_0_, f32[32,128]{1,0:T(8,128)S(1)} %collective-permute-done.1.refs_1_, f32[2,128,128]{2,1,0:T(8,128)S(1)} %get-tuple-element.26.refs_2_, f32[3,2,40,2048]{3,2,1,0:T(8,128)S(1)} %copy-done, f32[3,2,40,2048]{3,2,1,0:T(8,128)S(1)} %collective-permute-done.2.refs_4_), custom_call_target="tpu_custom_call" | custom-call | tf_op jit(solution)/shard_map/update/pallas_call | solution.py:377
Async XLA Ops:
  0.0 71.5 %collective-permute-start.2 = (f32[3,2,40,2048]{3,2,1,0:T(8,128)}, f32[3,2,40,2048]{3,2,1,0:T(8,128)S(1)}, u32[]{:S(2)}, u32[]{:S(2)}) collective-permute-start(f32[3,2,40,2048]{3,2,1,0:T(8,128)} %refs_3_.1), channel_id=1, source_target_pairs={{0,1},{1,0},{2,3},{3,2},{4,5},{5,4},{6,7},{7,6},{8,9},{9,8},{10,11... | collective-permute-start | bytes 5898248 | tf_op jit(solution)/shard_map/ppermute | solution.py:387
  3.2 68.3 %copy-start = (f32[3,2,40,2048]{3,2,1,0:T(8,128)S(1)}, f32[3,2,40,2048]{3,2,1,0:T(8,128)}, u32[]{:S(2)}) copy-start(f32[3,2,40,2048]{3,2,1,0:T(8,128)} %refs_3_.1) | copy-start | bytes 5898244
  16.6 0.7 copy-start.1
  17.3 0.7 copy-start.2
  40.6 3.4 %collective-permute-start = (f32[56,128]{1,0:T(8,128)S(1)}, f32[56,128]{1,0:T(8,128)S(1)}, u32[]{:S(2)}, u32[]{:S(2)}) collective-permute-start(f32[56,128]{1,0:T(8,128)S(1)} %combine.2.refs_0_), channel_id=1, source_target_pairs={{0,1},{1,0},{2,3},{3,2},{4,5},{5,4},{6,7},{7,6},{8,9},{9,8},{10,11... | collective-permute-start | bytes 86024 | tf_op jit(solution)/shard_map/ppermute | solution.py:415
  68.1 3.4 %collective-permute-start.1 = (f32[32,128]{1,0:T(8,128)S(1)}, f32[32,128]{1,0:T(8,128)S(1)}, u32[]{:S(2)}, u32[]{:S(2)}) collective-permute-start(f32[32,128]{1,0:T(8,128)S(1)} %combine.3.refs_0_), channel_id=1, source_target_pairs={{0,1},{1,0},{2,3},{3,2},{4,5},{5,4},{6,7},{7,6},{8,9},{9,8},{10,11... | collective-permute-start | bytes 49160 | tf_op jit(solution)/shard_map/ppermute | solution.py:415

commit v5 on v4

--- a/solution.py
+++ b/solution.py
@@ -78,7 +78,9 @@
         at_home = (sub8.astype(F32) == home).astype(F32)
         count = jnp.dot(at_home.astype(BF16), earlier, preferred_element_type=F32)
         rank = jnp.sum(at_home * count, axis=0, keepdims=True)
-        places.append(home * float(slots) + rank)
+        ahead = region_f - home
+        ahead = jnp.where(ahead < 0.0, ahead + float(regions), ahead)
+        places.append(ahead * float(slots) + rank)
         firsts.append(first)
         live = sub[:rays] < len_ref[step:step + 1]
         for v in range(nv):
@@ -87,7 +89,7 @@
     mine = []
     for step in range(STEPS):
         ours = (slot >= float(step * slots)) & (slot < float((step + 1) * slots))
-        mine.append(((places[step] == slot + (region_f - float(step)) * float(slots)) & ours).astype(F32))
+        mine.append(((places[step] == slot - float(step * slots)) & ours).astype(F32))
     mine = jnp.concatenate(mine, axis=1)
 
     @pl.when(worst > 0.5)
@@ -208,41 +210,37 @@
     return turned[nm:nm + 1] - (band + turned[:nm])
 
 
-def local_kernel(step, nl, nm, regions, slots, levels, level_count, cores,
-                 got_ref, meta_ref, *refs):
+def local_kernel(step, nl, nm, regions, slots, levels, level_count, cores, *refs):
+    *got, meta_ref, msg_ref, local_ref, spread_ref = refs
+    region = lax.axis_index("region")
     level = lax.axis_index("level")
     member = lax.axis_index("member")
     members = nm * cores
     scale = levels / 4.0
     lane8 = iota((SUB, LANES), 1)
-    fetches = []
-    if step == 0:
-        later_hbm, msg_ref, local_ref, meta_out, later_ref, spread_ref, sem = refs
-        fetches = [pltpu.make_async_copy(meta_ref, meta_out, sem.at[0]), pltpu.make_async_copy(later_hbm, later_ref, sem.at[1])]
-        meta_ref = meta_out
-    else:
-        msg_ref, local_ref, spread_ref = refs
-    for copy in fetches:
-        copy.start()
+    packed = -(-(nl * nm // SUB) // regions)
     all_spread = []
     for l in range(nl):
         rows = []
-        for c in (member, 1 - member):
+        for half, c in enumerate((member, 1 - member)):
             for r in range(nm // SUB):
                 g = l * (nm // SUB) + r
                 j, k = g // regions, g % regions
                 row = None
-                for p in range(regions):
-                    part = turn(got_ref[p * cores + c, j * SUB:(j + 1) * SUB], slots * (p - k))
-                    row = part if row is None else jnp.where(lane8 >= slots * p, part, row)
+                for s in range(regions):
+                    if len(got) == 1:
+                        source = jnp.where(region >= s, region - s, region - s + regions)
+                        part = got[0][source * cores + c, j * SUB:(j + 1) * SUB]
+                    else:
+                        part = got[s][(half * packed + j) * SUB:(half * packed + j + 1) * SUB]
+                    part = turn(part, slots * (s - k))
+                    row = part if row is None else jnp.where(lane8 >= slots * s, part, row)
                 rows.append(row)
         predicted = jnp.concatenate(rows, axis=0)
         mean = jnp.sum(predicted, axis=0, keepdims=True) * (1.0 / members)
         spread = predicted - mean
         variance = jnp.sum(spread * spread, axis=0, keepdims=True) * (1.0 / (members - 1.0))
         all_spread.append((mean, spread, variance))
-    for copy in fetches:
-        copy.wait()
     mats = []
     for l, (mean, spread, variance) in enumerate(all_spread):
         obs_var = meta_ref[step, l:l + 1]
@@ -286,37 +284,33 @@
 def forecast_kernel(nl, nm, regions, slots, own_ref, other_ref, mix_ref, msg_ref, full_ref):
     lane8 = iota((SUB, LANES), 1)
     lane = iota((nm, LANES), 1)
-    groups = nl * nm // SUB
-    packed = -(-groups // regions)
+    per = nm // SUB
+    packed = -(-nl * per // regions)
     first = own_ref.shape[0] - packed * SUB
     rows = first // nl
-    parts = [jnp.zeros((SUB, LANES), F32) for _ in range(packed)]
+    parts = [jnp.zeros((SUB, LANES), F32) for _ in range(2 * packed)]
+    rest = jnp.zeros((LANES - 2 * nm, LANES), F32)
     for l in range(nl):
         pieces = []
         for ref in (own_ref, other_ref):
-            for r in range(nm // SUB):
-                g = l * (nm // SUB) + r
-                j, k = g // regions, g % regions
+            for r in range(per):
+                j, k = (l * per + r) // regions, (l * per + r) % regions
                 pieces.append(turn(ref[first + j * SUB:first + (j + 1) * SUB], -slots * k))
-        own = jnp.concatenate(pieces[:nm // SUB], axis=0)
-        pieces.append(jnp.zeros((LANES - 2 * nm, LANES), F32))
-        full_ref[l] = jnp.concatenate(pieces, axis=0)
+        prior = jnp.concatenate(pieces + [rest], axis=0)
+        full_ref[l] = prior
         bands = [unpack_mixing(ref[l * rows:(l + 1) * rows], nm) for ref in (own_ref, other_ref)]
-        upper = mixing_rows(bands[0], bands[1], nm)
-        mix_ref[l, 0:nm] = upper
-        result = own + dot(upper, full_ref[l])
-        for r in range(nm // SUB):
-            g = l * (nm // SUB) + r
-            j, k = g // regions, g % regions
-            keep = (lane8 >= slots * k) & (lane8 < slots * (k + 1))
-            parts[j] = jnp.where(keep, turn(result[r * SUB:(r + 1) * SUB], slots * k), parts[j])
         lower = mixing_rows(bands[1], bands[0], nm)
         swapped = jnp.where(lane < nm, turn(lower, -nm), jnp.where(lane < 2 * nm, turn(lower, nm), 0.0))
-        mix_ref[l, nm:2 * nm] = swapped
-        mix_ref[l, 2 * nm:] = jnp.zeros((LANES - 2 * nm, LANES), F32)
-    for d in range(msg_ref.shape[0]):
-        for j in range(packed):
-            msg_ref[d, j * SUB:(j + 1) * SUB] = parts[j]
+        mix_ref[l] = jnp.concatenate([mixing_rows(bands[0], bands[1], nm), swapped, rest], axis=0)
+        result = prior + dot(mix_ref[l], full_ref[l])
+        for half in range(2):
+            for r in range(per):
+                j, k = (l * per + r) // regions, (l * per + r) % regions
+                keep = (lane8 >= slots * k) & (lane8 < slots * (k + 1))
+                at = half * per + r
+                j += half * packed
+                parts[j] = jnp.where(keep, turn(result[at * SUB:(at + 1) * SUB], slots * k), parts[j])
+    msg_ref[...] = jnp.concatenate(parts, axis=0)
 
 
 def split(x):
@@ -371,12 +365,13 @@
     swap = [(0, 1), (1, 0)]
     dma = pltpu.SemaphoreType.DMA
 
-    def call(kernel, statics, outs, scratch, *args, specs=None, out_specs=None, name=None, limit=32):
+    def call(kernel, statics, outs, scratch, *args, specs=None, out_specs=None, name=None, limit=32,
+             kind=jax.ShapeDtypeStruct):
         def wrapped(*refs):
             return kernel(*statics, *refs)
         return pl.pallas_call(
             wrapped,
-            out_shape=[jax.ShapeDtypeStruct(s, F32) for s in outs],
+            out_shape=[kind(s, F32) for s in outs],
             in_specs=specs or [whole] * len(args),
             out_specs=out_specs or [whole] * len(outs),
             scratch_shapes=scratch,
@@ -393,34 +388,28 @@
         [VMEM(state.shape, F32)] + [VMEM(a.shape, a.dtype) for a in given]
         + [VMEM((-(-nv * rays // LANES) * LANES, STEPS * LANES), F32), VMEM((nv * rays, STEPS * LANES), F32),
            VMEM((nv, 2 * STEPS * slots, nc), BF16), VMEM((SUB, LANES), F32), dma((nv,)), dma((len(given),))],
-        state, *given, specs=[outside] * (1 + len(given)), name="predict", limit=60,
+        state, *given, specs=[outside] * (1 + len(given)), name="predict", limit=60, kind=VMEM,
     )
 
-    def assimilate(step, msg, meta, later=None):
-        got = lax.all_to_all(msg, ("region", "member"), 0, 0, tiled=True)
-        statics = (step, nl, nm, regions, slots, levels, level_count, cores)
-        outs, scratch = [(level_count,) + mixing, (nl,) + mixing], [VMEM((nl, LANES, LANES), F32)]
-        if later is None:
-            out, local = call(local_kernel, statics, outs, scratch, got, meta, name="local")
-            more = []
-        else:
-            out, local, meta, later = call(
-                local_kernel, statics, outs + [meta.shape, later.shape], scratch + [dma((2,))],
-                got, meta, later, specs=[whole] + [outside] * 2, name="local",
-            )
-            more = [later]
+    def assimilate(step, got, *more):
+        out, local = call(
+            local_kernel, (step, nl, nm, regions, slots, levels, level_count, cores),
+            [(level_count,) + mixing, (nl,) + mixing], [VMEM((nl, LANES, LANES), F32)],
+            *got, meta, name="local",
+        )
         got = lax.all_to_all(out, "level", 0, 0, tiled=True)
         rows = nl * mixing[0] + sum(a.shape[0] for a in more)
         own, = call(combine_kernel, (nl, levels, level_count), [(rows, LANES)], [], got, local, *more, name="combine")
-        return own, lax.ppermute(own, "member", swap), meta
-
-    own, other, meta = assimilate(0, msg, meta, later)
+        return own, lax.ppermute(own, "member", swap)
+
+    own, other = assimilate(0, [lax.all_to_all(msg, ("region", "member"), 0, 0, tiled=True)], later)
     mix, msg = call(
         forecast_kernel, (nl, nm, regions, slots),
-        [(nl, LANES, LANES), (regions * cores,) + block], [VMEM((nl, LANES, LANES), F32)],
+        [(nl, LANES, LANES), (2 * block[0], LANES)], [VMEM((nl, LANES, LANES), F32)],
         own, other, name="forecast",
     )
-    own, other, _ = assimilate(1, msg, meta)
+    rings = [[(i, (i + s) % regions) for i in range(regions)] for s in range(1, regions)]
+    own, other = assimilate(1, [msg] + [lax.ppermute(msg, "region", ring) for ring in rings])
     out, = call(
         update_kernel, (nl, nm), [state.shape],
         [VMEM(state.shape, F32), VMEM((nl, nm, 2 * LANES), F32), dma((nv * nl,))],

time: 74.7 us -> 71.4 us (0.956)
  blocking collectives: 52.3 us -> 43.7 us
  waiting for transfers between devices: 1.7 us -> 5.89 us
  starting transfers between devices: 8.34 us -> 11.8 us
  local copies, waits for them, and re-layouts: 1.41 us -> 0.01 us
    all_to_all x2 -> x1, blocking collectives: 16 us -> 7.45 us  [body(): lax.all_to_all(msg, ('region', 'member'), 0, 0, tiled=True)]
    ppermute x2 -> x5, waiting for transfers between devices: 1.69 us -> 5.88 us  [the longest x3 4.19 us: body(): lax.ppermute(msg, 'region', ring)]
    ppermute x2 -> x5, starting transfers between devices: 5.1 us -> 8.54 us  [the longest x2 6.39 us: assimilate(): return (own, lax.ppermute(own, 'member', swap))]
    unnamed x6 -> x2, local copies, waits for them, and re-layouts: 1.41 us -> 0.01 us
  transfers between devices with their start and end apart: 3 -> 6, of which waited for: 2 -> 5; matrix products, arithmetic and copies ran while one was open for 0% -> 0% of each run, Pallas kernels for 10% -> 10%
where the time goes in v5:
time: 71.4 us; the launch traced here: 71.2 us
  blocking collectives  43.7 us (61%)
  starting transfers between devices  11.8 us (17%)
  Pallas kernels  9.82 us (14%)
  waiting for transfers between devices  5.89 us (8%)
    all_to_all x2, blocking collectives, assimilate(): got = lax.all_to_all(out, 'level', 0, 0, tiled=True)  36.2 us
    pallas_call x7, Pallas kernels, call(): pl.pallas_call(wrapped, out_shape=[kind(s, F32) for s in outs], in_specs=...  9.82 us
    all_to_all x1, blocking collectives, body(): lax.all_to_all(msg, ('region', 'member'), 0, 0, tiled=True)  7.45 us
    ppermute x2, starting transfers between devices, assimilate(): return (own, lax.ppermute(own, 'member', swap))  6.39 us
    ppermute x3, waiting for transfers between devices, body(): lax.ppermute(msg, 'region', ring)  4.19 us
    ppermute x1, starting transfers between devices, body(): other_state = lax.ppermute(state, 'member', swap)  3.24 us
    ppermute x3, starting transfers between devices, body(): lax.ppermute(msg, 'region', ring)  2.15 us
    ppermute x2, waiting for transfers between devices, assimilate(): return (own, lax.ppermute(own, 'member', swap))  1.69 us
  transfers between devices with their start and end apart: 6, of which 5 were waited for; matrix products, arithmetic and copies ran while one was open for 0% of the time, Pallas kernels for 10%

profile of v5, /device:TPU:1, one launch (start us, length us, event | category | flops | bytes accessed | tf_op | source)
XLA Modules:
  0.0 71.2 jit_solution(5119784477176499233)
XLA Ops:
  0.0 3.2 %collective-permute-start.5 = (f32[3,2,40,2048]{3,2,1,0:T(8,128)}, f32[3,2,40,2048]{3,2,1,0:T(8,128)S(1)}, u32[]{:S(2)}, u32[]{:S(2)}) collective-permute-start(f32[3,2,40,2048]{3,2,1,0:T(8,128)} %refs_3_.1), channel_id=1, source_target_pairs={{0,1},{1,0},{2,3},{3,2},{4,5},{5,4},{6,7},{7,6},{8,9},{9,8},{10,11... | collective-permute-start | bytes 5898248 | tf_op jit(solution)/shard_map/ppermute | solution.py:382
  3.2 0.0 copy-start
  3.2 4.5 %predict.1 = (f32[8,24,128]{2,1,0:T(8,128)S(1)}, f32[24,128]{1,0:T(8,128)S(1)}, f32[2,8,128]{2,1,0:T(8,128)S(1)}) custom-call(f32[3,2,40,2048]{3,2,1,0:T(8,128)} %refs_3_.1, s32[2,64,128]{2,1,0:T(8,128)} %bitcast.7, s32[2,128]{1,0:T(2,128)} %refs_2_.1, f32[2,3,64,128]{3,2,1,0:T(8,128)} %bitcast.6, s32[2,128]{1,0:T(2,128)} %refs_4_.1, s32[2,2,128]{2,1,0:T(2,128)} %bitcast.10, ...), custom_call_target="tpu_custom_call" | custom-call | tf_op jit(solution)/shard_map/predict/pallas_call | solution.py:372
  7.7 7.5 %all_to_all.15.refs_0_ = f32[8,24,128]{2,1,0:T(8,128)S(1)} all-to-all(f32[8,24,128]{2,1,0:T(8,128)S(1)} %get-tuple-element.14), channel_id=1, replica_groups=mesh['region'=4,'level'=32,'member'=2] {'region','member'}, dimensions={0} | all-to-all | bytes 196608 | tf_op jit(solution)/shard_map/all_to_all | solution.py:405
  15.2 0.7 %local.2 = (f32[32,16,128]{2,1,0:T(8,128)S(1)}, f32[2,16,128]{2,1,0:T(8,128)S(1)}) custom-call(f32[8,24,128]{2,1,0:T(8,128)S(1)} %all_to_all.15.refs_0_, f32[2,8,128]{2,1,0:T(8,128)S(1)} %get-tuple-element.15.refs_1_.refs_4_), custom_call_target="tpu_custom_call" | custom-call | tf_op jit(solution)/shard_map/local/pallas_call | solution.py:372
  15.9 22.2 %all_to_all.16.refs_0_ = f32[32,16,128]{2,1,0:T(8,128)S(1)} all-to-all(f32[32,16,128]{2,1,0:T(8,128)S(1)} %get-tuple-element.16), channel_id=1, replica_groups=mesh['region'=4,'level'=32,'member'=2] {'level'}, dimensions={0} | all-to-all | bytes 524288 | tf_op jit(solution)/shard_map/all_to_all | solution.py:400
  38.1 0.2 combine.2.refs_0_
  38.3 2.5 %collective-permute-start = (f32[56,128]{1,0:T(8,128)S(1)}, f32[56,128]{1,0:T(8,128)S(1)}, u32[]{:S(2)}, u32[]{:S(2)}) collective-permute-start(f32[56,128]{1,0:T(8,128)S(1)} %combine.2.refs_0_), channel_id=1, source_target_pairs={{0,1},{1,0},{2,3},{3,2},{4,5},{5,4},{6,7},{7,6},{8,9},{9,8},{10,11... | collective-permute-start | bytes 86024 | tf_op jit(solution)/shard_map/ppermute | solution.py:403
  40.8 0.9 %collective-permute-done.refs_1_ = f32[56,128]{1,0:T(8,128)S(1)} collective-permute-done((f32[56,128]{1,0:T(8,128)S(1)}, f32[56,128]{1,0:T(8,128)S(1)}, u32[]{:S(2)}, u32[]{:S(2)}) %collective-permute-start) | collective-permute-done | bytes 28704 | tf_op jit(solution)/shard_map/ppermute | solution.py:403
  41.7 0.9 %forecast.1 = (f32[2,128,128]{2,1,0:T(8,128)S(1)}, f32[48,128]{1,0:T(8,128)S(1)}) custom-call(f32[56,128]{1,0:T(8,128)S(1)} %combine.2.refs_0_, f32[56,128]{1,0:T(8,128)S(1)} %collective-permute-done.refs_1_), custom_call_target="tpu_custom_call" | custom-call | tf_op jit(solution)/shard_map/forecast/pallas_call | solution.py:372
  42.5 1.0 %collective-permute-start.3 = (f32[48,128]{1,0:T(8,128)S(1)}, f32[48,128]{1,0:T(8,128)S(1)}, u32[]{:S(2)}, u32[]{:S(2)}) collective-permute-start(f32[48,128]{1,0:T(8,128)S(1)} %get-tuple-element.19.refs_0_), channel_id=1, source_target_pairs={{0,192},{64,0},{128,64},{192,128},{1,193},{65,1},{129,65},{193,129... | collective-permute-start | bytes 73736 | tf_op jit(solution)/shard_map/ppermute | solution.py:412
  43.5 1.2 %collective-permute-start.2 = (f32[48,128]{1,0:T(8,128)S(1)}, f32[48,128]{1,0:T(8,128)S(1)}, u32[]{:S(2)}, u32[]{:S(2)}) collective-permute-start(f32[48,128]{1,0:T(8,128)S(1)} %get-tuple-element.19.refs_0_), channel_id=1, source_target_pairs={{0,128},{64,192},{128,0},{192,64},{1,129},{65,193},{129,1},{193,65... | collective-permute-start | bytes 73736 | tf_op jit(solution)/shard_map/ppermute | solution.py:412
  44.7 0.0 collective-permute-start.1
  44.7 0.6 collective-permute-done.3.refs_3_
  45.3 2.4 %collective-permute-done.2.refs_2_ = f32[48,128]{1,0:T(8,128)S(1)} collective-permute-done((f32[48,128]{1,0:T(8,128)S(1)}, f32[48,128]{1,0:T(8,128)S(1)}, u32[]{:S(2)}, u32[]{:S(2)}) %collective-permute-start.2) | collective-permute-done | bytes 24608 | tf_op jit(solution)/shard_map/ppermute | solution.py:412
  47.7 1.2 %collective-permute-done.1.refs_1_ = f32[48,128]{1,0:T(8,128)S(1)} collective-permute-done((f32[48,128]{1,0:T(8,128)S(1)}, f32[48,128]{1,0:T(8,128)S(1)}, u32[]{:S(2)}, u32[]{:S(2)}) %collective-permute-start.1) | collective-permute-done | bytes 24608 | tf_op jit(solution)/shard_map/ppermute | solution.py:412
  48.9 0.7 %local.3 = (f32[32,16,128]{2,1,0:T(8,128)S(1)}, f32[2,16,128]{2,1,0:T(8,128)S(1)}) custom-call(f32[48,128]{1,0:T(8,128)S(1)} %get-tuple-element.19.refs_0_, f32[48,128]{1,0:T(8,128)S(1)} %collective-permute-done.1.refs_1_, f32[48,128]{1,0:T(8,128)S(1)} %collective-permute-done.2.refs_2_, f32[48,128]{1,0:T(8,128)S(1)} %collective-permute-done.3.refs_3_, ...), custom_call_target="tpu_custom_call" | custom-call | tf_op jit(solution)/shard_map/local/pallas_call | solution.py:372
  49.6 14.0 %all_to_all.17.refs_0_ = f32[32,16,128]{2,1,0:T(8,128)S(1)} all-to-all(f32[32,16,128]{2,1,0:T(8,128)S(1)} %get-tuple-element.20), channel_id=1, replica_groups=mesh['region'=4,'level'=32,'member'=2] {'level'}, dimensions={0} | all-to-all | bytes 524288 | tf_op jit(solution)/shard_map/all_to_all | solution.py:400
  63.6 0.2 combine.3.refs_0_
  63.8 3.8 %collective-permute-start.4 = (f32[32,128]{1,0:T(8,128)S(1)}, f32[32,128]{1,0:T(8,128)S(1)}, u32[]{:S(2)}, u32[]{:S(2)}) collective-permute-start(f32[32,128]{1,0:T(8,128)S(1)} %combine.3.refs_0_), channel_id=1, source_target_pairs={{0,1},{1,0},{2,3},{3,2},{4,5},{5,4},{6,7},{7,6},{8,9},{9,8},{10,11... | collective-permute-start | bytes 49160 | tf_op jit(solution)/shard_map/ppermute | solution.py:403
  67.7 0.8 %collective-permute-done.4.refs_1_ = f32[32,128]{1,0:T(8,128)S(1)} collective-permute-done((f32[32,128]{1,0:T(8,128)S(1)}, f32[32,128]{1,0:T(8,128)S(1)}, u32[]{:S(2)}, u32[]{:S(2)}) %collective-permute-start.4) | collective-permute-done | bytes 16416 | tf_op jit(solution)/shard_map/ppermute | solution.py:403
  68.5 0.0 collective-permute-done.5.refs_4_
  68.5 0.0 copy-done
  68.5 2.7 %update.1 = f32[3,2,40,2048]{3,2,1,0:T(8,128)} custom-call(f32[32,128]{1,0:T(8,128)S(1)} %combine.3.refs_0_, f32[32,128]{1,0:T(8,128)S(1)} %collective-permute-done.4.refs_1_, f32[2,128,128]{2,1,0:T(8,128)S(1)} %get-tuple-element.22.refs_2_, f32[3,2,40,2048]{3,2,1,0:T(8,128)S(1)} %copy-done, f32[3,2,40,2048]{3,2,1,0:T(8,128)S(1)} %collective-permute-done.5.refs_4_), custom_call_target="tpu_custom_call" | custom-call | tf_op jit(solution)/shard_map/update/pallas_call | solution.py:372
Async XLA Ops:
  0.0 68.5 %collective-permute-start.5 = (f32[3,2,40,2048]{3,2,1,0:T(8,128)}, f32[3,2,40,2048]{3,2,1,0:T(8,128)S(1)}, u32[]{:S(2)}, u32[]{:S(2)}) collective-permute-start(f32[3,2,40,2048]{3,2,1,0:T(8,128)} %refs_3_.1), channel_id=1, source_target_pairs={{0,1},{1,0},{2,3},{3,2},{4,5},{5,4},{6,7},{7,6},{8,9},{9,8},{10,11... | collective-permute-start | bytes 5898248 | tf_op jit(solution)/shard_map/ppermute | solution.py:382
  3.2 65.3 %copy-start = (f32[3,2,40,2048]{3,2,1,0:T(8,128)S(1)}, f32[3,2,40,2048]{3,2,1,0:T(8,128)}, u32[]{:S(2)}) copy-start(f32[3,2,40,2048]{3,2,1,0:T(8,128)} %refs_3_.1) | copy-start | bytes 5898244
  38.3 3.4 %collective-permute-start = (f32[56,128]{1,0:T(8,128)S(1)}, f32[56,128]{1,0:T(8,128)S(1)}, u32[]{:S(2)}, u32[]{:S(2)}) collective-permute-start(f32[56,128]{1,0:T(8,128)S(1)} %combine.2.refs_0_), channel_id=1, source_target_pairs={{0,1},{1,0},{2,3},{3,2},{4,5},{5,4},{6,7},{7,6},{8,9},{9,8},{10,11... | collective-permute-start | bytes 86024 | tf_op jit(solution)/shard_map/ppermute | solution.py:403
  42.5 2.8 %collective-permute-start.3 = (f32[48,128]{1,0:T(8,128)S(1)}, f32[48,128]{1,0:T(8,128)S(1)}, u32[]{:S(2)}, u32[]{:S(2)}) collective-permute-start(f32[48,128]{1,0:T(8,128)S(1)} %get-tuple-element.19.refs_0_), channel_id=1, source_target_pairs={{0,192},{64,0},{128,64},{192,128},{1,193},{65,1},{129,65},{193,129... | collective-permute-start | bytes 73736 | tf_op jit(solution)/shard_map/ppermute | solution.py:412
  43.5 4.2 %collective-permute-start.2 = (f32[48,128]{1,0:T(8,128)S(1)}, f32[48,128]{1,0:T(8,128)S(1)}, u32[]{:S(2)}, u32[]{:S(2)}) collective-permute-start(f32[48,128]{1,0:T(8,128)S(1)} %get-tuple-element.19.refs_0_), channel_id=1, source_target_pairs={{0,128},{64,192},{128,0},{192,64},{1,129},{65,193},{129,1},{193,65... | collective-permute-start | bytes 73736 | tf_op jit(solution)/shard_map/ppermute | solution.py:412
  44.7 4.2 %collective-permute-start.1 = (f32[48,128]{1,0:T(8,128)S(1)}, f32[48,128]{1,0:T(8,128)S(1)}, u32[]{:S(2)}, u32[]{:S(2)}) collective-permute-start(f32[48,128]{1,0:T(8,128)S(1)} %get-tuple-element.19.refs_0_), channel_id=1, source_target_pairs={{0,64},{64,128},{128,192},{192,0},{1,65},{65,129},{129,193},{193,1... | collective-permute-start | bytes 73736 | tf_op jit(solution)/shard_map/ppermute | solution.py:412
  63.8 4.7 %collective-permute-start.4 = (f32[32,128]{1,0:T(8,128)S(1)}, f32[32,128]{1,0:T(8,128)S(1)}, u32[]{:S(2)}, u32[]{:S(2)}) collective-permute-start(f32[32,128]{1,0:T(8,128)S(1)} %combine.3.refs_0_), channel_id=1, source_target_pairs={{0,1},{1,0},{2,3},{3,2},{4,5},{5,4},{6,7},{7,6},{8,9},{9,8},{10,11... | collective-permute-start | bytes 49160 | tf_op jit(solution)/shard_map/ppermute | solution.py:403

commit v6 on v5

--- a/solution.py
+++ b/solution.py
@@ -43,8 +43,8 @@
 
 def predict_kernel(nl, nm, nc, regions, slots, rays,
                    state_hbm, cols_hbm, len_hbm, weight_hbm, owner_hbm, locr_hbm, locw_hbm, obs_hbm, var_hbm,
-                   msg_ref, later_ref, meta_ref,
-                   held, cols_ref, len_ref, weight_ref, owner_ref, locr_ref, locw_ref, obs_ref, var_ref,
+                   msg_ref, later_ref, meta_ref, held,
+                   cols_ref, len_ref, weight_ref, owner_ref, locr_ref, locw_ref, obs_ref, var_ref,
                    masked, sorted_ref, spread_out, meta_in, state_sem, arg_sem):
     nv = state_hbm.shape[0]
     region = lax.axis_index("region")
@@ -210,6 +210,48 @@
     return turned[nm:nm + 1] - (band + turned[:nm])
 
 
+def pack_rows(x):
+    nm = x.shape[0] - SUB
+    width = nm + nm // 2 + 1
+    lane8 = iota((SUB, LANES), 1)
+    sub8 = iota((SUB, LANES), 0)
+    w = x[nm:nm + 1]
+    pieces = []
+    for g in range(nm // SUB):
+        part = x[g * SUB:(g + 1) * SUB]
+        part = jnp.where(lane8 < nm, part, jnp.where(lane8 < width, skew(part, -g * SUB, -1), 0.0))
+        if g % 2:
+            pieces[-1] = pieces[-1] + turn(part, width)
+        else:
+            pieces.append(part)
+    others = (sub8 == 0) & (lane8 >= 64) & (lane8 < 64 + nm)
+    owns = (sub8 == 1) & (lane8 >= 64) & (lane8 < 64 + nm)
+    pieces[-1] = pieces[-1] + jnp.where(others, turn(w, 64), 0.0) + jnp.where(owns, turn(w, 64 - nm), 0.0)
+    return jnp.concatenate(pieces, axis=0)
+
+
+def unpack_rows(p, nm):
+    width = nm + nm // 2 + 1
+    lane8 = iota((SUB, LANES), 1)
+    lane = iota((nm, LANES), 1)
+    sub = iota((nm, LANES), 0)
+    others, band = [], []
+    for g in range(nm // SUB):
+        part = turn(p[g // 2 * SUB:(g // 2 + 1) * SUB], -width * (g % 2))
+        others.append(jnp.where(lane8 < nm, part, 0.0))
+        band.append(skew(jnp.where((lane8 >= nm) & (lane8 < width), part, 0.0), g * SUB - nm, 1))
+    others, band = jnp.concatenate(others, axis=0), jnp.concatenate(band, axis=0)
+    band = jnp.where(lane < nm, band, 0.0) + turn(jnp.where(lane >= nm, band, 0.0), -nm)
+    apart = lane - sub
+    apart = jnp.where(apart < 0, apart + nm, apart)
+    once = jnp.where((lane < nm) & (apart >= 1) & (apart < nm // 2), band, 0.0)
+    turned = jnp.concatenate([once, jnp.zeros((LANES - nm, LANES), F32)], axis=0).T[:nm]
+    last = p[-SUB:]
+    w = jnp.where(lane8[:1] < nm, turn(last[1:2], -64), 0.0)
+    w = w + turn(jnp.where(lane8[:1] < nm, turn(last[0:1], -64), 0.0), nm)
+    return w - (jnp.where(lane < nm, band, 0.0) + turned + turn(others, nm))
+
+
 def local_kernel(step, nl, nm, regions, slots, levels, level_count, cores, *refs):
     *got, meta_ref, msg_ref, local_ref, spread_ref = refs
     region = lax.axis_index("region")
@@ -250,12 +292,18 @@
         gain = (obs_value - mean) / total_var
         shrink = 1.0 / (1.0 + jnp.sqrt(obs_var / total_var))
         scaled = horiz * (1.0 / (members - 1.0))
-        spread_ref[l, 0:members] = spread
-        spread_ref[l, members:] = jnp.zeros((LANES - members, LANES), F32)
         own = spread[:nm]
         left = scaled * (shrink / total_var) * own
-        s = lax.dot_general(left, spread_ref[l], BY_LANES, precision=HIGHEST, preferred_element_type=F32)
-        mats.append(pack_mixing(s, jnp.sum(scaled * gain * own, axis=1, keepdims=True)))
+        if step + 1 < STEPS:
+            spread_ref[l] = jnp.concatenate([spread, jnp.zeros((LANES - members, LANES), F32)], axis=0)
+        else:
+            spread_ref[l] = jnp.concatenate([spread[nm:], own, own, jnp.zeros((LANES - 3 * nm, LANES), F32)], axis=0)
+            left = jnp.concatenate([left, jnp.broadcast_to(scaled * gain, (SUB, LANES))], axis=0)
+        product = lax.dot_general(left, spread_ref[l], BY_LANES, precision=HIGHEST, preferred_element_type=F32)
+        if step + 1 < STEPS:
+            mats.append(pack_mixing(product, jnp.sum(scaled * gain * own, axis=1, keepdims=True)))
+        else:
+            mats.append(pack_rows(product))
     up = sum(math.exp(-(nl - 1 - l) / scale) * mats[l] for l in range(nl))
     down = sum(math.exp(-l / scale) * mats[l] for l in range(nl))
     for l in range(nl):
@@ -264,21 +312,20 @@
         msg_ref[d] = jnp.where(d > level, up, down)
 
 
-def combine_kernel(nl, levels, level_count, got_ref, local_ref, *refs):
-    out_ref = refs[-1]
+def combine(nl, levels, level_count, got_ref, local_ref):
     level = lax.axis_index("level")
     scale = levels / 4.0
     fade = math.exp(-nl / scale)
-    rows = got_ref.shape[1]
     zero = jnp.zeros(got_ref.shape[1:], F32)
     below = lax.fori_loop(0, level, lambda d, acc: acc * fade + got_ref[d], zero)
     above = lax.fori_loop(0, level_count - 1 - level, lambda d, acc: acc * fade + got_ref[level_count - 1 - d], zero)
-    for l in range(nl):
-        out_ref[l * rows:(l + 1) * rows] = (
-            math.exp(-(l + 1) / scale) * below + math.exp(-(nl - l) / scale) * above + local_ref[l]
-        )
-    if len(refs) > 1:
-        out_ref[nl * rows:] = refs[0][...]
+    return [
+        math.exp(-(l + 1) / scale) * below + math.exp(-(nl - l) / scale) * above + local_ref[l] for l in range(nl)
+    ]
+
+
+def combine_kernel(nl, levels, level_count, got_ref, local_ref, later_ref, out_ref):
+    out_ref[...] = jnp.concatenate(combine(nl, levels, level_count, got_ref, local_ref) + [later_ref[...]], axis=0)
 
 
 def forecast_kernel(nl, nm, regions, slots, own_ref, other_ref, mix_ref, msg_ref, full_ref):
@@ -318,16 +365,14 @@
     return high, x - high
 
 
-def update_kernel(nl, nm, own_ref, other_ref, mix_ref, state_ref, theirs_ref, out_hbm,
+def update_kernel(nl, nm, levels, level_count, got_ref, local_ref, mix_ref, state_ref, theirs_ref, out_hbm,
                   out_v, left_ref, out_sem):
     nv = state_ref.shape[0]
     members = 2 * nm
     blocks = [(v, l) for l in range(nl) for v in range(nv)]
-    rows = own_ref.shape[0] // nl
     lane = iota((nm, LANES), 1)
-    for l in range(nl):
-        bands = [unpack_mixing(ref[l * rows:(l + 1) * rows], nm) for ref in (own_ref, other_ref)]
-        second = mixing_rows(bands[0], bands[1], nm)
+    for l, packed in enumerate(combine(nl, levels, level_count, got_ref, local_ref)):
+        second = unpack_rows(packed, nm)
         both = second + mix_ref[l, 0:nm] + dot(second, mix_ref[l])
         high, low = split(both)
         again = turn(high, members)
@@ -359,7 +404,6 @@
     assert LANES % rays == 0 and 2 * STEPS * slots == LANES
     groups = nl * nm // SUB
     block = (-(-groups // regions) * SUB, LANES)
-    mixing = (-(-(nm // SUB) // (LANES // (nm + 2))) * SUB, LANES)
     whole = pl.BlockSpec(memory_space=VMEM)
     outside = pl.BlockSpec(memory_space=pltpu.HBM)
     swap = [(0, 1), (1, 0)]
@@ -382,38 +426,39 @@
     other_state = lax.ppermute(state, "member", swap)
     given = [ray_cols.swapaxes(1, 2), ray_len, ray_weight.transpose(0, 2, 3, 1), owner, loc_regions.swapaxes(1, 2),
              loc_weight.swapaxes(1, 2), obs_value.swapaxes(1, 2), obs_var.swapaxes(1, 2)]
-    msg, later, meta = call(
+    msg, later, meta, held = call(
         predict_kernel, (nl, nm, nc, regions, slots, rays),
-        [(regions * cores,) + block, block, (STEPS, SUB, LANES)],
-        [VMEM(state.shape, F32)] + [VMEM(a.shape, a.dtype) for a in given]
+        [(regions * cores,) + block, block, (STEPS, SUB, LANES), state.shape],
+        [VMEM(a.shape, a.dtype) for a in given]
         + [VMEM((-(-nv * rays // LANES) * LANES, STEPS * LANES), F32), VMEM((nv * rays, STEPS * LANES), F32),
            VMEM((nv, 2 * STEPS * slots, nc), BF16), VMEM((SUB, LANES), F32), dma((nv,)), dma((len(given),))],
-        state, *given, specs=[outside] * (1 + len(given)), name="predict", limit=60, kind=VMEM,
+        state, *given, specs=[outside] * (1 + len(given)), name="predict", limit=56, kind=VMEM,
     )
 
-    def assimilate(step, got, *more):
+    def assimilate(step, got, rows):
         out, local = call(
             local_kernel, (step, nl, nm, regions, slots, levels, level_count, cores),
-            [(level_count,) + mixing, (nl,) + mixing], [VMEM((nl, LANES, LANES), F32)],
+            [(level_count, rows, LANES), (nl, rows, LANES)], [VMEM((nl, LANES, LANES), F32)],
             *got, meta, name="local",
         )
-        got = lax.all_to_all(out, "level", 0, 0, tiled=True)
-        rows = nl * mixing[0] + sum(a.shape[0] for a in more)
-        own, = call(combine_kernel, (nl, levels, level_count), [(rows, LANES)], [], got, local, *more, name="combine")
-        return own, lax.ppermute(own, "member", swap)
-
-    own, other = assimilate(0, [lax.all_to_all(msg, ("region", "member"), 0, 0, tiled=True)], later)
+        return lax.all_to_all(out, "level", 0, 0, tiled=True), local
+
+    band = -(-(nm // SUB) // (LANES // (nm + 2))) * SUB
+    got = assimilate(0, [lax.all_to_all(msg, ("region", "member"), 0, 0, tiled=True)], band)
+    own, = call(
+        combine_kernel, (nl, levels, level_count), [(nl * band + block[0], LANES)], [], *got, later, name="combine",
+    )
     mix, msg = call(
         forecast_kernel, (nl, nm, regions, slots),
         [(nl, LANES, LANES), (2 * block[0], LANES)], [VMEM((nl, LANES, LANES), F32)],
-        own, other, name="forecast",
+        own, lax.ppermute(own, "member", swap), name="forecast",
     )
     rings = [[(i, (i + s) % regions) for i in range(regions)] for s in range(1, regions)]
-    own, other = assimilate(1, [msg] + [lax.ppermute(msg, "region", ring) for ring in rings])
+    got = assimilate(1, [msg] + [lax.ppermute(msg, "region", ring) for ring in rings], -(-(nm // SUB) // 2) * SUB)
     out, = call(
-        update_kernel, (nl, nm), [state.shape],
+        update_kernel, (nl, nm, levels, level_count), [state.shape],
         [VMEM(state.shape, F32), VMEM((nl, nm, 2 * LANES), F32), dma((nv * nl,))],
-        own, other, mix, state, other_state, out_specs=[outside], name="update",
+        *got, mix, held, other_state, out_specs=[outside], name="update",
     )
     return out
 

time: 71.4 us -> 70.4 us (0.986)
  the two profiles are of different devices: /device:TPU:1 before, /device:TPU:32 now
where the time goes in v6:
time: 70.4 us; the launch traced here: 70.2 us
  blocking collectives  51.2 us (73%)
  Pallas kernels  9.87 us (14%)
  waiting for transfers between devices  6.22 us (9%)
  starting transfers between devices  2.81 us (4%)
    all_to_all x2, blocking collectives, assimilate(): return (lax.all_to_all(out, 'level', 0, 0, tiled=True), local)  41.2 us
    all_to_all x1, blocking collectives, body(): lax.all_to_all(msg, ('region', 'member'), 0, 0, tiled=True)  10 us
    pallas_call x6, Pallas kernels, call(): pl.pallas_call(wrapped, out_shape=[kind(s, F32) for s in outs], in_specs=...  9.87 us
    ppermute x3, waiting for transfers between devices, body(): lax.ppermute(msg, 'region', ring)  5.03 us
    ppermute x3, starting transfers between devices, body(): lax.ppermute(msg, 'region', ring)  2.71 us
  transfers between devices with their start and end apart: 5, of which 4 were waited for; matrix products, arithmetic and copies ran while one was open for 0% of the time, Pallas kernels for 10%

profile of v6, /device:TPU:32, one launch (start us, length us, event | category | flops | bytes accessed | tf_op | source)
XLA Modules:
  0.0 70.2 jit_solution(18086505197758889963)
XLA Ops:
  0.0 0.0 collective-permute-start.4
  0.0 4.4 %predict.1 = (f32[8,24,128]{2,1,0:T(8,128)S(1)}, f32[24,128]{1,0:T(8,128)S(1)}, f32[2,8,128]{2,1,0:T(8,128)S(1)}, f32[3,2,40,2048]{3,2,1,0:T(8,128)S(1)}) custom-call(f32[3,2,40,2048]{3,2,1,0:T(8,128)} %refs_0_.1, s32[2,64,128]{2,1,0:T(8,128)} %bitcast.7, s32[2,128]{1,0:T(2,128)} %refs_2_.1, f32[2,3,64,128]{3,2,1,0:T(8,128)} %bitcast.6, s32[2,128]{1,0:T(2,128)} %refs_4_.1, ...), custom_call_target="tpu_custom_call" | custom-call | tf_op jit(solution)/shard_map/predict/pallas_call | solution.py:416
  4.4 10.0 %all_to_all.15.refs_0_ = f32[8,24,128]{2,1,0:T(8,128)S(1)} all-to-all(f32[8,24,128]{2,1,0:T(8,128)S(1)} %get-tuple-element.15), channel_id=1, replica_groups=mesh['region'=4,'level'=32,'member'=2] {'region','member'}, dimensions={0} | all-to-all | bytes 196608 | tf_op jit(solution)/shard_map/all_to_all | solution.py:447
  14.4 0.7 %local.2 = (f32[32,16,128]{2,1,0:T(8,128)S(1)}, f32[2,16,128]{2,1,0:T(8,128)S(1)}) custom-call(f32[8,24,128]{2,1,0:T(8,128)S(1)} %all_to_all.15.refs_0_, f32[2,8,128]{2,1,0:T(8,128)S(1)} %get-tuple-element.16.refs_1_.refs_4_), custom_call_target="tpu_custom_call" | custom-call | tf_op jit(solution)/shard_map/local/pallas_call | solution.py:416
  15.1 23.1 %all_to_all.16.refs_0_ = f32[32,16,128]{2,1,0:T(8,128)S(1)} all-to-all(f32[32,16,128]{2,1,0:T(8,128)S(1)} %get-tuple-element.17), channel_id=1, replica_groups=mesh['region'=4,'level'=32,'member'=2] {'level'}, dimensions={0} | all-to-all | bytes 524288 | tf_op jit(solution)/shard_map/all_to_all | solution.py:444
  38.3 0.2 combine.1.refs_0_
  38.4 0.1 collective-permute-start
  38.5 1.2 %collective-permute-done.refs_1_ = f32[56,128]{1,0:T(8,128)S(1)} collective-permute-done((f32[56,128]{1,0:T(8,128)S(1)}, f32[56,128]{1,0:T(8,128)S(1)}, u32[]{:S(2)}, u32[]{:S(2)}) %collective-permute-start) | collective-permute-done | bytes 28704 | tf_op jit(solution)/shard_map/ppermute | solution.py:454
  39.7 0.9 %forecast.1 = (f32[2,128,128]{2,1,0:T(8,128)S(1)}, f32[48,128]{1,0:T(8,128)S(1)}) custom-call(f32[56,128]{1,0:T(8,128)S(1)} %combine.1.refs_0_, f32[56,128]{1,0:T(8,128)S(1)} %collective-permute-done.refs_1_), custom_call_target="tpu_custom_call" | custom-call | tf_op jit(solution)/shard_map/forecast/pallas_call | solution.py:416
  40.6 1.2 %collective-permute-start.3 = (f32[48,128]{1,0:T(8,128)S(1)}, f32[48,128]{1,0:T(8,128)S(1)}, u32[]{:S(2)}, u32[]{:S(2)}) collective-permute-start(f32[48,128]{1,0:T(8,128)S(1)} %get-tuple-element.20.refs_0_), channel_id=1, source_target_pairs={{0,192},{64,0},{128,64},{192,128},{1,193},{65,1},{129,65},{193,129... | collective-permute-start | bytes 73736 | tf_op jit(solution)/shard_map/ppermute | solution.py:457
  41.8 1.5 %collective-permute-start.2 = (f32[48,128]{1,0:T(8,128)S(1)}, f32[48,128]{1,0:T(8,128)S(1)}, u32[]{:S(2)}, u32[]{:S(2)}) collective-permute-start(f32[48,128]{1,0:T(8,128)S(1)} %get-tuple-element.20.refs_0_), channel_id=1, source_target_pairs={{0,128},{64,192},{128,0},{192,64},{1,129},{65,193},{129,1},{193,65... | collective-permute-start | bytes 73736 | tf_op jit(solution)/shard_map/ppermute | solution.py:457
  43.3 0.0 collective-permute-start.1
  43.3 1.2 %collective-permute-done.3.refs_3_ = f32[48,128]{1,0:T(8,128)S(1)} collective-permute-done((f32[48,128]{1,0:T(8,128)S(1)}, f32[48,128]{1,0:T(8,128)S(1)}, u32[]{:S(2)}, u32[]{:S(2)}) %collective-permute-start.3) | collective-permute-done | bytes 24608 | tf_op jit(solution)/shard_map/ppermute | solution.py:457
  44.5 2.8 %collective-permute-done.2.refs_2_ = f32[48,128]{1,0:T(8,128)S(1)} collective-permute-done((f32[48,128]{1,0:T(8,128)S(1)}, f32[48,128]{1,0:T(8,128)S(1)}, u32[]{:S(2)}, u32[]{:S(2)}) %collective-permute-start.2) | collective-permute-done | bytes 24608 | tf_op jit(solution)/shard_map/ppermute | solution.py:457
  47.3 1.0 %collective-permute-done.1.refs_1_ = f32[48,128]{1,0:T(8,128)S(1)} collective-permute-done((f32[48,128]{1,0:T(8,128)S(1)}, f32[48,128]{1,0:T(8,128)S(1)}, u32[]{:S(2)}, u32[]{:S(2)}) %collective-permute-start.1) | collective-permute-done | bytes 24608 | tf_op jit(solution)/shard_map/ppermute | solution.py:457
  48.3 0.8 %local.3 = (f32[32,24,128]{2,1,0:T(8,128)S(1)}, f32[2,24,128]{2,1,0:T(8,128)S(1)}) custom-call(f32[48,128]{1,0:T(8,128)S(1)} %get-tuple-element.20.refs_0_, f32[48,128]{1,0:T(8,128)S(1)} %collective-permute-done.1.refs_1_, f32[48,128]{1,0:T(8,128)S(1)} %collective-permute-done.2.refs_2_, f32[48,128]{1,0:T(8,128)S(1)} %collective-permute-done.3.refs_3_, ...), custom_call_target="tpu_custom_call" | custom-call | tf_op jit(solution)/shard_map/local/pallas_call | solution.py:416
  49.2 18.1 %all_to_all.17.refs_0_ = f32[32,24,128]{2,1,0:T(8,128)S(1)} all-to-all(f32[32,24,128]{2,1,0:T(8,128)S(1)} %get-tuple-element.21), channel_id=1, replica_groups=mesh['region'=4,'level'=32,'member'=2] {'level'}, dimensions={0} | all-to-all | bytes 786432 | tf_op jit(solution)/shard_map/all_to_all | solution.py:444
  67.3 0.0 collective-permute-done.4.refs_4_
  67.3 2.9 %update.1 = f32[3,2,40,2048]{3,2,1,0:T(8,128)} custom-call(f32[32,24,128]{2,1,0:T(8,128)S(1)} %all_to_all.17.refs_0_, f32[2,24,128]{2,1,0:T(8,128)S(1)} %get-tuple-element.22.refs_1_, f32[2,128,128]{2,1,0:T(8,128)S(1)} %get-tuple-element.23.refs_2_, f32[3,2,40,2048]{3,2,1,0:T(8,128)S(1)} %get-tuple-element.24.refs_3_, ...), custom_call_target="tpu_custom_call" | custom-call | tf_op jit(solution)/shard_map/update/pallas_call | solution.py:416
Async XLA Ops:
  0.0 67.3 %collective-permute-start.4 = (f32[3,2,40,2048]{3,2,1,0:T(8,128)}, f32[3,2,40,2048]{3,2,1,0:T(8,128)S(1)}, u32[]{:S(2)}, u32[]{:S(2)}) collective-permute-start(f32[3,2,40,2048]{3,2,1,0:T(8,128)} %refs_0_.1), channel_id=1, source_target_pairs={{0,1},{1,0},{2,3},{3,2},{4,5},{5,4},{6,7},{7,6},{8,9},{9,8},{10,11... | collective-permute-start | bytes 5898248 | tf_op jit(solution)/shard_map/ppermute | solution.py:426
  38.4 1.3 %collective-permute-start = (f32[56,128]{1,0:T(8,128)S(1)}, f32[56,128]{1,0:T(8,128)S(1)}, u32[]{:S(2)}, u32[]{:S(2)}) collective-permute-start(f32[56,128]{1,0:T(8,128)S(1)} %combine.1.refs_0_), channel_id=1, source_target_pairs={{0,1},{1,0},{2,3},{3,2},{4,5},{5,4},{6,7},{7,6},{8,9},{9,8},{10,11... | collective-permute-start | bytes 86024 | tf_op jit(solution)/shard_map/ppermute | solution.py:454
  40.6 3.9 %collective-permute-start.3 = (f32[48,128]{1,0:T(8,128)S(1)}, f32[48,128]{1,0:T(8,128)S(1)}, u32[]{:S(2)}, u32[]{:S(2)}) collective-permute-start(f32[48,128]{1,0:T(8,128)S(1)} %get-tuple-element.20.refs_0_), channel_id=1, source_target_pairs={{0,192},{64,0},{128,64},{192,128},{1,193},{65,1},{129,65},{193,129... | collective-permute-start | bytes 73736 | tf_op jit(solution)/shard_map/ppermute | solution.py:457
  41.8 5.5 %collective-permute-start.2 = (f32[48,128]{1,0:T(8,128)S(1)}, f32[48,128]{1,0:T(8,128)S(1)}, u32[]{:S(2)}, u32[]{:S(2)}) collective-permute-start(f32[48,128]{1,0:T(8,128)S(1)} %get-tuple-element.20.refs_0_), channel_id=1, source_target_pairs={{0,128},{64,192},{128,0},{192,64},{1,129},{65,193},{129,1},{193,65... | collective-permute-start | bytes 73736 | tf_op jit(solution)/shard_map/ppermute | solution.py:457
  43.3 5.0 %collective-permute-start.1 = (f32[48,128]{1,0:T(8,128)S(1)}, f32[48,128]{1,0:T(8,128)S(1)}, u32[]{:S(2)}, u32[]{:S(2)}) collective-permute-start(f32[48,128]{1,0:T(8,128)S(1)} %get-tuple-element.20.refs_0_), channel_id=1, source_target_pairs={{0,64},{64,128},{128,192},{192,0},{1,65},{65,129},{129,193},{193,1... | collective-permute-start | bytes 73736 | tf_op jit(solution)/shard_map/ppermute | solution.py:457

commit v7 on v6

--- a/solution.py
+++ b/solution.py
@@ -21,8 +21,18 @@
     return lax.broadcasted_iota(jnp.int32, shape, dim)
 
 
-def dot(a, b):
-    return jnp.dot(a, b, precision=HIGHEST, preferred_element_type=F32)
+def parts(x):
+    high = x.astype(BF16)
+    return high, (x - high.astype(F32)).astype(BF16)
+
+
+def dot(a, b, by_lanes=False):
+    (a_high, a_low), (b_high, b_low) = parts(a), parts(b)
+    dims = BY_LANES if by_lanes else (((1,), (0,)), ((), ()))
+    left = jnp.concatenate([a_high, a_low], axis=1)
+    right = jnp.concatenate([b_high, b_high], axis=1 if by_lanes else 0)
+    total = lax.dot_general(left, right, dims, preferred_element_type=F32)
+    return total + lax.dot_general(a_high, b_low, dims, preferred_element_type=F32)
 
 
 def turn(x, by):
@@ -299,7 +309,7 @@
         else:
             spread_ref[l] = jnp.concatenate([spread[nm:], own, own, jnp.zeros((LANES - 3 * nm, LANES), F32)], axis=0)
             left = jnp.concatenate([left, jnp.broadcast_to(scaled * gain, (SUB, LANES))], axis=0)
-        product = lax.dot_general(left, spread_ref[l], BY_LANES, precision=HIGHEST, preferred_element_type=F32)
+        product = dot(left, spread_ref[l], by_lanes=True)
         if step + 1 < STEPS:
             mats.append(pack_mixing(product, jnp.sum(scaled * gain * own, axis=1, keepdims=True)))
         else:
@@ -335,7 +345,7 @@
     packed = -(-nl * per // regions)
     first = own_ref.shape[0] - packed * SUB
     rows = first // nl
-    parts = [jnp.zeros((SUB, LANES), F32) for _ in range(2 * packed)]
+    pieces_out = [jnp.zeros((SUB, LANES), F32) for _ in range(2 * packed)]
     rest = jnp.zeros((LANES - 2 * nm, LANES), F32)
     for l in range(nl):
         pieces = []
@@ -356,8 +366,8 @@
                 keep = (lane8 >= slots * k) & (lane8 < slots * (k + 1))
                 at = half * per + r
                 j += half * packed
-                parts[j] = jnp.where(keep, turn(result[at * SUB:(at + 1) * SUB], slots * k), parts[j])
-    msg_ref[...] = jnp.concatenate(parts, axis=0)
+                pieces_out[j] = jnp.where(keep, turn(result[at * SUB:(at + 1) * SUB], slots * k), pieces_out[j])
+    msg_ref[...] = jnp.concatenate(pieces_out, axis=0)
 
 
 def split(x):

time: 70.4 us -> 70 us (level)
  no operation moved by 1% of the time
where the time goes in v7:
time: 70 us; the launch traced here: 69.8 us
  blocking collectives  51.2 us (73%)
  Pallas kernels  9.51 us (14%)
  waiting for transfers between devices  6.22 us (9%)
  starting transfers between devices  2.81 us (4%)
    all_to_all x2, blocking collectives, assimilate(): return (lax.all_to_all(out, 'level', 0, 0, tiled=True), local)  41.2 us
    all_to_all x1, blocking collectives, body(): lax.all_to_all(msg, ('region', 'member'), 0, 0, tiled=True)  10 us
    pallas_call x6, Pallas kernels, call(): pl.pallas_call(wrapped, out_shape=[kind(s, F32) for s in outs], in_specs=...  9.51 us
    ppermute x3, waiting for transfers between devices, body(): lax.ppermute(msg, 'region', ring)  5.03 us
    ppermute x3, starting transfers between devices, body(): lax.ppermute(msg, 'region', ring)  2.71 us
  transfers between devices with their start and end apart: 5, of which 4 were waited for; matrix products, arithmetic and copies ran while one was open for 0% of the time, Pallas kernels for 10%

profile of v7, /device:TPU:32, one launch (start us, length us, event | category | flops | bytes accessed | tf_op | source)
XLA Modules:
  0.0 69.8 jit_solution(4170604004196910857)
XLA Ops:
  0.0 0.0 collective-permute-start.4
  0.0 4.4 %predict.1 = (f32[8,24,128]{2,1,0:T(8,128)S(1)}, f32[24,128]{1,0:T(8,128)S(1)}, f32[2,8,128]{2,1,0:T(8,128)S(1)}, f32[3,2,40,2048]{3,2,1,0:T(8,128)S(1)}) custom-call(f32[3,2,40,2048]{3,2,1,0:T(8,128)} %refs_0_.1, s32[2,64,128]{2,1,0:T(8,128)} %bitcast.7, s32[2,128]{1,0:T(2,128)} %refs_2_.1, f32[2,3,64,128]{3,2,1,0:T(8,128)} %bitcast.6, s32[2,128]{1,0:T(2,128)} %refs_4_.1, ...), custom_call_target="tpu_custom_call" | custom-call | tf_op jit(solution)/shard_map/predict/pallas_call | solution.py:426
  4.4 10.0 %all_to_all.15.refs_0_ = f32[8,24,128]{2,1,0:T(8,128)S(1)} all-to-all(f32[8,24,128]{2,1,0:T(8,128)S(1)} %get-tuple-element.15), channel_id=1, replica_groups=mesh['region'=4,'level'=32,'member'=2] {'region','member'}, dimensions={0} | all-to-all | bytes 196608 | tf_op jit(solution)/shard_map/all_to_all | solution.py:457
  14.4 0.7 local.2
  15.0 23.1 %all_to_all.16.refs_0_ = f32[32,16,128]{2,1,0:T(8,128)S(1)} all-to-all(f32[32,16,128]{2,1,0:T(8,128)S(1)} %get-tuple-element.17), channel_id=1, replica_groups=mesh['region'=4,'level'=32,'member'=2] {'level'}, dimensions={0} | all-to-all | bytes 524288 | tf_op jit(solution)/shard_map/all_to_all | solution.py:454
  38.2 0.2 combine.1.refs_0_
  38.3 0.1 collective-permute-start
  38.4 1.2 %collective-permute-done.refs_1_ = f32[56,128]{1,0:T(8,128)S(1)} collective-permute-done((f32[56,128]{1,0:T(8,128)S(1)}, f32[56,128]{1,0:T(8,128)S(1)}, u32[]{:S(2)}, u32[]{:S(2)}) %collective-permute-start) | collective-permute-done | bytes 28704 | tf_op jit(solution)/shard_map/ppermute | solution.py:464
  39.6 0.7 %forecast.1 = (f32[2,128,128]{2,1,0:T(8,128)S(1)}, f32[48,128]{1,0:T(8,128)S(1)}) custom-call(f32[56,128]{1,0:T(8,128)S(1)} %combine.1.refs_0_, f32[56,128]{1,0:T(8,128)S(1)} %collective-permute-done.refs_1_), custom_call_target="tpu_custom_call" | custom-call | tf_op jit(solution)/shard_map/forecast/pallas_call | solution.py:426
  40.4 1.2 %collective-permute-start.3 = (f32[48,128]{1,0:T(8,128)S(1)}, f32[48,128]{1,0:T(8,128)S(1)}, u32[]{:S(2)}, u32[]{:S(2)}) collective-permute-start(f32[48,128]{1,0:T(8,128)S(1)} %get-tuple-element.20.refs_0_), channel_id=1, source_target_pairs={{0,192},{64,0},{128,64},{192,128},{1,193},{65,1},{129,65},{193,129... | collective-permute-start | bytes 73736 | tf_op jit(solution)/shard_map/ppermute | solution.py:467
  41.6 1.5 %collective-permute-start.2 = (f32[48,128]{1,0:T(8,128)S(1)}, f32[48,128]{1,0:T(8,128)S(1)}, u32[]{:S(2)}, u32[]{:S(2)}) collective-permute-start(f32[48,128]{1,0:T(8,128)S(1)} %get-tuple-element.20.refs_0_), channel_id=1, source_target_pairs={{0,128},{64,192},{128,0},{192,64},{1,129},{65,193},{129,1},{193,65... | collective-permute-start | bytes 73736 | tf_op jit(solution)/shard_map/ppermute | solution.py:467
  43.1 0.0 collective-permute-start.1
  43.1 1.2 %collective-permute-done.3.refs_3_ = f32[48,128]{1,0:T(8,128)S(1)} collective-permute-done((f32[48,128]{1,0:T(8,128)S(1)}, f32[48,128]{1,0:T(8,128)S(1)}, u32[]{:S(2)}, u32[]{:S(2)}) %collective-permute-start.3) | collective-permute-done | bytes 24608 | tf_op jit(solution)/shard_map/ppermute | solution.py:467
  44.3 2.8 %collective-permute-done.2.refs_2_ = f32[48,128]{1,0:T(8,128)S(1)} collective-permute-done((f32[48,128]{1,0:T(8,128)S(1)}, f32[48,128]{1,0:T(8,128)S(1)}, u32[]{:S(2)}, u32[]{:S(2)}) %collective-permute-start.2) | collective-permute-done | bytes 24608 | tf_op jit(solution)/shard_map/ppermute | solution.py:467
  47.1 1.0 %collective-permute-done.1.refs_1_ = f32[48,128]{1,0:T(8,128)S(1)} collective-permute-done((f32[48,128]{1,0:T(8,128)S(1)}, f32[48,128]{1,0:T(8,128)S(1)}, u32[]{:S(2)}, u32[]{:S(2)}) %collective-permute-start.1) | collective-permute-done | bytes 24608 | tf_op jit(solution)/shard_map/ppermute | solution.py:467
  48.1 0.7 %local.3 = (f32[32,24,128]{2,1,0:T(8,128)S(1)}, f32[2,24,128]{2,1,0:T(8,128)S(1)}) custom-call(f32[48,128]{1,0:T(8,128)S(1)} %get-tuple-element.20.refs_0_, f32[48,128]{1,0:T(8,128)S(1)} %collective-permute-done.1.refs_1_, f32[48,128]{1,0:T(8,128)S(1)} %collective-permute-done.2.refs_2_, f32[48,128]{1,0:T(8,128)S(1)} %collective-permute-done.3.refs_3_, ...), custom_call_target="tpu_custom_call" | custom-call | tf_op jit(solution)/shard_map/local/pallas_call | solution.py:426
  48.9 18.1 %all_to_all.17.refs_0_ = f32[32,24,128]{2,1,0:T(8,128)S(1)} all-to-all(f32[32,24,128]{2,1,0:T(8,128)S(1)} %get-tuple-element.21), channel_id=1, replica_groups=mesh['region'=4,'level'=32,'member'=2] {'level'}, dimensions={0} | all-to-all | bytes 786432 | tf_op jit(solution)/shard_map/all_to_all | solution.py:454
  67.0 0.0 collective-permute-done.4.refs_4_
  67.0 2.9 %update.1 = f32[3,2,40,2048]{3,2,1,0:T(8,128)} custom-call(f32[32,24,128]{2,1,0:T(8,128)S(1)} %all_to_all.17.refs_0_, f32[2,24,128]{2,1,0:T(8,128)S(1)} %get-tuple-element.22.refs_1_, f32[2,128,128]{2,1,0:T(8,128)S(1)} %get-tuple-element.23.refs_2_, f32[3,2,40,2048]{3,2,1,0:T(8,128)S(1)} %get-tuple-element.24.refs_3_, ...), custom_call_target="tpu_custom_call" | custom-call | tf_op jit(solution)/shard_map/update/pallas_call | solution.py:426
Async XLA Ops:
  0.0 67.0 %collective-permute-start.4 = (f32[3,2,40,2048]{3,2,1,0:T(8,128)}, f32[3,2,40,2048]{3,2,1,0:T(8,128)S(1)}, u32[]{:S(2)}, u32[]{:S(2)}) collective-permute-start(f32[3,2,40,2048]{3,2,1,0:T(8,128)} %refs_0_.1), channel_id=1, source_target_pairs={{0,1},{1,0},{2,3},{3,2},{4,5},{5,4},{6,7},{7,6},{8,9},{9,8},{10,11... | collective-permute-start | bytes 5898248 | tf_op jit(solution)/shard_map/ppermute | solution.py:436
  38.3 1.3 %collective-permute-start = (f32[56,128]{1,0:T(8,128)S(1)}, f32[56,128]{1,0:T(8,128)S(1)}, u32[]{:S(2)}, u32[]{:S(2)}) collective-permute-start(f32[56,128]{1,0:T(8,128)S(1)} %combine.1.refs_0_), channel_id=1, source_target_pairs={{0,1},{1,0},{2,3},{3,2},{4,5},{5,4},{6,7},{7,6},{8,9},{9,8},{10,11... | collective-permute-start | bytes 86024 | tf_op jit(solution)/shard_map/ppermute | solution.py:464
  40.4 3.9 %collective-permute-start.3 = (f32[48,128]{1,0:T(8,128)S(1)}, f32[48,128]{1,0:T(8,128)S(1)}, u32[]{:S(2)}, u32[]{:S(2)}) collective-permute-start(f32[48,128]{1,0:T(8,128)S(1)} %get-tuple-element.20.refs_0_), channel_id=1, source_target_pairs={{0,192},{64,0},{128,64},{192,128},{1,193},{65,1},{129,65},{193,129... | collective-permute-start | bytes 73736 | tf_op jit(solution)/shard_map/ppermute | solution.py:467
  41.6 5.5 %collective-permute-start.2 = (f32[48,128]{1,0:T(8,128)S(1)}, f32[48,128]{1,0:T(8,128)S(1)}, u32[]{:S(2)}, u32[]{:S(2)}) collective-permute-start(f32[48,128]{1,0:T(8,128)S(1)} %get-tuple-element.20.refs_0_), channel_id=1, source_target_pairs={{0,128},{64,192},{128,0},{192,64},{1,129},{65,193},{129,1},{193,65... | collective-permute-start | bytes 73736 | tf_op jit(solution)/shard_map/ppermute | solution.py:467
  43.1 5.0 %collective-permute-start.1 = (f32[48,128]{1,0:T(8,128)S(1)}, f32[48,128]{1,0:T(8,128)S(1)}, u32[]{:S(2)}, u32[]{:S(2)}) collective-permute-start(f32[48,128]{1,0:T(8,128)S(1)} %get-tuple-element.20.refs_0_), channel_id=1, source_target_pairs={{0,64},{64,128},{128,192},{192,0},{1,65},{65,129},{129,193},{193,1... | collective-permute-start | bytes 73736 | tf_op jit(solution)/shard_map/ppermute | solution.py:467

commit v8 on v7

--- a/solution.py
+++ b/solution.py
@@ -433,7 +433,6 @@
             name=name,
         )(*args)
 
-    other_state = lax.ppermute(state, "member", swap)
     given = [ray_cols.swapaxes(1, 2), ray_len, ray_weight.transpose(0, 2, 3, 1), owner, loc_regions.swapaxes(1, 2),
              loc_weight.swapaxes(1, 2), obs_value.swapaxes(1, 2), obs_var.swapaxes(1, 2)]
     msg, later, meta, held = call(
@@ -465,6 +464,7 @@
     )
     rings = [[(i, (i + s) % regions) for i in range(regions)] for s in range(1, regions)]
     got = assimilate(1, [msg] + [lax.ppermute(msg, "region", ring) for ring in rings], -(-(nm // SUB) // 2) * SUB)
+    other_state = lax.ppermute(held, "member", swap)
     out, = call(
         update_kernel, (nl, nm, levels, level_count), [state.shape],
         [VMEM(state.shape, F32), VMEM((nl, nm, 2 * LANES), F32), dma((nv * nl,))],

time: 70 us -> 70.2 us (level)
  transfers between devices with their start and end apart: 5 -> 5, of which waited for: 4 -> 4; matrix products, arithmetic and copies ran while one was open for 0% -> 0% of each run, Pallas kernels for 10% -> 3%
where the time goes in v8:
time: 70.2 us; the launch traced here: 69.9 us
  blocking collectives  51.2 us (73%)
  Pallas kernels  9.55 us (14%)
  waiting for transfers between devices  6.22 us (9%)
  starting transfers between devices  2.9 us (4%)
    all_to_all x2, blocking collectives, assimilate(): return (lax.all_to_all(out, 'level', 0, 0, tiled=True), local)  41.2 us
    all_to_all x1, blocking collectives, body(): lax.all_to_all(msg, ('region', 'member'), 0, 0, tiled=True)  9.98 us
    pallas_call x6, Pallas kernels, call(): pl.pallas_call(wrapped, out_shape=[kind(s, F32) for s in outs], in_specs=...  9.55 us
    ppermute x3, waiting for transfers between devices, body(): lax.ppermute(msg, 'region', ring)  5.03 us
    ppermute x3, starting transfers between devices, body(): lax.ppermute(msg, 'region', ring)  2.71 us
  transfers between devices with their start and end apart: 5, of which 4 were waited for; matrix products, arithmetic and copies ran while one was open for 0% of the time, Pallas kernels for 3%

profile of v8, /device:TPU:32, one launch (start us, length us, event | category | flops | bytes accessed | tf_op | source)
XLA Modules:
  0.0 69.9 jit_solution(2424040757394309960)
XLA Ops:
  0.0 4.4 %predict.1 = (f32[8,24,128]{2,1,0:T(8,128)S(1)}, f32[24,128]{1,0:T(8,128)S(1)}, f32[2,8,128]{2,1,0:T(8,128)S(1)}, f32[3,2,40,2048]{3,2,1,0:T(8,128)S(1)}) custom-call(f32[3,2,40,2048]{3,2,1,0:T(8,128)} %refs_0_.1, s32[2,64,128]{2,1,0:T(8,128)} %bitcast.7, s32[2,128]{1,0:T(2,128)} %refs_2_.1, f32[2,3,64,128]{3,2,1,0:T(8,128)} %bitcast.6, s32[2,128]{1,0:T(2,128)} %refs_4_.1, ...), custom_call_target="tpu_custom_call" | custom-call | tf_op jit(solution)/shard_map/predict/pallas_call | solution.py:426
  4.4 0.1 collective-permute-start.4
  4.5 10.0 %all_to_all.15.refs_0_ = f32[8,24,128]{2,1,0:T(8,128)S(1)} all-to-all(f32[8,24,128]{2,1,0:T(8,128)S(1)} %get-tuple-element.15), channel_id=1, replica_groups=mesh['region'=4,'level'=32,'member'=2] {'region','member'}, dimensions={0} | all-to-all | bytes 196608 | tf_op jit(solution)/shard_map/all_to_all | solution.py:456
  14.5 0.7 local.2
  15.1 23.1 %all_to_all.16.refs_0_ = f32[32,16,128]{2,1,0:T(8,128)S(1)} all-to-all(f32[32,16,128]{2,1,0:T(8,128)S(1)} %get-tuple-element.17), channel_id=1, replica_groups=mesh['region'=4,'level'=32,'member'=2] {'level'}, dimensions={0} | all-to-all | bytes 524288 | tf_op jit(solution)/shard_map/all_to_all | solution.py:453
  38.2 0.2 combine.1.refs_0_
  38.4 0.1 collective-permute-start
  38.5 1.2 %collective-permute-done.refs_1_ = f32[56,128]{1,0:T(8,128)S(1)} collective-permute-done((f32[56,128]{1,0:T(8,128)S(1)}, f32[56,128]{1,0:T(8,128)S(1)}, u32[]{:S(2)}, u32[]{:S(2)}) %collective-permute-start) | collective-permute-done | bytes 28704 | tf_op jit(solution)/shard_map/ppermute | solution.py:463
  39.7 0.7 %forecast.1 = (f32[2,128,128]{2,1,0:T(8,128)S(1)}, f32[48,128]{1,0:T(8,128)S(1)}) custom-call(f32[56,128]{1,0:T(8,128)S(1)} %combine.1.refs_0_, f32[56,128]{1,0:T(8,128)S(1)} %collective-permute-done.refs_1_), custom_call_target="tpu_custom_call" | custom-call | tf_op jit(solution)/shard_map/forecast/pallas_call | solution.py:426
  40.4 1.2 %collective-permute-start.3 = (f32[48,128]{1,0:T(8,128)S(1)}, f32[48,128]{1,0:T(8,128)S(1)}, u32[]{:S(2)}, u32[]{:S(2)}) collective-permute-start(f32[48,128]{1,0:T(8,128)S(1)} %get-tuple-element.20.refs_0_), channel_id=1, source_target_pairs={{0,192},{64,0},{128,64},{192,128},{1,193},{65,1},{129,65},{193,129... | collective-permute-start | bytes 73736 | tf_op jit(solution)/shard_map/ppermute | solution.py:466
  41.7 1.5 %collective-permute-start.2 = (f32[48,128]{1,0:T(8,128)S(1)}, f32[48,128]{1,0:T(8,128)S(1)}, u32[]{:S(2)}, u32[]{:S(2)}) collective-permute-start(f32[48,128]{1,0:T(8,128)S(1)} %get-tuple-element.20.refs_0_), channel_id=1, source_target_pairs={{0,128},{64,192},{128,0},{192,64},{1,129},{65,193},{129,1},{193,65... | collective-permute-start | bytes 73736 | tf_op jit(solution)/shard_map/ppermute | solution.py:466
  43.2 0.0 collective-permute-start.1
  43.2 1.2 %collective-permute-done.3.refs_3_ = f32[48,128]{1,0:T(8,128)S(1)} collective-permute-done((f32[48,128]{1,0:T(8,128)S(1)}, f32[48,128]{1,0:T(8,128)S(1)}, u32[]{:S(2)}, u32[]{:S(2)}) %collective-permute-start.3) | collective-permute-done | bytes 24608 | tf_op jit(solution)/shard_map/ppermute | solution.py:466
  44.4 2.8 %collective-permute-done.2.refs_2_ = f32[48,128]{1,0:T(8,128)S(1)} collective-permute-done((f32[48,128]{1,0:T(8,128)S(1)}, f32[48,128]{1,0:T(8,128)S(1)}, u32[]{:S(2)}, u32[]{:S(2)}) %collective-permute-start.2) | collective-permute-done | bytes 24608 | tf_op jit(solution)/shard_map/ppermute | solution.py:466
  47.2 1.0 %collective-permute-done.1.refs_1_ = f32[48,128]{1,0:T(8,128)S(1)} collective-permute-done((f32[48,128]{1,0:T(8,128)S(1)}, f32[48,128]{1,0:T(8,128)S(1)}, u32[]{:S(2)}, u32[]{:S(2)}) %collective-permute-start.1) | collective-permute-done | bytes 24608 | tf_op jit(solution)/shard_map/ppermute | solution.py:466
  48.2 0.7 %local.3 = (f32[32,24,128]{2,1,0:T(8,128)S(1)}, f32[2,24,128]{2,1,0:T(8,128)S(1)}) custom-call(f32[48,128]{1,0:T(8,128)S(1)} %get-tuple-element.20.refs_0_, f32[48,128]{1,0:T(8,128)S(1)} %collective-permute-done.1.refs_1_, f32[48,128]{1,0:T(8,128)S(1)} %collective-permute-done.2.refs_2_, f32[48,128]{1,0:T(8,128)S(1)} %collective-permute-done.3.refs_3_, ...), custom_call_target="tpu_custom_call" | custom-call | tf_op jit(solution)/shard_map/local/pallas_call | solution.py:426
  48.9 18.1 %all_to_all.17.refs_0_ = f32[32,24,128]{2,1,0:T(8,128)S(1)} all-to-all(f32[32,24,128]{2,1,0:T(8,128)S(1)} %get-tuple-element.21), channel_id=1, replica_groups=mesh['region'=4,'level'=32,'member'=2] {'level'}, dimensions={0} | all-to-all | bytes 786432 | tf_op jit(solution)/shard_map/all_to_all | solution.py:453
  67.0 0.0 collective-permute-done.4.refs_4_
  67.0 2.9 %update.1 = f32[3,2,40,2048]{3,2,1,0:T(8,128)} custom-call(f32[32,24,128]{2,1,0:T(8,128)S(1)} %all_to_all.17.refs_0_, f32[2,24,128]{2,1,0:T(8,128)S(1)} %get-tuple-element.22.refs_1_, f32[2,128,128]{2,1,0:T(8,128)S(1)} %get-tuple-element.23.refs_2_, f32[3,2,40,2048]{3,2,1,0:T(8,128)S(1)} %get-tuple-element.24.refs_3_, ...), custom_call_target="tpu_custom_call" | custom-call | tf_op jit(solution)/shard_map/update/pallas_call | solution.py:426
Async XLA Ops:
  4.4 62.7 %collective-permute-start.4 = (f32[3,2,40,2048]{3,2,1,0:T(8,128)S(1)}, f32[3,2,40,2048]{3,2,1,0:T(8,128)S(1)}, u32[]{:S(2)}, u32[]{:S(2)}) collective-permute-start(f32[3,2,40,2048]{3,2,1,0:T(8,128)S(1)} %get-tuple-element.24.refs_3_), channel_id=1, source_target_pairs={{0,1},{1,0},{2,3},{3,2},{4,5},{5,4},{6,7},{7,6},{8,9},{9,8},{10,11... | collective-permute-start | bytes 5898248 | tf_op jit(solution)/shard_map/ppermute | solution.py:467
  38.4 1.3 %collective-permute-start = (f32[56,128]{1,0:T(8,128)S(1)}, f32[56,128]{1,0:T(8,128)S(1)}, u32[]{:S(2)}, u32[]{:S(2)}) collective-permute-start(f32[56,128]{1,0:T(8,128)S(1)} %combine.1.refs_0_), channel_id=1, source_target_pairs={{0,1},{1,0},{2,3},{3,2},{4,5},{5,4},{6,7},{7,6},{8,9},{9,8},{10,11... | collective-permute-start | bytes 86024 | tf_op jit(solution)/shard_map/ppermute | solution.py:463
  40.4 3.9 %collective-permute-start.3 = (f32[48,128]{1,0:T(8,128)S(1)}, f32[48,128]{1,0:T(8,128)S(1)}, u32[]{:S(2)}, u32[]{:S(2)}) collective-permute-start(f32[48,128]{1,0:T(8,128)S(1)} %get-tuple-element.20.refs_0_), channel_id=1, source_target_pairs={{0,192},{64,0},{128,64},{192,128},{1,193},{65,1},{129,65},{193,129... | collective-permute-start | bytes 73736 | tf_op jit(solution)/shard_map/ppermute | solution.py:466
  41.7 5.5 %collective-permute-start.2 = (f32[48,128]{1,0:T(8,128)S(1)}, f32[48,128]{1,0:T(8,128)S(1)}, u32[]{:S(2)}, u32[]{:S(2)}) collective-permute-start(f32[48,128]{1,0:T(8,128)S(1)} %get-tuple-element.20.refs_0_), channel_id=1, source_target_pairs={{0,128},{64,192},{128,0},{192,64},{1,129},{65,193},{129,1},{193,65... | collective-permute-start | bytes 73736 | tf_op jit(solution)/shard_map/ppermute | solution.py:466
  43.2 5.0 %collective-permute-start.1 = (f32[48,128]{1,0:T(8,128)S(1)}, f32[48,128]{1,0:T(8,128)S(1)}, u32[]{:S(2)}, u32[]{:S(2)}) collective-permute-start(f32[48,128]{1,0:T(8,128)S(1)} %get-tuple-element.20.refs_0_), channel_id=1, source_target_pairs={{0,64},{64,128},{128,192},{192,0},{1,65},{65,129},{129,193},{193,1... | collective-permute-start | bytes 73736 | tf_op jit(solution)/shard_map/ppermute | solution.py:466

commit v9 on v7

--- a/solution.py
+++ b/solution.py
@@ -318,24 +318,57 @@
     down = sum(math.exp(-l / scale) * mats[l] for l in range(nl))
     for l in range(nl):
         local_ref[l] = sum(math.exp(-abs(l - k) / scale) * mats[k] for k in range(nl))
-    for d in range(level_count):
-        msg_ref[d] = jnp.where(d > level, up, down)
-
-
-def combine(nl, levels, level_count, got_ref, local_ref):
+    if step + 1 < STEPS:
+        for d in range(level_count):
+            msg_ref[d] = jnp.where(d > level, up, down)
+    else:
+        msg_ref[...] = jnp.concatenate([up, down], axis=0)
+
+
+def combine(nl, levels, inner, got_ref, local_ref):
     level = lax.axis_index("level")
+    outer, place = lax.div(level, inner), lax.rem(level, inner)
     scale = levels / 4.0
-    fade = math.exp(-nl / scale)
+    count, near = got_ref.shape[0], nl * inner
+    fade = math.exp(-near / scale)
     zero = jnp.zeros(got_ref.shape[1:], F32)
-    below = lax.fori_loop(0, level, lambda d, acc: acc * fade + got_ref[d], zero)
-    above = lax.fori_loop(0, level_count - 1 - level, lambda d, acc: acc * fade + got_ref[level_count - 1 - d], zero)
+    below = lax.fori_loop(0, outer, lambda d, acc: acc * fade + got_ref[d], zero)
+    above = lax.fori_loop(0, count - 1 - outer, lambda d, acc: acc * fade + got_ref[count - 1 - d], zero)
+    at = jnp.zeros((1, LANES), F32) + place.astype(F32) * float(nl)
     return [
-        math.exp(-(l + 1) / scale) * below + math.exp(-(nl - l) / scale) * above + local_ref[l] for l in range(nl)
+        jnp.exp(-(at + float(l + 1)) / scale) * below + jnp.exp((at + float(l - near)) / scale) * above + local_ref[l]
+        for l in range(nl)
     ]
 
 
-def combine_kernel(nl, levels, level_count, got_ref, local_ref, later_ref, out_ref):
-    out_ref[...] = jnp.concatenate(combine(nl, levels, level_count, got_ref, local_ref) + [later_ref[...]], axis=0)
+def group_kernel(nl, levels, inner, *refs):
+    *got, local_ref, msg_ref, part_ref = refs
+    level = lax.axis_index("level")
+    outer, place = lax.div(level, inner), lax.rem(level, inner)
+    scale = levels / 4.0
+    rows = local_ref.shape[1]
+    up = down = None
+    near = [local_ref[l] for l in range(nl)]
+    for s, ref in enumerate(got):
+        rise, fall = ref[0:rows], ref[rows:2 * rows]
+        source = jnp.where(place >= s, place - s, place - s + inner)
+        at = jnp.zeros((1, LANES), F32) + source.astype(F32) * float(nl)
+        higher = jnp.exp((at - float(nl * (inner - 1))) / scale) * rise
+        lower = jnp.exp(-at / scale) * fall
+        up, down = (higher, lower) if up is None else (up + higher, down + lower)
+        if s:
+            for l in range(nl):
+                from_below = math.exp(-(l + 1 + (s - 1) * nl) / scale) * rise
+                from_above = math.exp(-((inner - s) * nl - l) / scale) * fall
+                near[l] = near[l] + jnp.where(place >= s, from_below, from_above)
+    for l in range(nl):
+        part_ref[l] = near[l]
+    for d in range(msg_ref.shape[0]):
+        msg_ref[d] = jnp.where(d > outer, up, down)
+
+
+def combine_kernel(nl, levels, got_ref, local_ref, later_ref, out_ref):
+    out_ref[...] = jnp.concatenate(combine(nl, levels, 1, got_ref, local_ref) + [later_ref[...]], axis=0)
 
 
 def forecast_kernel(nl, nm, regions, slots, own_ref, other_ref, mix_ref, msg_ref, full_ref):
@@ -375,13 +408,13 @@
     return high, x - high
 
 
-def update_kernel(nl, nm, levels, level_count, got_ref, local_ref, mix_ref, state_ref, theirs_ref, out_hbm,
+def update_kernel(nl, nm, levels, inner, got_ref, local_ref, mix_ref, state_ref, theirs_ref, out_hbm,
                   out_v, left_ref, out_sem):
     nv = state_ref.shape[0]
     members = 2 * nm
     blocks = [(v, l) for l in range(nl) for v in range(nv)]
     lane = iota((nm, LANES), 1)
-    for l, packed in enumerate(combine(nl, levels, level_count, got_ref, local_ref)):
+    for l, packed in enumerate(combine(nl, levels, inner, got_ref, local_ref)):
         second = unpack_rows(packed, nm)
         both = second + mix_ref[l, 0:nm] + dot(second, mix_ref[l])
         high, low = split(both)
@@ -402,6 +435,9 @@
         copy.wait()
 
 
+INNER = 4
+
+
 def body(state, ray_cols, ray_len, ray_weight, owner, loc_regions, loc_weight, obs_value, obs_var):
     regions = lax.axis_size("region")
     level_count = lax.axis_size("level")
@@ -445,18 +481,19 @@
         state, *given, specs=[outside] * (1 + len(given)), name="predict", limit=56, kind=VMEM,
     )
 
-    def assimilate(step, got, rows):
-        out, local = call(
+    def assimilate(step, got, shape):
+        return call(
             local_kernel, (step, nl, nm, regions, slots, levels, level_count, cores),
-            [(level_count, rows, LANES), (nl, rows, LANES)], [VMEM((nl, LANES, LANES), F32)],
-            *got, meta, name="local",
+            [shape, (nl,) + shape[-2:] if step == 0 else (nl, shape[0] // 2, LANES)],
+            [VMEM((nl, LANES, LANES), F32)], *got, meta, name="local",
         )
-        return lax.all_to_all(out, "level", 0, 0, tiled=True), local
 
     band = -(-(nm // SUB) // (LANES // (nm + 2))) * SUB
-    got = assimilate(0, [lax.all_to_all(msg, ("region", "member"), 0, 0, tiled=True)], band)
+    got = lax.all_to_all(msg, ("region", "member"), 0, 0, tiled=True)
+    out, local = assimilate(0, [got], (level_count, band, LANES))
+    got = [lax.all_to_all(out, "level", 0, 0, tiled=True), local]
     own, = call(
-        combine_kernel, (nl, levels, level_count), [(nl * band + block[0], LANES)], [], *got, later, name="combine",
+        combine_kernel, (nl, levels), [(nl * band + block[0], LANES)], [], *got, later, name="combine",
     )
     mix, msg = call(
         forecast_kernel, (nl, nm, regions, slots),
@@ -464,11 +501,22 @@
         own, lax.ppermute(own, "member", swap), name="forecast",
     )
     rings = [[(i, (i + s) % regions) for i in range(regions)] for s in range(1, regions)]
-    got = assimilate(1, [msg] + [lax.ppermute(msg, "region", ring) for ring in rings], -(-(nm // SUB) // 2) * SUB)
+    rows = -(-(nm // SUB) // 2) * SUB
+    out, local = assimilate(1, [msg] + [lax.ppermute(msg, "region", ring) for ring in rings], (2 * rows, LANES))
+    outer = level_count // INNER
+    rings = [
+        [(z * INNER + y, z * INNER + (y + s) % INNER) for z in range(outer) for y in range(INNER)] for s in range(1, INNER)
+    ]
+    columns = [[z * INNER + y for z in range(outer)] for y in range(INNER)]
+    out, local = call(
+        group_kernel, (nl, levels, INNER), [(outer, rows, LANES), (nl, rows, LANES)], [],
+        out, *[lax.ppermute(out, "level", ring) for ring in rings], local, name="group",
+    )
+    got = lax.all_to_all(out, "level", 0, 0, tiled=True, axis_index_groups=columns)
     out, = call(
-        update_kernel, (nl, nm, levels, level_count), [state.shape],
+        update_kernel, (nl, nm, levels, INNER), [state.shape],
         [VMEM(state.shape, F32), VMEM((nl, nm, 2 * LANES), F32), dma((nv * nl,))],
-        *got, mix, held, other_state, out_specs=[outside], name="update",
+        got, local, mix, held, other_state, out_specs=[outside], name="update",
     )
     return out
 

time: 70 us -> 70.3 us (level)
  blocking collectives: 51.2 us -> 43.9 us
  waiting for transfers between devices: 6.22 us -> 11.2 us
  starting transfers between devices: 2.81 us -> 5.5 us
    all_to_all x3, blocking collectives: 51.2 us -> 43.9 us  [the longest x1 23.1 us: body(): got = [lax.all_to_all(out, 'level', 0, 0, tiled=True), local]]
    ppermute x0 -> x3, waiting for transfers between devices: none -> 4.99 us  [body(): lax.ppermute(out, 'level', ring)]
    ppermute x0 -> x3, starting transfers between devices: none -> 2.69 us  [body(): lax.ppermute(out, 'level', ring)]
    pallas_call x6 -> x7, Pallas kernels: 9.51 us -> 9.41 us  [call(): pl.pallas_call(wrapped, out_shape=[kind(s, F32) for s in outs], in_specs=...]
  transfers between devices with their start and end apart: 5 -> 8, of which waited for: 4 -> 7; matrix products, arithmetic and copies ran while one was open for 0% -> 0% of each run, Pallas kernels for 10% -> 9%
where the time goes in v9:
time: 70.3 us; the launch traced here: 70.1 us
  blocking collectives  43.9 us (62%)
  waiting for transfers between devices  11.2 us (16%)
  Pallas kernels  9.41 us (13%)
  starting transfers between devices  5.5 us (8%)
    all_to_all x1, blocking collectives, body(): got = [lax.all_to_all(out, 'level', 0, 0, tiled=True), local]  23.1 us
    all_to_all x1, blocking collectives, body(): lax.all_to_all(out, 'level', 0, 0, tiled=True, axis_index_groups=columns)  10.8 us
    all_to_all x1, blocking collectives, body(): got = lax.all_to_all(msg, ('region', 'member'), 0, 0, tiled=True)  10 us
    pallas_call x7, Pallas kernels, call(): pl.pallas_call(wrapped, out_shape=[kind(s, F32) for s in outs], in_specs=...  9.41 us
    ppermute x3, waiting for transfers between devices, body(): lax.ppermute(msg, 'region', ring)  5.03 us
    ppermute x3, waiting for transfers between devices, body(): lax.ppermute(out, 'level', ring)  4.99 us
    ppermute x3, starting transfers between devices, body(): lax.ppermute(msg, 'region', ring)  2.71 us
    ppermute x3, starting transfers between devices, body(): lax.ppermute(out, 'level', ring)  2.69 us
  transfers between devices with their start and end apart: 8, of which 7 were waited for; matrix products, arithmetic and copies ran while one was open for 0% of the time, Pallas kernels for 9%

profile of v9, /device:TPU:32, one launch (start us, length us, event | category | flops | bytes accessed | tf_op | source)
XLA Modules:
  0.0 70.1 jit_solution(492081382623144532)
XLA Ops:
  0.0 0.0 collective-permute-start.7
  0.0 4.4 %predict.1 = (f32[8,24,128]{2,1,0:T(8,128)S(1)}, f32[24,128]{1,0:T(8,128)S(1)}, f32[2,8,128]{2,1,0:T(8,128)S(1)}, f32[3,2,40,2048]{3,2,1,0:T(8,128)S(1)}) custom-call(f32[3,2,40,2048]{3,2,1,0:T(8,128)} %refs_0_.1, s32[2,64,128]{2,1,0:T(8,128)} %bitcast.7, s32[2,128]{1,0:T(2,128)} %refs_2_.1, f32[2,3,64,128]{3,2,1,0:T(8,128)} %bitcast.6, s32[2,128]{1,0:T(2,128)} %refs_4_.1, ...), custom_call_target="tpu_custom_call" | custom-call | tf_op jit(solution)/shard_map/predict/pallas_call | solution.py:462
  4.4 10.0 %all_to_all.15.refs_0_ = f32[8,24,128]{2,1,0:T(8,128)S(1)} all-to-all(f32[8,24,128]{2,1,0:T(8,128)S(1)} %get-tuple-element.17), channel_id=1, replica_groups=mesh['region'=4,'level'=32,'member'=2] {'region','member'}, dimensions={0} | all-to-all | bytes 196608 | tf_op jit(solution)/shard_map/all_to_all | solution.py:492
  14.4 0.7 local.2
  15.0 23.1 %all_to_all.16.refs_0_ = f32[32,16,128]{2,1,0:T(8,128)S(1)} all-to-all(f32[32,16,128]{2,1,0:T(8,128)S(1)} %get-tuple-element.19), channel_id=1, replica_groups=mesh['region'=4,'level'=32,'member'=2] {'level'}, dimensions={0} | all-to-all | bytes 524288 | tf_op jit(solution)/shard_map/all_to_all | solution.py:494
  38.2 0.2 combine.1.refs_0_
  38.3 0.1 collective-permute-start
  38.4 1.2 %collective-permute-done.refs_1_ = f32[56,128]{1,0:T(8,128)S(1)} collective-permute-done((f32[56,128]{1,0:T(8,128)S(1)}, f32[56,128]{1,0:T(8,128)S(1)}, u32[]{:S(2)}, u32[]{:S(2)}) %collective-permute-start) | collective-permute-done | bytes 28704 | tf_op jit(solution)/shard_map/ppermute | solution.py:501
  39.6 0.7 %forecast.1 = (f32[2,128,128]{2,1,0:T(8,128)S(1)}, f32[48,128]{1,0:T(8,128)S(1)}) custom-call(f32[56,128]{1,0:T(8,128)S(1)} %combine.1.refs_0_, f32[56,128]{1,0:T(8,128)S(1)} %collective-permute-done.refs_1_), custom_call_target="tpu_custom_call" | custom-call | tf_op jit(solution)/shard_map/forecast/pallas_call | solution.py:462
  40.4 1.2 %collective-permute-start.3 = (f32[48,128]{1,0:T(8,128)S(1)}, f32[48,128]{1,0:T(8,128)S(1)}, u32[]{:S(2)}, u32[]{:S(2)}) collective-permute-start(f32[48,128]{1,0:T(8,128)S(1)} %get-tuple-element.22.refs_0_), channel_id=1, source_target_pairs={{0,192},{64,0},{128,64},{192,128},{1,193},{65,1},{129,65},{193,129... | collective-permute-start | bytes 73736 | tf_op jit(solution)/shard_map/ppermute | solution.py:505
  41.6 1.5 %collective-permute-start.2 = (f32[48,128]{1,0:T(8,128)S(1)}, f32[48,128]{1,0:T(8,128)S(1)}, u32[]{:S(2)}, u32[]{:S(2)}) collective-permute-start(f32[48,128]{1,0:T(8,128)S(1)} %get-tuple-element.22.refs_0_), channel_id=1, source_target_pairs={{0,128},{64,192},{128,0},{192,64},{1,129},{65,193},{129,1},{193,65... | collective-permute-start | bytes 73736 | tf_op jit(solution)/shard_map/ppermute | solution.py:505
  43.1 0.0 collective-permute-start.1
  43.1 1.2 %collective-permute-done.3.refs_3_ = f32[48,128]{1,0:T(8,128)S(1)} collective-permute-done((f32[48,128]{1,0:T(8,128)S(1)}, f32[48,128]{1,0:T(8,128)S(1)}, u32[]{:S(2)}, u32[]{:S(2)}) %collective-permute-start.3) | collective-permute-done | bytes 24608 | tf_op jit(solution)/shard_map/ppermute | solution.py:505
  44.3 2.8 %collective-permute-done.2.refs_2_ = f32[48,128]{1,0:T(8,128)S(1)} collective-permute-done((f32[48,128]{1,0:T(8,128)S(1)}, f32[48,128]{1,0:T(8,128)S(1)}, u32[]{:S(2)}, u32[]{:S(2)}) %collective-permute-start.2) | collective-permute-done | bytes 24608 | tf_op jit(solution)/shard_map/ppermute | solution.py:505
  47.1 1.0 %collective-permute-done.1.refs_1_ = f32[48,128]{1,0:T(8,128)S(1)} collective-permute-done((f32[48,128]{1,0:T(8,128)S(1)}, f32[48,128]{1,0:T(8,128)S(1)}, u32[]{:S(2)}, u32[]{:S(2)}) %collective-permute-start.1) | collective-permute-done | bytes 24608 | tf_op jit(solution)/shard_map/ppermute | solution.py:505
  48.1 0.7 local.3
  48.8 1.4 %collective-permute-start.6 = (f32[48,128]{1,0:T(8,128)S(1)}, f32[48,128]{1,0:T(8,128)S(1)}, u32[]{:S(2)}, u32[]{:S(2)}) collective-permute-start(f32[48,128]{1,0:T(8,128)S(1)} %get-tuple-element.23.refs_0_), channel_id=1, source_target_pairs={{0,6},{2,0},{4,2},{6,4},{8,14},{10,8},{12,10},{14,12},{16,22},{18,... | collective-permute-start | bytes 73736 | tf_op jit(solution)/shard_map/ppermute | solution.py:513
  50.2 1.3 %collective-permute-start.5 = (f32[48,128]{1,0:T(8,128)S(1)}, f32[48,128]{1,0:T(8,128)S(1)}, u32[]{:S(2)}, u32[]{:S(2)}) collective-permute-start(f32[48,128]{1,0:T(8,128)S(1)} %get-tuple-element.23.refs_0_), channel_id=1, source_target_pairs={{0,4},{2,6},{4,0},{6,2},{8,12},{10,14},{12,8},{14,10},{16,20},{18,... | collective-permute-start | bytes 73736 | tf_op jit(solution)/shard_map/ppermute | solution.py:513
  51.5 0.0 collective-permute-start.4
  51.5 1.2 %collective-permute-done.6.refs_3_ = f32[48,128]{1,0:T(8,128)S(1)} collective-permute-done((f32[48,128]{1,0:T(8,128)S(1)}, f32[48,128]{1,0:T(8,128)S(1)}, u32[]{:S(2)}, u32[]{:S(2)}) %collective-permute-start.6) | collective-permute-done | bytes 24608 | tf_op jit(solution)/shard_map/ppermute | solution.py:513
  52.7 2.8 %collective-permute-done.5.refs_2_ = f32[48,128]{1,0:T(8,128)S(1)} collective-permute-done((f32[48,128]{1,0:T(8,128)S(1)}, f32[48,128]{1,0:T(8,128)S(1)}, u32[]{:S(2)}, u32[]{:S(2)}) %collective-permute-start.5) | collective-permute-done | bytes 24608 | tf_op jit(solution)/shard_map/ppermute | solution.py:513
  55.5 1.0 %collective-permute-done.4.refs_1_ = f32[48,128]{1,0:T(8,128)S(1)} collective-permute-done((f32[48,128]{1,0:T(8,128)S(1)}, f32[48,128]{1,0:T(8,128)S(1)}, u32[]{:S(2)}, u32[]{:S(2)}) %collective-permute-start.4) | collective-permute-done | bytes 24608 | tf_op jit(solution)/shard_map/ppermute | solution.py:513
  56.6 10.8 %all_to_all.17.refs_0_ = f32[8,24,128]{2,1,0:T(8,128)S(1)} all-to-all(f32[8,24,128]{2,1,0:T(8,128)S(1)} %get-tuple-element.25), channel_id=1, replica_groups={{0,8,16,24,32,40,48,56},{2,10,18,26,34,42,50,58},{4,12,20,28,36,44,52,6..., dimensions={0} | all-to-all | bytes 196608 | tf_op jit(solution)/shard_map/all_to_all | solution.py:515
  67.4 0.0 collective-permute-done.7.refs_4_
  67.4 2.8 %update.1 = f32[3,2,40,2048]{3,2,1,0:T(8,128)} custom-call(f32[8,24,128]{2,1,0:T(8,128)S(1)} %all_to_all.17.refs_0_, f32[2,24,128]{2,1,0:T(8,128)S(1)} %get-tuple-element.26.refs_1_, f32[2,128,128]{2,1,0:T(8,128)S(1)} %get-tuple-element.27.refs_2_, f32[3,2,40,2048]{3,2,1,0:T(8,128)S(1)} %get-tuple-element.28.refs_3_, ...), custom_call_target="tpu_custom_call" | custom-call | tf_op jit(solution)/shard_map/update/pallas_call | solution.py:462
  (1 shorter events, 0.0 us)
Async XLA Ops:
  0.0 67.4 %collective-permute-start.7 = (f32[3,2,40,2048]{3,2,1,0:T(8,128)}, f32[3,2,40,2048]{3,2,1,0:T(8,128)S(1)}, u32[]{:S(2)}, u32[]{:S(2)}) collective-permute-start(f32[3,2,40,2048]{3,2,1,0:T(8,128)} %refs_0_.1), channel_id=1, source_target_pairs={{0,1},{1,0},{2,3},{3,2},{4,5},{5,4},{6,7},{7,6},{8,9},{9,8},{10,11... | collective-permute-start | bytes 5898248 | tf_op jit(solution)/shard_map/ppermute | solution.py:472
  38.3 1.3 %collective-permute-start = (f32[56,128]{1,0:T(8,128)S(1)}, f32[56,128]{1,0:T(8,128)S(1)}, u32[]{:S(2)}, u32[]{:S(2)}) collective-permute-start(f32[56,128]{1,0:T(8,128)S(1)} %combine.1.refs_0_), channel_id=1, source_target_pairs={{0,1},{1,0},{2,3},{3,2},{4,5},{5,4},{6,7},{7,6},{8,9},{9,8},{10,11... | collective-permute-start | bytes 86024 | tf_op jit(solution)/shard_map/ppermute | solution.py:501
  40.4 3.9 %collective-permute-start.3 = (f32[48,128]{1,0:T(8,128)S(1)}, f32[48,128]{1,0:T(8,128)S(1)}, u32[]{:S(2)}, u32[]{:S(2)}) collective-permute-start(f32[48,128]{1,0:T(8,128)S(1)} %get-tuple-element.22.refs_0_), channel_id=1, source_target_pairs={{0,192},{64,0},{128,64},{192,128},{1,193},{65,1},{129,65},{193,129... | collective-permute-start | bytes 73736 | tf_op jit(solution)/shard_map/ppermute | solution.py:505
  41.6 5.5 %collective-permute-start.2 = (f32[48,128]{1,0:T(8,128)S(1)}, f32[48,128]{1,0:T(8,128)S(1)}, u32[]{:S(2)}, u32[]{:S(2)}) collective-permute-start(f32[48,128]{1,0:T(8,128)S(1)} %get-tuple-element.22.refs_0_), channel_id=1, source_target_pairs={{0,128},{64,192},{128,0},{192,64},{1,129},{65,193},{129,1},{193,65... | collective-permute-start | bytes 73736 | tf_op jit(solution)/shard_map/ppermute | solution.py:505
  43.1 5.0 %collective-permute-start.1 = (f32[48,128]{1,0:T(8,128)S(1)}, f32[48,128]{1,0:T(8,128)S(1)}, u32[]{:S(2)}, u32[]{:S(2)}) collective-permute-start(f32[48,128]{1,0:T(8,128)S(1)} %get-tuple-element.22.refs_0_), channel_id=1, source_target_pairs={{0,64},{64,128},{128,192},{192,0},{1,65},{65,129},{129,193},{193,1... | collective-permute-start | bytes 73736 | tf_op jit(solution)/shard_map/ppermute | solution.py:505
  48.8 3.9 %collective-permute-start.6 = (f32[48,128]{1,0:T(8,128)S(1)}, f32[48,128]{1,0:T(8,128)S(1)}, u32[]{:S(2)}, u32[]{:S(2)}) collective-permute-start(f32[48,128]{1,0:T(8,128)S(1)} %get-tuple-element.23.refs_0_), channel_id=1, source_target_pairs={{0,6},{2,0},{4,2},{6,4},{8,14},{10,8},{12,10},{14,12},{16,22},{18,... | collective-permute-start | bytes 73736 | tf_op jit(solution)/shard_map/ppermute | solution.py:513
  50.2 5.3 %collective-permute-start.5 = (f32[48,128]{1,0:T(8,128)S(1)}, f32[48,128]{1,0:T(8,128)S(1)}, u32[]{:S(2)}, u32[]{:S(2)}) collective-permute-start(f32[48,128]{1,0:T(8,128)S(1)} %get-tuple-element.23.refs_0_), channel_id=1, source_target_pairs={{0,4},{2,6},{4,0},{6,2},{8,12},{10,14},{12,8},{14,10},{16,20},{18,... | collective-permute-start | bytes 73736 | tf_op jit(solution)/shard_map/ppermute | solution.py:513
  51.5 5.0 %collective-permute-start.4 = (f32[48,128]{1,0:T(8,128)S(1)}, f32[48,128]{1,0:T(8,128)S(1)}, u32[]{:S(2)}, u32[]{:S(2)}) collective-permute-start(f32[48,128]{1,0:T(8,128)S(1)} %get-tuple-element.23.refs_0_), channel_id=1, source_target_pairs={{0,2},{2,4},{4,6},{6,0},{8,10},{10,12},{12,14},{14,8},{16,18},{18,... | collective-permute-start | bytes 73736 | tf_op jit(solution)/shard_map/ppermute | solution.py:513
